TPU v7x, 32 devices: a whole 2x2x4 slice. The times are simulated.
32 devices in a mesh: tok: 8 (over y, x, core), head: 4 (over z).
Axes of the slice: x: 2, y: 2, z: 4, core: 2. Of those that a mesh axis runs over, the one named last changes fastest.
Arguments:
- tokens: bfloat16 [4096, 1536], P(('tok', 'head')), may hold values from -6 to 6
- segments: int32 [4096], replicated, may hold values from 0 to 63, never falling along the last dimension, each value on 1 to 512 neighbouring positions
- group_ids: int32 [64], replicated, may hold values from 0 to 7
- prefix_owner: int32 [8], replicated, may hold values from 0 to 7, each once
- slab_fill: int32 [8], replicated, may hold values from 256 to 512
- prefix_cache: bfloat16 [4096, 1024], P('tok', 'head'), may hold values from -400 to 400, as said below
- attn_gain: float32 [1536], replicated, may hold values from 0.5 to 1.5
- w_query: bfloat16 [1536, 1536], P(None, 'head'), may hold values from -0.15625 to 0.15625
- w_keyval: bfloat16 [1536, 1024], P(None, 'head'), may hold values from -0.15625 to 0.15625
- w_out: bfloat16 [1536, 1536], P('head'), may hold values from -0.15625 to 0.15625
- ffn_gain: float32 [1536], replicated, may hold values from 0.5 to 1.5
- routes: int32 [4096, 8], P(('tok', 'head')), may hold values from 0 to 31, all different within a row; in each aligned block of 128 rows (0 to 127, 128 to 255, ...) at most 64 rows name the same one
- route_gates: float32 [4096, 8], P(('tok', 'head')), may hold values from 0.05 to 0.5
- w_gate: bfloat16 [32, 1536, 512], P('tok'), may hold values from -0.15625 to 0.15625
- w_up: bfloat16 [32, 1536, 512], P('tok'), may hold values from -0.15625 to 0.15625
- w_down: bfloat16 [32, 512, 1536], P('tok'), may hold values from -0.25 to 0.25
Outputs:
- layer_out: bfloat16 [4096, 1536], P(('tok', 'head'))
Inputs may be any that keep to these rules, and one draw needn't show every extreme that they name: `segments`: request ids never fall along the tokens; every request has 1 to 512 tokens and some request exactly 512. `prefix_owner`: each group's prefix lies in exactly one slab. `prefix_cache`: keys are already rotated by their positions 0 to fill - 1; rows at fill and past it are padding. `routes`: each row names 8 different experts; the rows of one device name any expert at most 64 times.
All inputs are finite; a program needn't handle non-finite values.
Results may differ from a plain program's by a relative error of at most 0.012.
Values may be sent and summed in bfloat16 or wider, within the bound.
No kernel may reach another device: no remote copies, remote signals or barrier semaphores. Data moves between devices by JAX's collectives and lax.ppermute only.
A program may use at most 192 MiB of HBM per device.

v0:
```python
import jax
import jax.numpy as jnp
from jax import lax
from jax.sharding import PartitionSpec as P

HS = 64
EXPERTS = 32
TOPK = 8
PREFIX = 512
CAP = 64


NEG_FILL = -1e30
NORM_EPS = 1e-06
key_block = 512


def shifted(block, axis, distance):
    devices = range(lax.axis_size(axis))
    route = [(i - distance, i) for i in devices if i - distance in devices]
    return lax.ppermute(block, axis, route)


def rms_scale(values, gain):
    widened = values.astype(jnp.float32)
    spread = jnp.mean(widened * widened, axis=-1, keepdims=True)
    return widened * lax.rsqrt(spread + NORM_EPS) * gain


def lookup(table, index):
    entries = jnp.arange(table.shape[0], dtype=jnp.int32)
    return jnp.sum(jnp.where(index[..., None] == entries, table, 0), axis=-1)


def token_tables(segments, group_ids, prefix_owner, slab_fill):
    length_all = segments.shape[0]
    places = jnp.arange(length_all, dtype=jnp.int32)
    opening = jnp.concatenate([jnp.ones((1,), dtype=bool), segments[1:] != segments[:-1]])
    begins = lax.cummax(jnp.where(opening, places, 0), axis=0)
    slab_ids = lookup(prefix_owner, lookup(group_ids, segments))
    token_fill = lookup(slab_fill, slab_ids)
    return (slab_ids, token_fill, token_fill + places - begins)


def rope_angles(positions, head_size):
    steps_idx = jnp.arange(head_size // 2, dtype=jnp.float32)
    inverse = jnp.exp(steps_idx * (-2.0 * jnp.log(10000.0) / head_size))
    return positions.astype(jnp.float32)[:, None] * inverse[None, :]


def rotate(values, angles):
    halfway = values.shape[-1] // 2
    leading = values[..., :halfway]
    trailing = values[..., halfway:]
    cosine = jnp.cos(angles)[:, None, :]
    sine_v = jnp.sin(angles)[:, None, :]
    return jnp.concatenate(
        [leading * cosine - trailing * sine_v, trailing * cosine + leading * sine_v], axis=-1
    )


def absorb(carry, query_heads, key_rows, value_rows, visible):
    peak_old, weight_sum, accum = carry
    scores = jnp.einsum(
        "qgrd,kgd->qgrk", query_heads, key_rows, preferred_element_type=jnp.float32
    ) * HS ** (-0.5)
    shown = visible[:, None, None, :]
    scores = jnp.where(shown, scores, NEG_FILL)
    peak_new = jnp.maximum(peak_old, jnp.max(scores, axis=-1))
    weights = jnp.where(shown, jnp.exp(scores - peak_new[..., None]), 0.0)
    factor = jnp.exp(peak_old - peak_new)
    weight_sum = weight_sum * factor + jnp.sum(weights, axis=-1)
    accum = accum * factor[..., None] + jnp.einsum(
        "qgrk,kgd->qgrd",
        weights.astype(jnp.bfloat16),
        value_rows,
        preferred_element_type=jnp.float32,
    )
    return (peak_new, weight_sum, accum)


def local(
    tokens,
    segments,
    group_ids,
    prefix_owner,
    slab_fill,
    prefix_cache,
    attn_gain,
    w_query,
    w_keyval,
    w_out,
    ffn_gain,
    routes,
    route_gates,
    w_gate,
    w_up,
    w_down,
):
    tok_count = lax.axis_size("tok")
    head_count = lax.axis_size("head")
    tok_place = lax.axis_index("tok")
    rows_dev = tokens.shape[0]
    row_len = rows_dev * head_count
    row_first = tok_place * row_len
    kv_local = w_keyval.shape[1] // (2 * HS)
    q_local = w_query.shape[1] // HS
    group_share = q_local // kv_local
    slab_ids, token_fill, positions = token_tables(segments, group_ids, prefix_owner, slab_fill)
    row_pos = lax.dynamic_slice_in_dim(positions, row_first, row_len, 0)
    row_segs = lax.dynamic_slice_in_dim(segments, row_first, row_len, 0)
    row_slab = lax.dynamic_slice_in_dim(slab_ids, row_first, row_len, 0)
    normed = rms_scale(tokens, attn_gain).astype(jnp.bfloat16)
    piece = lax.all_gather(normed, "head", axis=0, tiled=True)
    projected = jnp.concatenate(
        [
            jnp.dot(piece, w_query, preferred_element_type=jnp.float32),
            jnp.dot(piece, w_keyval, preferred_element_type=jnp.float32),
        ],
        axis=1,
    )
    angles = rope_angles(row_pos, HS)
    query_part = projected[:, : q_local * HS].reshape(row_len, q_local, HS)
    keyval = projected[:, q_local * HS :].reshape(row_len, kv_local, 2, HS)
    query_flat = rotate(query_part, angles).astype(jnp.bfloat16).reshape(row_len, q_local * HS)
    query_heads = query_flat.reshape(row_len, kv_local, group_share, HS)
    key_rows = rotate(keyval[:, :, 0], angles)
    kv_now = (
        jnp.stack([key_rows, keyval[:, :, 1]], axis=2)
        .astype(jnp.bfloat16)
        .reshape(row_len, kv_local * 2 * HS)
    )
    kv_prev = shifted(kv_now, "tok", 1)
    near = jnp.concatenate([kv_prev, kv_now], axis=0).reshape(2 * row_len, kv_local, 2, HS)
    segs_pad = jnp.concatenate([jnp.full((row_len,), -1, jnp.int32), segments], axis=0)
    near_segs = lax.dynamic_slice_in_dim(segs_pad, row_first, 2 * row_len, 0)
    near_pos = row_first - row_len + jnp.arange(2 * row_len, dtype=jnp.int32)
    query_pos = row_first + jnp.arange(row_len, dtype=jnp.int32)
    near_mask = (near_segs[None, :] == row_segs[:, None]) & (
        near_pos[None, :] <= query_pos[:, None]
    )
    start_carry = (
        jnp.full((row_len, kv_local, group_share), NEG_FILL, jnp.float32),
        jnp.zeros((row_len, kv_local, group_share), jnp.float32),
        jnp.zeros((row_len, kv_local, group_share, HS), jnp.float32),
    )
    carry = absorb(start_carry, query_heads, near[:, :, 0], near[:, :, 1], near_mask)

    def one_block(state, block_rows, first_row):
        where_rows = first_row + jnp.arange(block_rows.shape[0], dtype=jnp.int32)
        slab_of = where_rows // PREFIX
        inside = where_rows - slab_of * PREFIX
        limit_rows = lookup(slab_fill, slab_of)
        visible = (slab_of[None, :] == row_slab[:, None]) & (inside < limit_rows)[None, :]
        split_rows = block_rows.reshape(block_rows.shape[0], kv_local, 2, HS)
        return absorb(state, query_heads, split_rows[:, :, 0], split_rows[:, :, 1], visible)

    state = carry
    piece = lax.all_gather(prefix_cache, "tok", axis=0, tiled=True)
    length_rows = piece.shape[0]
    stacked = piece.reshape(length_rows // key_block, key_block, piece.shape[1])

    def advance(inner_state, entry_pair):
        return (one_block(inner_state, entry_pair[0], entry_pair[1] * key_block), None)

    state, _ = lax.scan(
        advance, state, (stacked, jnp.arange(length_rows // key_block, dtype=jnp.int32))
    )
    carry = state
    final_peak, final_sum, final_acc = carry
    mixed = (final_acc / final_sum[..., None]).reshape(row_len, q_local * HS).astype(jnp.bfloat16)
    attended = lax.psum_scatter(
        jnp.dot(mixed, w_out, preferred_element_type=jnp.float32).astype(jnp.bfloat16),
        "head",
        scatter_dimension=0,
        tiled=True,
    ).astype(jnp.float32)
    hidden = tokens.astype(jnp.float32) + attended
    expert_in = rms_scale(hidden, ffn_gain).astype(jnp.bfloat16)
    exp_local = w_gate.shape[0]
    flat_routes = routes.reshape(-1)
    route_count = flat_routes.shape[0]
    onehot = flat_routes[:, None] == jnp.arange(EXPERTS, dtype=jnp.int32)[None, :]
    ranks = jnp.sum(jnp.where(onehot, jnp.cumsum(onehot.astype(jnp.int32), axis=0) - 1, 0), axis=1)
    slot_of = flat_routes * CAP + ranks
    source_row = jnp.arange(route_count, dtype=jnp.int32) // TOPK
    slot_token = jnp.zeros((EXPERTS * CAP,), jnp.int32).at[slot_of].set(source_row)
    slot_used = jnp.zeros((EXPERTS * CAP,), jnp.bool_).at[slot_of].set(True)
    outgoing = jnp.where(slot_used[:, None], expert_in[slot_token], 0.0)
    outgoing = outgoing.reshape(tok_count, exp_local, CAP, expert_in.shape[1])
    arrived = lax.all_to_all(outgoing, "tok", split_axis=0, concat_axis=0, tiled=True)
    gate_val = jnp.einsum("secd,edf->secf", arrived, w_gate, preferred_element_type=jnp.float32)
    up_val = jnp.einsum("secd,edf->secf", arrived, w_up, preferred_element_type=jnp.float32)
    inner_act = (jax.nn.silu(gate_val) * up_val).astype(jnp.bfloat16)
    answered = jnp.einsum(
        "secf,efd->secd", inner_act, w_down, preferred_element_type=jnp.float32
    ).astype(jnp.bfloat16)
    returned = lax.all_to_all(answered, "tok", split_axis=0, concat_axis=0, tiled=True).reshape(
        EXPERTS * CAP, expert_in.shape[1]
    )
    per_route = returned[slot_of].reshape(rows_dev, TOPK, expert_in.shape[1])
    mixture = hidden
    for choice_rank in range(TOPK):
        mixture = mixture + route_gates[:, choice_rank, None] * per_route[:, choice_rank].astype(
            jnp.float32
        )
    return mixture.astype(jnp.bfloat16)


def solution(mesh):
    return jax.shard_map(
        local,
        mesh=mesh,
        in_specs=(
            P(("tok", "head"), None),
            P(),
            P(),
            P(),
            P(),
            P("tok", "head"),
            P(),
            P(None, "head"),
            P(None, "head"),
            P("head", None),
            P(),
            P(("tok", "head"), None),
            P(("tok", "head"), None),
            P("tok", None, None),
            P("tok", None, None),
            P("tok", None, None),
        ),
        out_specs=P(("tok", "head"), None),
        check_vma=False,
    )
```

profile of v0, /device:TPU:0, one launch (start us, length us, event | category | flops | bytes accessed | tf_op | source)
XLA Modules:
  0.0 406.9 jit_solution(11464707548338416298)
XLA Ops:
  6.5 1.3 fusion.54
  7.8 1.9 fusion.56
  17.5 32.2 %all-gather.3.cloned.1.call-done = bf16[512,1536]{1,0:T(8,128)(2,1)} async-done(((bf16[128,1536]{1,0:T(8,128)(2,1)}), bf16[512,1536]{1,0:T(8,128)(2,1)}) %all-gather.3.cloned.1.call-update) | async-done | bytes 1572880 | tf_op jit(solution)/shard_map/all_gather | solution.py:114
  49.7 2.2 fusion.93
  52.1 1.6 collective-permute-start
  53.7 2.6 fusion.94
  56.5 2.1 fusion.19
  58.6 3.4 fusion.21
  62.0 3.9 fusion.51
  66.0 12.4 %all-gather.5.cloned.1.call-done = bf16[4096,256]{1,0:T(8,128)(2,1)} async-done(((bf16[512,256]{1,0:T(8,128)(2,1)}), bf16[4096,256]{1,0:T(8,128)(2,1)}) %all-gather.5.cloned.1.call-update) | async-done | bytes 2097168 | tf_op jit(solution)/shard_map/all_gather | solution.py:159
  78.4 60.3 %while.16 = (s32[]{:T(128)}, f32[512,2,3]{0,2,1:T(4,128)S(1)}, f32[512,2,3]{0,2,1:T(4,128)S(1)}, f32[512,2,3,64]{0,3,2,1:T(8,128)S(1)}, s32[8]{0:T(128)S(1)}, /*...) while((s32[]{:T(128)}, f32[512,2,3]{0,2,1:T(4,128)S(1)}, ...), condition=%wide.region_12.13_spmd, body=%wide.region_8.12_spmd.sunk | while | flops 424053760 | bytes 23418032 | solution.py:166
  81.1 1.2 fusion.111
  82.3 1.5 fusion.112
  83.8 2.0 fusion.113
  88.6 1.2 fusion.111
  89.8 1.5 fusion.112
  91.4 2.0 fusion.113
  96.2 1.2 fusion.111
  97.4 1.5 fusion.112
  98.9 2.0 fusion.113
  104.9 1.5 fusion.112
  106.5 2.0 fusion.113
  112.4 1.5 fusion.112
  114.0 2.0 fusion.113
  120.0 1.5 fusion.112
  121.5 2.0 fusion.113
  127.5 1.5 fusion.112
  129.1 2.0 fusion.113
  135.0 1.5 fusion.112
  136.6 2.0 fusion.113
  138.8 2.2 convolution_convert_fusion
  141.3 9.0 %reduce-window.19 = s32[32,8,128]{2,1,0:T(8,128)S(1)} reduce-window(s32[32,8,128]{2,1,0:T(8,128)S(1)} %fusion.75, s32[]{:T(128)} %constant.122.clone.1), window={size=1x1x128 pad=0_0x0_0x127_0}, to_apply=%region_14.15 | reduce-window | flops 4161536 | bytes 262148 | tf_op jit(solution)/shard_map/reduce-window.2
  151.1 4.3 %scatter_custom_fusion.1 = s32[2048]{0:T(1024)S(1)} fusion(s32[1024]{0:T(1024)S(1)} %bitcast.255, s32[1024]{0:T(1024)S(1)} %add_select_fusion.2, s32[]{:T(128)} %constant.122.clone.1), kind=kCustom, calls=%fused_computation.147 | custom fusion | bytes 8196 | tf_op jit(solution)/shard_map/scatter | solution.py:187
  155.4 4.6 %scatter_custom_fusion = pred[2048]{0:T(1024)(128)(4,1)S(1)} fusion(s32[1024]{0:T(1024)S(1)} %bitcast.256, pred[1024]{0:T(1024)(128)(4,1)S(1)} %broadcast.409, pred[]{:T(512)} %constant.140.clone.1), kind=kCustom, calls=%fused_computation.151 | custom fusion | bytes 2049 | tf_op jit(solution)/shard_map/scatter | solution.py:188
  160.1 16.6 %reduce-scatter.2.cloned.1.call-done = bf16[128,1536]{1,0:T(8,128)(2,1)} async-done(((bf16[512,1536]{1,0:T(8,128)(2,1)}), bf16[128,1536]{1,0:T(8,128)(2,1)}) %reduce-scatter.2.cloned.1.call-update) | async-done | bytes 393232 | tf_op jit(solution)/shard_map/reduce_scatter | solution.py:172
  176.6 1.2 multiply_reduce_fusion
  179.0 10.1 %gather_fusion = bf16[2048,1536]{1,0:T(8,128)(2,1)} fusion(bf16[128,1536]{1,0:T(8,128)(2,1)S(1)} %multiply_convert_fusion, s32[2048]{0:T(1024)S(1)} %fusion.76), kind=kCustom, calls=%fused_computation | custom fusion | bytes 12591104 | tf_op jit(solution)/shard_map/gather | solution.py:189
  189.1 3.3 broadcast_select_fusion
  192.4 74.9 %all_to_all.10 = bf16[8,4,64,1536]{3,2,1,0:T(8,128)(2,1)S(1)} all-to-all(bf16[8,4,64,1536]{3,2,1,0:T(8,128)(2,1)S(1)} %broadcast_select_fusion), channel_id=1, replica_groups=mesh['tok'=8,'head'=4] {'tok'}, dimensions={0} | all-to-all | bytes 12582912 | tf_op jit(solution)/shard_map/all_to_all | solution.py:191
  267.3 2.7 copy-done.3
  270.0 7.7 %fusion.26 = f32[4,8,64,512]{3,2,1,0:T(8,128)} fusion(bf16[4,1536,512]{2,1,0:T(8,128)(2,1)} %param.31, bf16[8,4,64,1536]{3,2,1,0:T(8,128)(2,1)S(1)} %all_to_all.10), kind=kOutput, calls=%fused_computation.44 | convolution fusion | flops 3221225472 | bytes 16777216 | tf_op jit(solution)/shard_map/secd,edf->secf/dot_general | solution.py:192
  277.7 13.0 %convert_bitcast_fusion = bf16[8,4,64,1536]{3,2,0,1:T(8,128)(2,1)} fusion(bf16[4,512,1536]{2,1,0:T(8,128)(2,1)} %param.33, f32[4,8,64,512]{3,2,1,0:T(8,128)} %fusion.26, bf16[4,1536,512]{2,1,0:T(8,128)(2,1)} %param.32, bf16[8,4,64,1536]{3,2,1,0:T(8,128)(2,1)} %copy-done.3), kind=kOutput, calls=%fused_computation.46 | convolution fusion | flops 6451888128 | bytes 29360128 | tf_op jit(solution)/shard_map/secf,efd->secd/dot_general | solution.py:195
  290.7 6.1 %copy.111 = bf16[8,4,64,1536]{3,2,1,0:T(8,128)(2,1)} copy(bf16[8,4,64,1536]{3,2,0,1:T(8,128)(2,1)} %convert_bitcast_fusion) | data formatting | bytes 12582912 | tf_op jit(solution)/shard_map/convert_element_type | solution.py:197
  296.8 5.1 %all-to-all-start.1 = ((bf16[8,4,64,1536]{3,2,1,0:T(8,128)(2,1)}), bf16[8,4,64,1536]{3,2,1,0:T(8,128)(2,1)}, u32[]{:S(2)}, u32[]{:S(2)}) async-start(bf16[8,4,64,1536]{3,2,1,0:T(8,128)(2,1)} %copy.111), calls=%async_computation.2 | async-start | bytes 12582912 | tf_op jit(solution)/shard_map/all_to_all | solution.py:198
  301.9 71.3 %all-to-all-done.1 = bf16[8,4,64,1536]{3,2,1,0:T(8,128)(2,1)} async-done(((bf16[8,4,64,1536]{3,2,1,0:T(8,128)(2,1)}), bf16[8,4,64,1536]{3,2,1,0:T(8,128)(2,1)}, u32[]{:S(2)}, u32[]{:S(2)}) %all-to-all-start.1) | async-done | bytes 6291488 | tf_op jit(solution)/shard_map/all_to_all | solution.py:198
  373.2 10.9 %gather_fusion.1 = bf16[1024,1536]{1,0:T(8,128)(2,1)} fusion(bf16[2048,1536]{1,0:T(8,128)(2,1)} %bitcast.45, s32[1024]{0:T(1024)S(1)} %broadcast_clamp_fusion), kind=kCustom, calls=%fused_computation.1 | custom fusion | bytes 6295552 | tf_op jit(solution)/shard_map/gather | solution.py:201
  384.2 14.7 %fusion.92 = (bf16[128,1,1536]{2,1,0:T(2,128)(2,1)S(1)}, bf16[128,1,1536]{2,1,0:T(2,128)(2,1)S(1)}, bf16[128,1,1536]{2,1,0:T(2,128)(2,1)S(1)}, bf16[128,1,1536]{...) fusion(bf16[128,8,1536]{2,1,0:T(8,128)(2,1)} %bitcast.238), kind=kLoop, calls=%fused_computation.177 | loop fusion | bytes 6291456 | tf_op jit(solution)/shard_map/slice | solution.py:204
  398.8 1.5 fusion.58
  (163 shorter events, 33.0 us)
Async XLA Ops:
  6.5 132.3 %copy-start = (bf16[384,1536]{1,0:T(8,128)(2,1)S(1)}, bf16[384,1536]{1,0:T(8,128)(2,1)}, u32[]{:S(2)}) copy-start(bf16[384,1536]{1,0:T(8,128)(2,1)} %param.27) | copy-start | bytes 3538948
  6.5 43.1 %all-gather.3.cloned.1.call-start = ((), (), s32[]{:S(2)}) async-start(), calls=%async_computation.3 | async-start | bytes 1966080 | tf_op jit(solution)/shard_map/all_gather | solution.py:114
  9.7 68.6 %all-gather.5.cloned.1.call-start = ((), (), s32[]{:S(2)}) async-start(), calls=%async_computation.4 | async-start | bytes 2359296 | tf_op jit(solution)/shard_map/all_gather | solution.py:159
  10.5 166.1 %reduce-scatter.2.cloned.1.call-start = ((), (), s32[]{:S(2)}) async-start(), calls=%async_computation.5 | async-start | bytes 1966080 | tf_op jit(solution)/shard_map/reduce_scatter | solution.py:172
  52.1 4.4 %collective-permute-start = (bf16[512,256]{0,1:T(8,128)(2,1)S(1)}, bf16[512,256]{0,1:T(8,128)(2,1)S(1)}, u32[]{:S(2)}, u32[]{:S(2)}) collective-permute-start(bf16[512,256]{0,1:T(8,128)(2,1)S(1)} %bitcast.252), channel_id=1, source_target_pairs={{0,4},{4,8},{8,12},{12,16},{16,20},{20,24},{24,28},{1,5},{5,9},{9,... | collective-permute-start | bytes 786440 | tf_op jit(solution)/shard_map/ppermute | solution.py:21
  62.0 16.3 %copy-start.5 = (s32[8]{0:T(128)S(1)}, s32[8]{0:T(128)}, u32[]{:S(2)}) copy-start(s32[8]{0:T(128)} %param.22) | copy-start | bytes 100
  78.4 62.6 %copy-start.6 = (s32[128,8]{0,1:T(8,128)S(1)}, s32[128,8]{0,1:T(8,128)}, u32[]{:S(2)}) copy-start(s32[128,8]{0,1:T(8,128)} %param.29) | copy-start | bytes 12292
  138.7 37.9 %copy-start.2 = (bf16[128,1536]{1,0:T(8,128)(2,1)S(1)}, bf16[128,1536]{1,0:T(8,128)(2,1)}, u32[]{:S(2)}) copy-start(bf16[128,1536]{1,0:T(8,128)(2,1)} %param.18) | copy-start | bytes 1179652
  138.7 39.2 %copy-start.7 = (f32[1536]{0:T(1024)S(1)}, f32[1536]{0:T(1024)}, u32[]{:S(2)}) copy-start(f32[1536]{0:T(1024)} %param.28) | copy-start | bytes 18436
  267.3 2.7 copy-start.3
  296.8 5.2 %copy-start.8 = (f32[128,8]{0,1:T(8,128)S(1)}, f32[128,8]{0,1:T(8,128)}, u32[]{:S(2)}) copy-start(f32[128,8]{0,1:T(8,128)} %param.30) | copy-start | bytes 12292
  296.8 76.5 %all-to-all-start.1 = ((bf16[8,4,64,1536]{3,2,1,0:T(8,128)(2,1)}), bf16[8,4,64,1536]{3,2,1,0:T(8,128)(2,1)}, u32[]{:S(2)}, u32[]{:S(2)}) async-start(bf16[8,4,64,1536]{3,2,1,0:T(8,128)(2,1)} %copy.111), calls=%async_computation.2 | async-start | bytes 12582912 | tf_op jit(solution)/shard_map/all_to_all | solution.py:198
  384.2 14.7 %copy-start.4 = (bf16[128,1536]{1,0:T(8,128)(2,1)S(1)}, bf16[128,1536]{1,0:T(8,128)(2,1)}, u32[]{:S(2)}) copy-start(bf16[128,1536]{1,0:T(8,128)(2,1)} %reduce-scatter.2.cloned.1.call-done) | copy-start | bytes 1179652
  384.2 16.2 %copy-start.1 = (bf16[384,1536]{1,0:T(8,128)(2,1)S(1)}, bf16[384,1536]{1,0:T(8,128)(2,1)}, u32[]{:S(2)}) copy-start(bf16[384,1536]{1,0:T(8,128)(2,1)} %param.27) | copy-start | bytes 3538948
Sparse Core Ops, SparseCore 0:
  9.9 39.7 all-gather.2
  51.6 26.7 all-gather.4
  141.1 35.4 reduce-scatter.1
where the time goes:
time: 408 us; the launch traced here: 407 us
  waiting for transfers between devices  133 us (33%)
  blocking collectives  74.9 us (18%)
  local copies, waits for them, and re-layouts  69 us (17%)
  matrix products  59.2 us (15%)
  other arithmetic  44.5 us (11%)
  between operations  13.5 us (3%)
  starting transfers between devices  6.85 us (2%)
  loops' own time  5.78 us (1%)
    all_to_all x1, blocking collectives, local(): lax.all_to_all(outgoing, 'tok', split_axis=0, concat_axis=0, tiled=True)  74.9 us
    all_to_all x1, waiting for transfers between devices, local(): lax.all_to_all(answered, 'tok', split_axis=0, concat_axis=0, tiled=True)  71.3 us
    all_gather x1, waiting for transfers between devices, local(): piece = lax.all_gather(normed, 'head', axis=0, tiled=True)  32.2 us
    dot_general x9, matrix products, absorb(): jnp.einsum('qgrk,kgd->qgrd', weights.astype(jnp.bfloat16), value_rows, pr...  20.2 us
    reduce_scatter x1, waiting for transfers between devices, local(): lax.psum_scatter(jnp.dot(mixed, w_out, preferred_element_type=jnp.float32...  16.6 us
    reduce_sum x9, other arithmetic, absorb(): weight_sum = weight_sum * factor + jnp.sum(weights, axis=-1)  15.5 us
    slice x1, local copies, waits for them, and re-layouts, local(): per_route[:, choice_rank].astype(jnp.float32)  14.7 us
    dynamic_slice x24, local copies, waits for them, and re-layouts, local(): lax.scan(advance, state, (stacked, jnp.arange(length_rows // key_block, d...  13.6 us
  transfers between devices with their start and end apart: 5, of which 4 were waited for; matrix products, arithmetic and copies ran while one was open for 10% of the time, Pallas kernels for 0%

commit v1 on v0

v1 whole, which is shorter than its diff:
```python
import functools

import jax
import jax.numpy as jnp
from jax import lax
from jax.experimental import pallas as pl
from jax.experimental.pallas import tpu as pltpu
from jax.sharding import PartitionSpec as P

HS = 64
CAP = 64
PREFIX = 512
LANES = 128
NEG_FILL = -1e30
NORM_EPS = 1e-06
F32 = jnp.float32
BF16 = jnp.bfloat16
VMEM_BYTES = 56 * 1024 * 1024


def vmem(*shape):
    return pl.BlockSpec(memory_space=pltpu.VMEM)


ANY = pl.BlockSpec(memory_space=pl.ANY)
SMEM = pl.BlockSpec(memory_space=pltpu.SMEM)


def params(**more):
    return pltpu.CompilerParams(vmem_limit_bytes=VMEM_BYTES, **more)


def lookup(table, index):
    entries = jnp.arange(table.shape[0], dtype=jnp.int32)
    return jnp.sum(jnp.where(index[..., None] == entries, table, 0), axis=-1)


def ring(block, axis, step):
    count = lax.axis_size(axis)
    route = [(i, (i + step) % count) for i in range(count)]
    held = [block]
    for _ in range(count - 1):
        held.append(lax.ppermute(held[-1], axis, route))
    return held


def cube_routes():
    first = [(t, t ^ (2 if t & 1 else 4)) for t in range(8)]
    second = [(t, t ^ (4 if t & 1 else 2)) for t in range(8)]
    partner = [(t, t ^ 1) for t in range(8)]
    return first, second, partner


def plane_origins():
    count = lax.axis_size("tok")
    if count != 8:
        return jnp.arange(count, dtype=jnp.int32)
    me = lax.axis_index("tok")
    one = jnp.where(me % 2 == 0, 4, 2)
    two = 6 - one
    other = me ^ 1
    return jnp.stack(
        [me, me ^ one, me ^ two, me ^ 6, other, other ^ two, other ^ one, other ^ 6]
    ).astype(jnp.int32)


def plane_gather(block, split, joined, ties=(None, None, None)):
    count = lax.axis_size("tok")
    rows = block.shape[0]
    if count != 8:
        whole = lax.all_gather(block, "tok", axis=0, tiled=True)
        return [[(whole, i * rows, rows)] for i in range(count)]
    first, second, partner = cube_routes()

    def to_partner(array):
        return lax.ppermute(array, "tok", partner)

    block = after(block, ties[0])
    half = rows // 2
    one = lax.ppermute(block, "tok", first)
    two = lax.ppermute(block, "tok", second)
    one, two = after((one, two), ties[1])
    if split:
        three = [
            lax.ppermute(one[:half], "tok", second),
            lax.ppermute(two[half:], "tok", first),
        ]
    else:
        three = [lax.ppermute(block, "tok", [(t, t ^ 6) for t in range(8)])]
    if not joined:
        mine = [[block], [one], [two], three]
        every = mine + [[to_partner(piece) for piece in pieces] for pieces in mine]
        return [[(piece, 0, piece.shape[0]) for piece in pieces] for pieces in every]
    if split:
        head = jnp.concatenate([block, one, two], axis=0)
        tail = jnp.concatenate(three, axis=0)
        sides = [(head, tail), (to_partner(head), to_partner(tail))]
        return [
            [(side[0], i * rows, rows)] if i < 3 else [(side[1], 0, rows)]
            for side in sides
            for i in range(4)
        ]
    every = after(jnp.concatenate([block, one, two] + three, axis=0), ties[2])
    return [
        [(side, i * rows, rows)] for side in (every, to_partner(every)) for i in range(4)
    ]


def flatten(blocks):
    arrays, spec = [], []
    for pieces in blocks:
        here = []
        for array, first, rows in pieces:
            known = [i for i, other in enumerate(arrays) if other is array]
            if not known:
                known = [len(arrays)]
                arrays.append(array)
            here.append((known[0], first, rows))
        spec.append(here)
    return arrays, spec


def row_ranges(pieces, first, count):
    base = 0
    for array, start, rows in pieces:
        low, high = max(first, base), min(first + count, base + rows)
        if low < high:
            yield array, start + low - base, low - first, high - low
        base += rows


def after(value, tie):
    return value if tie is None else lax.optimization_barrier((value, tie))[0]


def plane_sum(near, far, last, rows):
    count = lax.axis_size("tok")
    if count != 8:
        every = jnp.concatenate([near, far, last], axis=0)
        return lax.psum_scatter(every, "tok", scatter_dimension=0, tiled=True).astype(F32)
    first, second, partner = cube_routes()
    half = rows // 2
    got_last = lax.ppermute(last, "tok", partner)
    got = lax.ppermute(far, "tok", partner)
    three = (near[3 * rows :].astype(F32) + got_last.astype(F32)).astype(BF16)
    across_upper = lax.ppermute(three[:half], "tok", second)
    across_lower = lax.ppermute(three[half:], "tok", first)
    near, got = after((near, got), (across_upper, across_lower))

    def pair(block):
        here = slice(block * rows, (block + 1) * rows)
        return near[here].astype(F32) + got[here].astype(F32)

    nothing = jnp.zeros(across_upper.shape, F32)
    add_upper = jnp.concatenate([across_upper.astype(F32), nothing], axis=0)
    add_lower = jnp.concatenate([nothing, across_lower.astype(F32)], axis=0)
    along = lax.ppermute((pair(1) + add_upper).astype(BF16), "tok", first)
    beside = lax.ppermute((pair(2) + add_lower).astype(BF16), "tok", second)
    return pair(0) + beside.astype(F32) + along.astype(F32)


def project_kernel(blocks, kv_local, q_local, *refs):
    pieces = refs[:blocks]
    gain, wq, wkv, cos, sin = refs[blocks : blocks + 5]
    q_outs = refs[blocks + 5 : 2 * blocks + 5]
    kv_out, normed = refs[2 * blocks + 5 :]
    half = pieces[0].shape[0]
    for i, piece in enumerate(pieces):
        wide = piece[...].astype(F32)
        spread = jnp.mean(wide * wide, axis=-1, keepdims=True)
        normed[i * half : (i + 1) * half, :] = (
            wide * lax.rsqrt(spread + NORM_EPS) * gain[...]
        ).astype(BF16)
    share = q_local // kv_local
    rows = normed.shape[0]
    rows_dev = rows // blocks
    lane = lax.broadcasted_iota(jnp.int32, (rows, LANES), 1)
    low_half = lane % HS < HS // 2
    low_head = lane < HS

    def turned(values, cosine, sine):
        swapped = jnp.where(
            low_half, pltpu.roll(values, LANES - HS // 2, 1), pltpu.roll(values, HS // 2, 1)
        )
        return values * cosine + swapped * sine

    cosine = cos[...]
    sine = sin[...]
    keyval = jnp.dot(normed[...], wkv[...], preferred_element_type=F32)
    cosine_kv = jnp.where(low_head, cosine, 1.0)
    sine_kv = jnp.where(low_head, sine, 0.0)
    for g in range(kv_local):
        here = slice(g * LANES, (g + 1) * LANES)
        kv_out[:, here] = turned(keyval[:, here], cosine_kv, sine_kv).astype(BF16)
    queries = jnp.dot(normed[...], wq[...], preferred_element_type=F32)
    for pair in range(queries.shape[1] // LANES):
        both = turned(queries[:, pair * LANES : (pair + 1) * LANES], cosine, sine) * HS ** (-0.5)
        for odd in range(2):
            head = 2 * pair + odd
            if head >= q_local:
                continue
            alone = pltpu.roll(both, HS, 1) if odd else both
            alone = jnp.where(low_head, alone, 0.0).astype(BF16)
            group, slot = head // share, head % share
            for j in range(blocks):
                q_outs[j][group, slot * rows_dev : (slot + 1) * rows_dev, :] = alone[
                    j * rows_dev : (j + 1) * rows_dev
                ]


def project(pieces, gain, w_query, w_keyval, cos, sin, kv_local, q_local):
    blocks = len(pieces)
    rows_dev, width = pieces[0].shape
    share = q_local // kv_local
    outs = pl.pallas_call(
        functools.partial(project_kernel, blocks, kv_local, q_local),
        out_shape=[jax.ShapeDtypeStruct((kv_local, share * rows_dev, LANES), BF16)] * blocks
        + [jax.ShapeDtypeStruct((blocks * rows_dev, kv_local * LANES), BF16)],
        in_specs=[vmem()] * (blocks + 5),
        out_specs=[vmem()] * (blocks + 1),
        scratch_shapes=[pltpu.VMEM((blocks * rows_dev, width), BF16)],
        compiler_params=params(),
        cost_estimate=pl.CostEstimate(
            flops=4 * 10**9, bytes_accessed=4 * 10**6, transcendentals=blocks * rows_dev
        ),
        name="norm_project_rotate",
    )(*pieces, gain, w_query, w_keyval, cos.reshape(-1, LANES), sin.reshape(-1, LANES))
    return list(outs[:-1]), outs[-1]


def attend_kernel(
    first, blocks, near_parts, slab_spec, q_local, near_list, reach, slab_list, slab_count, fill, slab_id, place, info, *refs
):
    parts = near_list.shape[0]
    total_in = blocks + near_parts + 1 + max(array for [(array, _, _)] in slab_spec)
    q_refs = refs[:blocks]
    near_refs = refs[blocks : blocks + near_parts]
    slab_refs = refs[blocks + near_parts : total_in]
    outs = refs[total_in : total_in + blocks]
    q_all, near, far, scores, peak, total, accum, begin, owner, heads, sems, slab_sems = refs[
        total_in + blocks :
    ]
    kv_local, stack, _ = q_refs[0].shape
    rows_dev = info.shape[1]
    share = stack // rows_dev
    cuts = PREFIX // LANES
    window = parts + 1
    wide = (stack, LANES)
    lane = lax.broadcasted_iota(jnp.int32, (1, LANES), 1)

    def lanes(ref, g, rows, start=0):
        return ref.at[pl.ds(start, rows), pl.ds(g * LANES, LANES)]

    copies = [
        pltpu.make_async_copy(ref, q_all.at[i], sems.at[i, 0]) for i, ref in enumerate(q_refs)
    ]
    base = 0
    for i, ref in enumerate(near_refs):
        for g in range(kv_local):
            copies.append(
                pltpu.make_async_copy(
                    lanes(ref, g, ref.shape[0]),
                    near.at[g, pl.ds(base, ref.shape[0])],
                    sems.at[blocks + i, g],
                )
            )
        base += ref.shape[0]
    slab_copies = [
        pltpu.make_async_copy(
            lanes(slab_refs[array], g, rows, start),
            far.at[g, pl.ds(i * PREFIX, PREFIX)],
            slab_sems.at[i, g],
        )
        for i, [(array, start, rows)] in enumerate(slab_spec)
        for g in range(kv_local)
    ]
    for copy in copies + slab_copies:
        copy.start()
    for copy in copies + slab_copies:
        copy.wait()

    @pl.loop(0, blocks)
    def _(i):
        block = lax.rem(first + i, parts)
        columns = info[block]
        for ref, column in ((owner, 0), (begin, 1)):
            tall = jnp.concatenate([columns[:, column : column + 1]] * share, axis=0)
            ref[...] = jnp.broadcast_to(tall, wide)
        row = lax.broadcasted_iota(jnp.int32, wide, 0)
        order = row - lax.div(row, rows_dev) * rows_dev

        def rows_near(g, back):
            unit = near_list[block, back]
            return near[g, pl.ds(pl.multiple_of(unit * rows_dev, rows_dev), rows_dev), :]

        def rows_window(g, backs):
            return jnp.concatenate([rows_near(g, back) for back in backs], axis=0)

        def rows_far(g, slab):
            return far[g, pl.ds(pl.multiple_of(slab * PREFIX, PREFIX), PREFIX), :]

        def score(g, rows):
            return lax.dot_general(
                q_all[i, g], rows, (((1,), (1,)), ((), ())), preferred_element_type=F32
            )

        def near_scores(backs, opening):
            for g in range(kv_local):
                every = score(g, rows_window(g, backs))
                top = None if opening else peak[g]
                for at, back in enumerate(backs):
                    there = place[near_list[block, back]] + lane
                    seen = there >= begin[...]
                    if back == 0:
                        seen = seen & (lane <= order)
                    here = every[:, at * LANES : (at + 1) * LANES]
                    here = jnp.where(seen, here, NEG_FILL)
                    scores[g, back] = here
                    top = here if top is None else jnp.maximum(top, here)
                peak[g] = top

        def far_scores(slab):
            mine = owner[...] == slab_id[slab]
            for g in range(kv_local):
                every = score(g, rows_far(g, slab))
                top = None
                for c in range(cuts):
                    here = every[:, c * LANES : (c + 1) * LANES]
                    if (c + 1) * LANES > PREFIX // 2:
                        here = jnp.where(lane + c * LANES < fill[slab], here, NEG_FILL)
                    scores[g, window + slab * cuts + c] = here
                    top = here if top is None else jnp.maximum(top, here)
                old = peak[g]
                peak[g] = jnp.where(mine, jnp.maximum(old, top), old)

        def near_values(backs, opening):
            for g in range(kv_local):
                weights = [jnp.exp(scores[g, back] - peak[g]) for back in backs]
                packed = jnp.concatenate([part.astype(BF16) for part in weights], axis=1)
                summed = functools.reduce(jnp.add, weights)
                mixed = jnp.dot(packed, rows_window(g, backs), preferred_element_type=F32)
                if opening:
                    total[g] = summed
                    accum[g] = mixed
                else:
                    total[g] += summed
                    accum[g] += mixed

        def far_values(slab):
            mine = owner[...] == slab_id[slab]
            for g in range(kv_local):
                shift = jnp.where(mine, peak[g], -NEG_FILL)
                weights = [
                    jnp.exp(scores[g, window + slab * cuts + c] - shift) for c in range(cuts)
                ]
                packed = jnp.concatenate([part.astype(BF16) for part in weights], axis=1)
                total[g] += functools.reduce(jnp.add, weights)
                accum[g] += jnp.dot(packed, rows_far(g, slab), preferred_element_type=F32)

        def sweep(near_body, far_body):
            near_body((0, 1), True)

            @pl.when(reach[block] != 0)
            def _():
                near_body(tuple(range(2, window)), False)

            @pl.loop(0, slab_count[block])
            def _(turn):
                far_body(slab_list[block, turn])

        sweep(near_scores, far_scores)
        for g in range(kv_local):
            peak[g] = jnp.broadcast_to(jnp.max(peak[g], axis=1, keepdims=True), wide)
        sweep(near_values, far_values)
        for g in range(kv_local):
            result = accum[g] / jnp.sum(total[g], axis=1, keepdims=True)
            for slot in range(share):
                heads[g * share + slot] = result[slot * rows_dev : (slot + 1) * rows_dev]

        low = lax.broadcasted_iota(jnp.int32, (rows_dev, LANES), 1) < HS
        done = []
        for pair in range((q_local + 1) // 2):
            left = pltpu.roll(heads[2 * pair], HS, 1)
            if 2 * pair + 1 < q_local:
                done.append(jnp.where(low, left, heads[2 * pair + 1]).astype(BF16))
            else:
                done.append(left[:, :HS].astype(BF16))
        for j in range(blocks):
            @pl.when(i == j)
            def _(j=j):
                for pair, part in enumerate(done):
                    outs[j][:, pair * LANES : pair * LANES + part.shape[1]] = part


def attend(first, tables, info, queries, near, slabs, q_local):
    blocks = len(queries)
    parts = info.shape[0]
    kv_local, stack, _ = queries[0].shape
    rows_dev = info.shape[1]
    units = parts + 1 + len(slabs) * (PREFIX // LANES)
    arrays, slab_spec = flatten(slabs)
    wide = (stack, LANES)
    return pl.pallas_call(
        functools.partial(attend_kernel, first, blocks, len(near), slab_spec, q_local),
        out_shape=[jax.ShapeDtypeStruct((rows_dev, q_local * HS), BF16)] * blocks,
        in_specs=[SMEM] * 7 + [vmem()] + [ANY] * (blocks + len(near) + len(arrays)),
        out_specs=[vmem()] * blocks,
        scratch_shapes=[
            pltpu.VMEM((blocks,) + queries[0].shape, BF16),
            pltpu.VMEM((kv_local, 2 * parts * rows_dev, LANES), BF16),
            pltpu.VMEM((kv_local, len(slabs) * PREFIX, LANES), BF16),
            pltpu.VMEM((kv_local, units) + wide, F32),
            pltpu.VMEM((kv_local,) + wide, F32),
            pltpu.VMEM((kv_local,) + wide, F32),
            pltpu.VMEM((kv_local,) + wide, F32),
            pltpu.VMEM(wide, jnp.int32),
            pltpu.VMEM(wide, jnp.int32),
            pltpu.VMEM((q_local, rows_dev, LANES), F32),
            pltpu.SemaphoreType.DMA((blocks + len(near), kv_local)),
            pltpu.SemaphoreType.DMA((len(slabs), kv_local)),
        ],
        compiler_params=params(),
        cost_estimate=pl.CostEstimate(
            flops=12 * 10**9, bytes_accessed=4 * 10**6, transcendentals=10**6
        ),
        name="attend",
    )(
        tables["near_list"],
        tables["reach"],
        tables["slab_list"],
        tables["slab_count"],
        tables["fill"],
        tables["slab_id"],
        tables["place"],
        info,
        *queries,
        *near,
        *arrays,
    )


def out_kernel(groups, cut, spec, origins, *refs):
    pieces = refs[:groups]
    w_own = refs[groups]
    w_far = refs[groups + 1 : -7]
    tokens, gain, hidden, expert_in, weights, sems, own_sem = refs[-7:]
    own = pltpu.make_async_copy(w_own, weights.at[0], own_sem)
    own.start()
    copies = []
    for k, pieces_k in enumerate(spec):
        if cut:
            first = pl.multiple_of(origins[k] * cut, 16)
            for j in range(groups - 1):
                for i, (array, there, offset, rows) in enumerate(
                    row_ranges(pieces_k, j * cut, cut)
                ):
                    copies.append(
                        pltpu.make_async_copy(
                            w_far[array].at[pl.ds(there, rows)],
                            weights.at[j + 1, pl.ds(first + offset, rows)],
                            sems.at[k, 2 * j + i],
                        )
                    )
        else:
            copies.append(
                pltpu.make_async_copy(w_far[pieces_k[0][0]], weights.at[k + 1], sems.at[k, 0])
            )
    for copy in copies:
        copy.start()
    own.wait()
    total = tokens[...].astype(F32) + jnp.dot(
        pieces[0][...], weights[0], preferred_element_type=F32
    )
    for copy in copies:
        copy.wait()
    for j in range(1, groups):
        total += jnp.dot(pieces[j][...], weights[j], preferred_element_type=F32)
    hidden[...] = total
    spread = jnp.mean(total * total, axis=-1, keepdims=True)
    expert_in[...] = (total * lax.rsqrt(spread + NORM_EPS) * gain[...]).astype(BF16)


def project_out(pieces, w_own, w_far, cut, origins, tokens, gain):
    groups = len(pieces)
    rows, width = tokens.shape
    w_far, spec = flatten(w_far)
    return pl.pallas_call(
        functools.partial(out_kernel, groups, cut, spec),
        out_shape=(
            jax.ShapeDtypeStruct((rows, width), F32),
            jax.ShapeDtypeStruct((rows, width), BF16),
        ),
        in_specs=[SMEM] + [vmem()] * groups + [ANY] * (1 + len(w_far)) + [vmem(), vmem()],
        out_specs=(vmem(), vmem()),
        scratch_shapes=[
            pltpu.VMEM((groups,) + w_own.shape, BF16),
            pltpu.SemaphoreType.DMA((len(spec), 2 * groups)),
            pltpu.SemaphoreType.DMA,
        ],
        compiler_params=params(),
        cost_estimate=pl.CostEstimate(
            flops=5 * 10**9,
            bytes_accessed=2 * groups * w_own.size + 8 * rows * width,
            transcendentals=rows,
        ),
        name="project_out_norm",
    )(origins, *pieces, w_own, *w_far, tokens, gain)


def expert_kernel(spec, rows, slot_row, gate_row, slot_col, *refs):
    count = len(spec)
    many = len(refs) - 15
    x_refs = refs[:many]
    wg_ref, wu_ref, wd_ref, near, far, last = refs[many : many + 6]
    x_all, wg, wu, wd, picked, answered, inner, x_sem, w_sem = refs[many + 6 :]
    exp_local = wg.shape[0]
    width = x_all.shape[1]
    span = 2 * rows
    slots = 2 * CAP
    pairs = count // 2
    chunk = 512

    x_copies = []
    base = 0
    for array, there, many_rows in [piece for pieces in spec for piece in pieces]:
        x_copies.append(
            pltpu.make_async_copy(
                x_refs[array].at[pl.ds(there, many_rows)],
                x_all.at[pl.ds(base, many_rows)],
                x_sem.at[len(x_copies)],
            )
        )
        base += many_rows
    for copy in x_copies:
        copy.start()

    def w_copies(e):
        return [
            pltpu.make_async_copy(source.at[e], target.at[e], w_sem.at[e, i])
            for i, (source, target) in enumerate(((wg_ref, wg), (wu_ref, wu), (wd_ref, wd)))
        ]

    for e in range(exp_local):
        for copy in w_copies(e):
            copy.start()
    for copy in x_copies:
        copy.wait()

    slot_iota = lax.broadcasted_iota(jnp.int32, (slots, span), 0)

    def pair_hits(e, b):
        there = slice(b * span, (b + 1) * span)
        return slot_iota == slot_row[pl.ds(e, 1), there]

    for b in range(pairs):
        hits = [jnp.where(pair_hits(e, b), 1.0, 0.0).astype(BF16) for e in range(exp_local)]
        chooser = jnp.concatenate(hits, axis=0)
        for c in range(0, width, chunk):
            found = jnp.dot(
                chooser,
                x_all[b * span : (b + 1) * span, c : c + chunk],
                preferred_element_type=F32,
            ).astype(BF16)
            for e in range(exp_local):
                picked[e, b * slots : (b + 1) * slots, c : c + chunk] = found[
                    e * slots : (e + 1) * slots
                ]

    @pl.loop(0, exp_local)
    def _(e):
        for copy in w_copies(e):
            copy.wait()
        rows_in = picked[e]
        for c in range(0, inner.shape[1], 256):
            gate = jnp.dot(rows_in, wg[e, :, c : c + 256], preferred_element_type=F32)
            up = jnp.dot(rows_in, wu[e, :, c : c + 256], preferred_element_type=F32)
            inner[:, c : c + 256] = (gate / (1.0 + jnp.exp(-gate)) * up).astype(BF16)
        scale = jnp.concatenate(
            [
                jnp.sum(
                    jnp.where(
                        pair_hits(e, b), gate_row[pl.ds(e, 1), b * span : (b + 1) * span], 0.0
                    ),
                    axis=1,
                    keepdims=True,
                )
                for b in range(pairs)
            ],
            axis=0,
        )
        for c in range(0, width, chunk):
            answer = jnp.dot(inner[...], wd[e, :, c : c + chunk], preferred_element_type=F32)
            answer = (answer * scale).astype(BF16)
            for b in range(pairs):
                first = pl.multiple_of(e * slots, slots)
                answered[b, pl.ds(first, slots), c : c + chunk] = answer[
                    b * slots : (b + 1) * slots
                ]

    lane = lax.broadcasted_iota(jnp.int32, (span, slots), 1)
    for b in range(pairs):
        there = slice(b * span, (b + 1) * span)
        spreader = jnp.concatenate(
            [
                jnp.where(lane == slot_col[there, e : e + 1], 1.0, 0.0).astype(BF16)
                for e in range(exp_local)
            ],
            axis=1,
        )
        for c in range(0, width, chunk):
            sums = jnp.dot(
                spreader, answered[b, :, c : c + chunk], preferred_element_type=F32
            ).astype(BF16)
            base = (b - pairs // 2) * span
            if b < pairs // 2:
                near[b * span : (b + 1) * span, c : c + chunk] = sums
            elif b < pairs - 1:
                far[base : base + span, c : c + chunk] = sums
            else:
                far[base : base + rows, c : c + chunk] = sums[:rows]
                last[:, c : c + chunk] = sums[rows:]


def experts(blocks, slot_row, gate_row, slot_col, w_gate, w_up, w_down):
    count = len(blocks)
    pieces, spec = flatten(blocks)
    parts = sum(len(one) for one in spec)
    rows, width = blocks[0][0][2], pieces[0].shape[1]
    exp_local, _, hidden = w_gate.shape
    pairs = count // 2
    slots = 2 * CAP
    work = exp_local * pairs * slots
    return pl.pallas_call(
        functools.partial(expert_kernel, spec, rows),
        out_shape=tuple(
            jax.ShapeDtypeStruct((many * rows, width), BF16)
            for many in (count // 2, count // 2 - 1, 1)
        ),
        in_specs=[vmem()] * 3 + [ANY] * (len(pieces) + 3),
        out_specs=(vmem(), vmem(), vmem()),
        scratch_shapes=[
            pltpu.VMEM((count * rows, width), BF16),
            pltpu.VMEM(w_gate.shape, BF16),
            pltpu.VMEM(w_up.shape, BF16),
            pltpu.VMEM(w_down.shape, BF16),
            pltpu.VMEM((exp_local, pairs * slots, width), BF16),
            pltpu.VMEM((pairs, exp_local * slots, width), BF16),
            pltpu.VMEM((pairs * slots, hidden), BF16),
            pltpu.SemaphoreType.DMA((parts,)),
            pltpu.SemaphoreType.DMA((exp_local, 3)),
        ],
        compiler_params=params(),
        cost_estimate=pl.CostEstimate(
            flops=2 * work * width * (3 * hidden + 4 * rows),
            bytes_accessed=2 * (3 * w_gate.size + 2 * count * rows * width),
            transcendentals=work * hidden,
        ),
        name="experts",
    )(slot_row, gate_row, slot_col, *pieces, w_gate, w_up, w_down)


def packed_routes(routes, route_gates, lanes):
    parts = [routes.T.astype(BF16)]
    rest = route_gates.T
    for _ in range(3):
        term = lax.reduce_precision(rest, 8, 7)
        parts.append(term.astype(BF16))
        rest = rest - term
    per = len(parts) * LANES // lanes
    return jnp.concatenate(
        [jnp.concatenate(parts[i : i + per], axis=0) for i in range(0, len(parts), per)], axis=1
    )


def route_kernel(spec, first_expert, *refs):
    count = len(spec)
    sources = refs[:-5]
    slot_row, gate_row, slot_col, packed, sems = refs[-5:]
    exp_local = slot_row.shape[0]
    tall = packed.shape[1]
    copies = [
        pltpu.make_async_copy(
            sources[array].at[pl.ds(there + rows - tall, tall), pl.ds(0, packed.shape[2])],
            packed.at[k],
            sems.at[k],
        )
        for k, (array, there, rows) in enumerate(pieces[-1] for pieces in spec)
    ]
    for copy in copies:
        copy.start()
    for copy in copies:
        copy.wait()
    here = lax.broadcasted_iota(jnp.int32, (LANES, LANES), 1)
    there = lax.broadcasted_iota(jnp.int32, (LANES, LANES), 0)
    earlier = jnp.where(there < here, 1.0, 0.0).astype(BF16)
    choices = tall * packed.shape[2] // (4 * LANES)
    for k in range(count):
        block = packed[k].astype(F32)
        parts = [
            block[r : r + choices, c : c + LANES]
            for c in range(0, packed.shape[2], LANES)
            for r in range(0, tall, choices)
        ]
        named = parts[0]
        gates = parts[1] + parts[2] + parts[3]
        hits, shares = [], []
        for e in range(exp_local):
            match = named == (first_expert[0] + e).astype(F32)
            hits.append(jnp.max(jnp.where(match, 1.0, 0.0), axis=0, keepdims=True))
            shares.append(jnp.sum(jnp.where(match, gates, 0.0), axis=0, keepdims=True))
        hits += [jnp.zeros((1, LANES), F32)] * (8 - exp_local)
        hit = jnp.concatenate(hits, axis=0)
        rank = jnp.dot(hit.astype(BF16), earlier, preferred_element_type=F32)
        slot = jnp.where(hit > 0.0, rank + float(k % 2 * CAP), -1.0)
        lanes = slice(k * LANES, (k + 1) * LANES)
        slot_row[:, lanes] = slot[:exp_local].astype(jnp.int32)
        gate_row[:, lanes] = jnp.concatenate(shares, axis=0)
        slot_col[lanes, :] = slot.T.astype(jnp.int32)


def route_tables(sources, tall, lanes, first_expert, exp_local):
    count = len(sources)
    sources, spec = flatten(sources)
    tokens = count * LANES
    return pl.pallas_call(
        functools.partial(route_kernel, spec),
        out_shape=(
            jax.ShapeDtypeStruct((exp_local, tokens), jnp.int32),
            jax.ShapeDtypeStruct((exp_local, tokens), F32),
            jax.ShapeDtypeStruct((tokens, 8), jnp.int32),
        ),
        in_specs=[SMEM] + [ANY] * len(sources),
        out_specs=(vmem(), vmem(), vmem()),
        scratch_shapes=[
            pltpu.VMEM((count, tall, lanes), BF16),
            pltpu.SemaphoreType.DMA((count,)),
        ],
        compiler_params=params(),
        cost_estimate=pl.CostEstimate(
            flops=3 * 10**9, bytes_accessed=10**6, transcendentals=0
        ),
        name="route_tables",
    )(first_expert, *sources)


def local(
    tokens,
    segments,
    group_ids,
    prefix_owner,
    slab_fill,
    prefix_cache,
    attn_gain,
    w_query,
    w_keyval,
    w_out,
    ffn_gain,
    routes,
    route_gates,
    w_gate,
    w_up,
    w_down,
):
    tok_count = lax.axis_size("tok")
    groups = lax.axis_size("head")
    me_tok = lax.axis_index("tok")
    me_head = lax.axis_index("head")
    rows_dev, width = tokens.shape
    row_len = rows_dev * groups
    row_first = me_tok * row_len
    kv_local = w_keyval.shape[1] // (2 * HS)
    q_local = w_query.shape[1] // HS
    origins = plane_origins()

    turns = ring(tokens, "head", 1)

    steps = jnp.arange(groups, dtype=jnp.int32)
    block_of = (me_head - steps) % groups
    token_id = row_first + block_of[:, None] * rows_dev + jnp.arange(rows_dev, dtype=jnp.int32)
    row_segs = lax.dynamic_slice_in_dim(segments, row_first, row_len, 0).reshape(groups, rows_dev)
    segs = jnp.sum(
        jnp.where((block_of[:, None] == steps[None, :])[:, :, None], row_segs[None], 0), axis=1
    )
    requests = jnp.arange(group_ids.shape[0], dtype=jnp.int32)
    starts = jnp.sum((segments[None, :] < requests[:, None]).astype(jnp.int32), axis=1)
    begin = lookup(starts, segs)
    slab = lookup(lookup(prefix_owner, group_ids), segs)
    fill = lookup(slab_fill, slab)
    position = fill + token_id - begin
    steps_idx = jnp.arange(HS // 2, dtype=F32)
    inverse = jnp.exp(steps_idx * (-2.0 * jnp.log(10000.0) / HS))
    angles = position.astype(F32)[:, :, None] * inverse
    cosine = jnp.cos(angles)
    sine = jnp.sin(angles)
    cos = jnp.concatenate([cosine] * 4, axis=2)
    sin = jnp.concatenate([-sine, sine, -sine, sine], axis=2)
    info = jnp.stack([slab, begin, token_id, token_id], axis=2)
    place = token_id[:, 0]
    backs = jnp.arange(groups + 1, dtype=jnp.int32)
    read = jnp.any(slab[:, :, None] == origins, axis=1).astype(jnp.int32)
    spot = jnp.arange(read.shape[1], dtype=jnp.int32)
    rank = jnp.sum(jnp.where(spot[:, None] < spot[None, :], read[:, :, None], 0), axis=1)
    tables = {
        "near_list": (steps[:, None] + backs[None, :]) % groups
        + jnp.where(block_of[:, None] >= backs[None, :], groups, 0),
        "reach": (begin[:, 0] < place - rows_dev).astype(jnp.int32),
        "slab_list": jnp.sum(
            jnp.where(
                (rank[:, :, None] == spot[None, None, :]) & (read[:, :, None] != 0),
                spot[None, :, None],
                0,
            ),
            axis=1,
        ),
        "slab_count": jnp.sum(read, axis=1),
        "fill": lookup(slab_fill, origins),
        "slab_id": origins,
        "place": jnp.concatenate([place - row_len, place]),
    }

    missing = -w_query.shape[1] % LANES
    if missing:
        w_query = jnp.pad(w_query, ((0, 0), (0, missing)))
    queries, own, prev = [], [], []
    for some in (slice(0, groups - 1), slice(groups - 1, groups)):
        query, keyval = project(
            after(turns[some], own[0]) if own else turns[some],
            attn_gain[None, :],
            w_query,
            w_keyval,
            cos[some],
            sin[some],
            kv_local,
            q_local,
        )
        queries += query
        own.append(keyval)
        prev.append(lax.ppermute(keyval, "tok", [(i, i + 1) for i in range(tok_count - 1)]))

    cached = plane_gather(prefix_cache, False, True, [turns[1], None, own[0]])

    def exchanged(block, j):
        return lax.ppermute(block, "head", [(i, (i - j) % groups) for i in range(groups)])

    near = prev + own
    cut = w_out.shape[0] // tok_count if tok_count == 8 else 0
    share = lax.dynamic_slice_in_dim(w_out, me_tok * cut, cut, 0) if cut else w_out
    share = after(share, own[-1])
    w_far = [exchanged(share, s) for s in range(1, groups)]
    middle = groups // 2
    early = attend(1, tables, info, queries[1 : middle + 1], near, cached, q_local)
    late = attend(
        middle + 1, tables, info, queries[middle + 1 :] + queries[:1], near, cached, q_local
    )
    mixed = [exchanged(block, 1 + i) for i, block in enumerate(early)]
    packed = packed_routes(routes, route_gates, 2 * LANES)
    if cut:
        w_far = after(w_far, early[0])
        packed = jnp.pad(packed, ((0, 0), (0, width - packed.shape[1])))
        w_far = plane_gather(
            jnp.concatenate(w_far + [packed], axis=0), True, True, [None, (late[0], mixed), None]
        )
        route_parts = w_far
    else:
        route_parts = plane_gather(packed, False, False)
        w_far = [[(block, 0, block.shape[0])] for block in w_far]
    exp_local = w_gate.shape[0]
    route = route_tables(
        route_parts,
        packed.shape[0],
        2 * LANES,
        (me_tok * exp_local).astype(jnp.int32).reshape(1),
        exp_local,
    )
    mixed += [exchanged(block, middle + 1 + i) for i, block in enumerate(late[:-1])]
    mixed = [late[-1]] + mixed
    hidden, expert_in = project_out(
        mixed, w_out, w_far, cut, origins, tokens, ffn_gain[None, :]
    )
    blocks = plane_gather(expert_in, True, False, [None, route[0], None])
    near, far, last = experts(blocks, *route, w_gate, w_up, w_down)
    return (hidden + plane_sum(near, far, last, rows_dev)).astype(BF16)


def solution(mesh):
    return jax.shard_map(
        local,
        mesh=mesh,
        in_specs=(
            P(("tok", "head"), None),
            P(),
            P(),
            P(),
            P(),
            P("tok", "head"),
            P(),
            P(None, "head"),
            P(None, "head"),
            P("head", None),
            P(),
            P(("tok", "head"), None),
            P(("tok", "head"), None),
            P("tok", None, None),
            P("tok", None, None),
            P("tok", None, None),
        ),
        out_specs=P(("tok", "head"), None),
        check_vma=False,
    )
```

time: 408 us -> 178 us (0.44)
  blocking collectives: 74.9 us -> 0 us
  waiting for transfers between devices: 133 us -> 59.1 us
  Pallas kernels: 0 us -> 59.7 us
  local copies, waits for them, and re-layouts: 69 us -> 9.78 us
  matrix products: 59.2 us -> 0 us
  other arithmetic: 44.5 us -> 14.2 us
  starting transfers between devices: 6.85 us -> 33.8 us
  between operations: 13.5 us -> 0.6 us
  loops' own time: 5.78 us -> 0 us
    all_to_all x1 -> x0, blocking collectives: 74.9 us -> none  [local(): lax.all_to_all(outgoing, 'tok', split_axis=0, concat_axis=0, tiled=True)]
    all_to_all x1 -> x0, waiting for transfers between devices: 71.3 us -> none  [local(): lax.all_to_all(answered, 'tok', split_axis=0, concat_axis=0, tiled=True)]
    pallas_call x0 -> x7, Pallas kernels: none -> 59.7 us  [the longest x1 23.6 us: experts(): pl.pallas_call(functools.partial(expert_kernel, spec, rows), out_shape=tu...]
    dot_general x23 -> x0, matrix products: 59.2 us -> none  [the longest x9 20.2 us: absorb(): jnp.einsum('qgrk,kgd->qgrd', weights.astype(jnp.bfloat16), value_rows, pr...]
    ppermute x1 -> x36, waiting for transfers between devices: 0.01 us -> 59.1 us  [the longest x3 12.1 us: ring(): held.append(lax.ppermute(held[-1], axis, route))]
    all_gather x2 -> x0, waiting for transfers between devices: 44.6 us -> none  [the longest x1 32.2 us: local(): piece = lax.all_gather(normed, 'head', axis=0, tiled=True)]
    ppermute x1 -> x36, starting transfers between devices: 1.64 us -> 33.8 us  [the longest x6 8.24 us: exchanged(): lax.ppermute(block, 'head', [(i, (i - j) % groups) for i in range(groups)])]
    gather x2 -> x0, local copies, waits for them, and re-layouts: 21 us -> none  [the longest x1 10.9 us: local(): per_route = returned[slot_of].reshape(rows_dev, TOPK, expert_in.shape[1])]
  transfers between devices with their start and end apart: 5 -> 36, of which waited for: 4 -> 15; matrix products, arithmetic and copies ran while one was open for 10% -> 10% of each run, Pallas kernels for 0% -> 15%
where the time goes in v1:
time: 178 us; the launch traced here: 177 us
  Pallas kernels  59.7 us (34%)
  waiting for transfers between devices  59.1 us (33%)
  starting transfers between devices  33.8 us (19%)
  other arithmetic  14.2 us (8%)
  local copies, waits for them, and re-layouts  9.78 us (5%)
    pallas_call x1, Pallas kernels, experts(): pl.pallas_call(functools.partial(expert_kernel, spec, rows), out_shape=tu...  23.6 us
    pallas_call x2, Pallas kernels, attend(): pl.pallas_call(functools.partial(attend_kernel, first, blocks, len(near),...  20.7 us
    ppermute x3, waiting for transfers between devices, ring(): held.append(lax.ppermute(held[-1], axis, route))  12.1 us
    ppermute x3, waiting for transfers between devices, plane_gather(): two = lax.ppermute(block, 'tok', second)  11 us
    ppermute x1, waiting for transfers between devices, plane_sum(): beside = lax.ppermute((pair(2) + add_lower).astype(BF16), 'tok', second)  9.48 us
    ppermute x6, starting transfers between devices, exchanged(): lax.ppermute(block, 'head', [(i, (i - j) % groups) for i in range(groups)])  8.24 us
    pallas_call x2, Pallas kernels, project(): pl.pallas_call(functools.partial(project_kernel, blocks, kv_local, q_loca...  7.56 us
    ppermute x2, waiting for transfers between devices, plane_gather(): lax.ppermute(one[:half], 'tok', second)  7.55 us
  transfers between devices with their start and end apart: 36, of which 15 were waited for; matrix products, arithmetic and copies ran while one was open for 10% of the time, Pallas kernels for 15%

profile of v1, /device:TPU:0, one launch (start us, length us, event | category | flops | bytes accessed | tf_op | source)
XLA Modules:
  0.0 177.2 jit_solution(17609513101881415439)
XLA Ops:
  0.0 3.0 %collective-permute-start = (bf16[128,1536]{1,0:T(8,128)(2,1)}, bf16[128,1536]{1,0:T(8,128)(2,1)S(1)}, u32[]{:S(2)}, u32[]{:S(2)}) collective-permute-start(bf16[128,1536]{1,0:T(8,128)(2,1)} %refs_9_.1), channel_id=1, source_target_pairs={{0,1},{1,2},{2,3},{3,0},{4,5},{5,6},{6,7},{7,4},{8,9},{9,10},{10,1... | collective-permute-start | bytes 1179656 | tf_op jit(solution)/shard_map/ppermute | solution.py:43
  3.8 0.9 convert_reduce_fusion
  4.7 0.8 dynamic-slice_bitcast_fusion
  5.5 0.8 select_reduce_fusion.7
  6.8 0.7 select_reduce_fusion.2
  9.0 0.7 reduce-precision_convert_fusion.1
  9.7 1.0 fusion.4
  11.2 3.1 %collective-permute-done.refs_1_ = bf16[128,1536]{1,0:T(8,128)(2,1)S(1)} collective-permute-done((bf16[128,1536]{1,0:T(8,128)(2,1)}, bf16[128,1536]{1,0:T(8,128)(2,1)S(1)}, u32[]{:S(2)}, u32[]{:S(2)}) %collective-permute-start) | collective-permute-done | bytes 393248 | tf_op jit(solution)/shard_map/ppermute | solution.py:43
  14.4 2.4 %collective-permute-start.7 = (bf16[512,256]{1,0:T(8,128)(2,1)S(1)}, bf16[512,256]{1,0:T(8,128)(2,1)S(1)}, u32[]{:S(2)}, u32[]{:S(2)}) collective-permute-start(bf16[512,256]{1,0:T(8,128)(2,1)S(1)} %copy-done.3), channel_id=1, source_target_pairs={{0,24},{4,28},{8,16},{12,20},{16,8},{20,12},{24,0},{28,4},{1,25},{... | collective-permute-start | bytes 786440 | tf_op jit(solution)/shard_map/ppermute | solution.py:89
  20.6 0.8 maximum_bitcast_fusion
  21.5 3.1 %collective-permute-done.7 = bf16[512,256]{1,0:T(8,128)(2,1)S(1)} collective-permute-done((bf16[512,256]{1,0:T(8,128)(2,1)S(1)}, bf16[512,256]{1,0:T(8,128)(2,1)S(1)}, u32[]{:S(2)}, u32[]{:S(2)}) %collective-permute-start.7) | collective-permute-done | bytes 262176 | tf_op jit(solution)/shard_map/ppermute | solution.py:89
  24.6 3.7 %collective-permute-done.6 = bf16[512,256]{1,0:T(8,128)(2,1)S(1)} collective-permute-done((bf16[512,256]{1,0:T(8,128)(2,1)S(1)}, bf16[512,256]{1,0:T(8,128)(2,1)S(1)}, u32[]{:S(2)}, u32[]{:S(2)}) %collective-permute-start.6) | collective-permute-done | bytes 262176 | tf_op jit(solution)/shard_map/ppermute | solution.py:81
  28.5 0.8 collective-permute-done.1.refs_2_
  29.2 0.7 copy-done.16
  30.0 4.4 %norm_project_rotate.2 = (bf16[2,384,128]{2,1,0:T(8,128)(2,1)}, bf16[2,384,128]{2,1,0:T(8,128)(2,1)}, bf16[2,384,128]{2,1,0:T(8,128)(2,1)}, bf16[384,256]{1,0:T(8,128)(2,1)}) custom-call(bf16[128,1536]{1,0:T(8,128)(2,1)} %refs_9_.1, bf16[128,1536]{1,0:T(8,128)(2,1)} %copy-done.15, bf16[128,1536]{1,0:T(8,128)(2,1)} %copy-done.16, ...), custom_call_target="tpu_custom_call" | custom-call | flops 4000000000 | bytes 4000000 | tf_op jit(solution)/shard_map/norm_project_rotate/pallas_call | solution.py:215
  34.5 0.8 select_reduce_fusion.6.fill
  36.2 1.0 pad_add_fusion.info
  37.2 0.9 constant_dynamic-slice_fusion
  38.2 2.4 %collective-permute-start.3 = (bf16[384,256]{1,0:T(8,128)(2,1)S(1)}, bf16[384,256]{1,0:T(8,128)(2,1)S(1)}, u32[]{:S(2)}, u32[]{:S(2)}) collective-permute-start(bf16[384,256]{1,0:T(8,128)(2,1)S(1)} %copy-done.21), channel_id=1, source_target_pairs={{0,4},{4,8},{8,12},{12,16},{16,20},{20,24},{24,28},{1,5},{5,9},{9,... | collective-permute-start | bytes 589832 | tf_op jit(solution)/shard_map/ppermute | solution.py:838
  40.6 8.2 %collective-permute-done.2.refs_0_ = bf16[128,1536]{1,0:T(8,128)(2,1)S(1)} collective-permute-done((bf16[128,1536]{1,0:T(8,128)(2,1)}, bf16[128,1536]{1,0:T(8,128)(2,1)S(1)}, u32[]{:S(2)}, u32[]{:S(2)}) %collective-permute-start.2) | collective-permute-done | bytes 393248 | tf_op jit(solution)/shard_map/ppermute | solution.py:43
  48.8 0.7 copy-done.20
  49.5 3.1 %norm_project_rotate.3 = (bf16[2,384,128]{2,1,0:T(8,128)(2,1)}, bf16[128,256]{1,0:T(8,128)(2,1)}) custom-call(bf16[128,1536]{1,0:T(8,128)(2,1)} %copy-done.20, f32[1,1536]{1,0:T(1,128)} %broadcast_in_dim.146.refs_3_.refs_1_, bf16[1536,384]{1,0:T(8,128)(2,1)} %refs_2_.1, bf16[1536,256]{1,0:T(8,128)(2,1)} %refs_3_.1, f32[128,128]{1,0:T(8,128)} %get-tuple-element.88.refs_4_, ...), custom_call_target="tpu_custom_call" | custom-call | flops 4000000000 | bytes 4000000 | tf_op jit(solution)/shard_map/norm_project_rotate/pallas_call | solution.py:215
  52.7 1.6 collective-permute-start.4
  55.1 3.7 %collective-permute-start.12 = (bf16[48,1536]{1,0:T(8,128)(2,1)S(1)}, bf16[48,1536]{1,0:T(8,128)(2,1)S(1)}, u32[]{:S(2)}, u32[]{:S(2)}) collective-permute-start(bf16[48,1536]{1,0:T(8,128)(2,1)S(1)} %constant_dynamic-slice_fusion), channel_id=1, source_target_pairs={{0,3},{1,0},{2,1},{3,2},{4,7},{5,4},{6,5},{7,6},{8,11},{9,8},{10,9... | collective-permute-start | bytes 442376 | tf_op jit(solution)/shard_map/ppermute | solution.py:843
  59.8 11.1 %attend.3 = (bf16[128,384]{1,0:T(8,128)(2,1)}, bf16[128,384]{1,0:T(8,128)(2,1)}) custom-call(s32[4,5]{1,0:T(4,128)} %fusion.12.near_list, s32[4]{0:T(128)} %compare_convert_fusion.reach, s32[4,8]{1,0:T(4,128)} %select_reduce_fusion.3.slab_list, s32[4]{0:T(128)} %convert_reduce_fusion.1.slab_count, s32[8]{0:T(128)} %select_reduce_fusion.6.fill, s32[8]{0:T(128)} %copy-done.10, ...), custom_call_target="tpu_custom_call" | custom-call | flops 12000000000 | bytes 4000000 | tf_op jit(solution)/shard_map/attend/pallas_call | solution.py:403
  71.7 0.8 collective-permute-start.16
  72.5 2.3 %collective-permute-start.15 = (bf16[160,1536]{1,0:T(8,128)(2,1)S(1)}, bf16[160,1536]{1,0:T(8,128)(2,1)S(1)}, u32[]{:S(2)}, u32[]{:S(2)}) collective-permute-start(bf16[160,1536]{1,0:T(8,128)(2,1)S(1)} %pad_maximum_fusion.1), channel_id=1, source_target_pairs={{0,16},{4,12},{8,24},{12,4},{16,0},{20,28},{24,8},{28,20},{1,17},{... | collective-permute-start | bytes 1474568 | tf_op jit(solution)/shard_map/ppermute | solution.py:80
  75.4 9.5 %attend.2 = (bf16[128,384]{1,0:T(8,128)(2,1)}, bf16[128,384]{1,0:T(8,128)(2,1)}) custom-call(s32[4,5]{1,0:T(4,128)} %fusion.12.near_list, s32[4]{0:T(128)} %compare_convert_fusion.reach, s32[4,8]{1,0:T(4,128)} %select_reduce_fusion.3.slab_list, s32[4]{0:T(128)} %convert_reduce_fusion.1.slab_count, s32[8]{0:T(128)} %select_reduce_fusion.6.fill, s32[8]{0:T(128)} %copy-done.10, ...), custom_call_target="tpu_custom_call" | custom-call | flops 12000000000 | bytes 4000000 | tf_op jit(solution)/shard_map/attend/pallas_call | solution.py:403
  86.7 7.5 %collective-permute-done.17 = bf16[80,1536]{1,0:T(8,128)(2,1)S(1)} collective-permute-done((bf16[80,1536]{1,0:T(8,128)(2,1)S(1)}, bf16[80,1536]{1,0:T(8,128)(2,1)S(1)}, u32[]{:S(2)}, u32[]{:S(2)}) %collective-permute-start.17) | collective-permute-done | bytes 245792 | tf_op jit(solution)/shard_map/ppermute | solution.py:85
  94.5 3.3 %collective-permute-start.11 = (bf16[128,384]{1,0:T(8,128)(2,1)S(1)}, bf16[128,384]{1,0:T(8,128)(2,1)S(1)}, u32[]{:S(2)}, u32[]{:S(2)}) collective-permute-start(bf16[128,384]{1,0:T(8,128)(2,1)S(1)} %copy-done.29), channel_id=1, source_target_pairs={{0,1},{1,2},{2,3},{3,0},{4,5},{5,6},{6,7},{7,4},{8,9},{9,10},{10,1... | collective-permute-start | bytes 294920 | tf_op jit(solution)/shard_map/ppermute | solution.py:843
  98.3 3.1 %collective-permute-done.11.refs_3_ = bf16[128,384]{1,0:T(8,128)(2,1)S(1)} collective-permute-done((bf16[128,384]{1,0:T(8,128)(2,1)S(1)}, bf16[128,384]{1,0:T(8,128)(2,1)S(1)}, u32[]{:S(2)}, u32[]{:S(2)}) %collective-permute-start.11) | collective-permute-done | bytes 98336 | tf_op jit(solution)/shard_map/ppermute | solution.py:843
  102.8 5.9 %project_out_norm.1 = (f32[128,1536]{1,0:T(8,128)}, bf16[128,1536]{1,0:T(8,128)(2,1)}) custom-call(s32[8]{0:T(128)} %copy-done.10, bf16[128,384]{1,0:T(8,128)(2,1)} %get-tuple-element.43.refs_0_, bf16[128,384]{1,0:T(8,128)(2,1)} %copy-done.27, bf16[128,384]{1,0:T(8,128)(2,1)} %copy-done.28, bf16[128,384]{1,0:T(8,128)(2,1)} %copy-done.31, ...), custom_call_target="tpu_custom_call" | custom-call | flops 5000000000 | bytes 6291456 | tf_op jit(solution)/shard_map/project_out_norm/pallas_call | solution.py:487
  109.2 0.8 collective-permute-start.21
  110.1 2.0 %route_tables.1 = (s32[4,1024]{1,0:T(4,128)}, f32[4,1024]{1,0:T(4,128)}, s32[1024,8]{1,0:T(8,128)}) custom-call(s32[1]{0:T(128)} %bitcast.17.first_expert, bf16[480,1536]{1,0:T(8,128)(2,1)} %copy-done.7, bf16[160,1536]{1,0:T(8,128)(2,1)} %copy-done.4, bf16[480,1536]{1,0:T(8,128)(2,1)} %copy-done.12, bf16[160,1536]{1,0:T(8,128)(2,1)} %copy-done.14), custom_call_target="tpu_custom_call" | custom-call | flops 3000000000 | bytes 1000000 | tf_op jit(solution)/shard_map/route_tables/pallas_call | solution.py:725
  112.1 7.3 %collective-permute-done.22.refs_2_ = bf16[128,1536]{1,0:T(8,128)(2,1)S(1)} collective-permute-done((bf16[128,1536]{1,0:T(8,128)(2,1)}, bf16[128,1536]{1,0:T(8,128)(2,1)S(1)}, u32[]{:S(2)}, u32[]{:S(2)}) %collective-permute-start.22) | collective-permute-done | bytes 393248 | tf_op jit(solution)/shard_map/ppermute | solution.py:81
  119.5 1.6 collective-permute-start.24
  122.4 4.6 %collective-permute-done.24.refs_4_ = bf16[64,1536]{1,0:T(8,128)(2,1)S(1)} collective-permute-done((bf16[64,1536]{1,0:T(8,128)(2,1)S(1)}, bf16[64,1536]{1,0:T(8,128)(2,1)S(1)}, u32[]{:S(2)}, u32[]{:S(2)}) %collective-permute-start.24) | collective-permute-done | bytes 196640 | tf_op jit(solution)/shard_map/ppermute | solution.py:86
  127.5 0.9 collective-permute-done.29.refs_9_
  129.6 23.6 %experts.1 = (bf16[512,1536]{1,0:T(8,128)(2,1)}, bf16[384,1536]{1,0:T(8,128)(2,1)}, bf16[128,1536]{1,0:T(8,128)(2,1)}) custom-call(s32[4,1024]{1,0:T(4,128)} %get-tuple-element.56.slot_row, f32[4,1024]{1,0:T(4,128)} %get-tuple-element.57.gate_row, s32[1024,8]{1,0:T(8,128)} %get-tuple-element.58.slot_col, bf16[128,1536]{1,0:T(8,128)(2,1)} %get-tuple-element.59.refs_0_, ...), custom_call_target="tpu_custom_call" | custom-call | flops 12884901888 | bytes 25165824 | tf_op jit(solution)/shard_map/experts/pallas_call | solution.py:633
  153.8 1.4 collective-permute-done.31
  155.2 1.1 add_convert_fusion.3
  156.4 1.3 collective-permute-start.33
  157.6 1.1 collective-permute-start.32
  158.7 5.3 %collective-permute-done.33 = bf16[64,1536]{1,0:T(8,128)(2,1)S(1)} collective-permute-done((bf16[64,1536]{1,0:T(8,128)(2,1)S(1)}, bf16[64,1536]{1,0:T(8,128)(2,1)S(1)}, u32[]{:S(2)}, u32[]{:S(2)}) %collective-permute-start.33) | collective-permute-done | bytes 196640 | tf_op jit(solution)/shard_map/ppermute | solution.py:147
  164.3 1.3 collective-permute-start.34
  165.5 1.2 collective-permute-start.35
  166.7 9.5 %collective-permute-done.34 = bf16[128,1536]{1,0:T(8,128)(2,1)S(1)} collective-permute-done((bf16[128,1536]{1,0:T(8,128)(2,1)S(1)}, bf16[128,1536]{1,0:T(8,128)(2,1)S(1)}, u32[]{:S(2)}, u32[]{:S(2)}) %collective-permute-start.34) | collective-permute-done | bytes 393248 | tf_op jit(solution)/shard_map/ppermute | solution.py:158
  176.2 1.0 add_convert_fusion
  (153 shorter events, 19.5 us)
Async XLA Ops:
  0.0 14.4 %copy-start.3 = (bf16[512,256]{1,0:T(8,128)(2,1)S(1)}, bf16[512,256]{1,0:T(8,128)(2,1)}, u32[]{:S(2)}) copy-start(bf16[512,256]{1,0:T(8,128)(2,1)} %param.21) | copy-start | bytes 786436
  0.0 18.7 %copy-start.8 = (f32[1536]{0:T(1024)S(1)}, f32[1536]{0:T(1024)}, u32[]{:S(2)}) copy-start(f32[1536]{0:T(1024)} %param.22) | copy-start | bytes 18436
  0.0 14.4 %collective-permute-start = (bf16[128,1536]{1,0:T(8,128)(2,1)}, bf16[128,1536]{1,0:T(8,128)(2,1)S(1)}, u32[]{:S(2)}, u32[]{:S(2)}) collective-permute-start(bf16[128,1536]{1,0:T(8,128)(2,1)} %refs_9_.1), channel_id=1, source_target_pairs={{0,1},{1,2},{2,3},{3,0},{4,5},{5,6},{6,7},{7,4},{8,9},{9,10},{10,1... | collective-permute-start | bytes 1179656 | tf_op jit(solution)/shard_map/ppermute | solution.py:43
  6.5 28.0 %copy-start.10 = (s32[8]{0:T(128)}, s32[8]{0:T(128)S(1)}, u32[]{:S(2)}) copy-start(s32[8]{0:T(128)S(1)} %stack.44.slab_id.origins) | copy-start | bytes 100
  14.4 14.1 %copy-start.15 = (bf16[128,1536]{1,0:T(8,128)(2,1)}, bf16[128,1536]{1,0:T(8,128)(2,1)S(1)}, u32[]{:S(2)}) copy-start(bf16[128,1536]{1,0:T(8,128)(2,1)S(1)} %collective-permute-done.refs_1_) | copy-start | bytes 1179652
  14.4 10.2 %collective-permute-start.7 = (bf16[512,256]{1,0:T(8,128)(2,1)S(1)}, bf16[512,256]{1,0:T(8,128)(2,1)S(1)}, u32[]{:S(2)}, u32[]{:S(2)}) collective-permute-start(bf16[512,256]{1,0:T(8,128)(2,1)S(1)} %copy-done.3), channel_id=1, source_target_pairs={{0,24},{4,28},{8,16},{12,20},{16,8},{20,12},{24,0},{28,4},{1,25},{... | collective-permute-start | bytes 786440 | tf_op jit(solution)/shard_map/ppermute | solution.py:89
  16.8 11.4 %collective-permute-start.6 = (bf16[512,256]{1,0:T(8,128)(2,1)S(1)}, bf16[512,256]{1,0:T(8,128)(2,1)S(1)}, u32[]{:S(2)}, u32[]{:S(2)}) collective-permute-start(bf16[512,256]{1,0:T(8,128)(2,1)S(1)} %copy-done.3), channel_id=1, source_target_pairs={{0,8},{4,20},{8,0},{12,28},{16,24},{20,4},{24,16},{28,12},{1,9},{5... | collective-permute-start | bytes 786440 | tf_op jit(solution)/shard_map/ppermute | solution.py:81
  17.4 11.0 %collective-permute-start.5 = (bf16[512,256]{1,0:T(8,128)(2,1)S(1)}, bf16[512,256]{1,0:T(8,128)(2,1)S(1)}, u32[]{:S(2)}, u32[]{:S(2)}) collective-permute-start(bf16[512,256]{1,0:T(8,128)(2,1)S(1)} %copy-done.3), channel_id=1, source_target_pairs={{0,16},{4,12},{8,24},{12,4},{16,0},{20,28},{24,8},{28,20},{1,17},{... | collective-permute-start | bytes 786440 | tf_op jit(solution)/shard_map/ppermute | solution.py:80
  18.0 11.3 %collective-permute-start.1 = (bf16[128,1536]{1,0:T(8,128)(2,1)S(1)}, bf16[128,1536]{1,0:T(8,128)(2,1)S(1)}, u32[]{:S(2)}, u32[]{:S(2)}) collective-permute-start(bf16[128,1536]{1,0:T(8,128)(2,1)S(1)} %collective-permute-done.refs_1_), channel_id=1, source_target_pairs={{0,1},{1,2},{2,3},{3,0},{4,5},{5,6},{6,7},{7,4},{8,9},{9,10},{10,1... | collective-permute-start | bytes 1179656 | tf_op jit(solution)/shard_map/ppermute | solution.py:43
  34.4 24.4 %collective-permute-start.8 = (bf16[2048,256]{1,0:T(8,128)(2,1)S(1)}, bf16[2048,256]{1,0:T(8,128)(2,1)S(1)}, u32[]{:S(2)}, u32[]{:S(2)}) collective-permute-start(bf16[2048,256]{1,0:T(8,128)(2,1)S(1)} %pad_maximum_fusion.refs_6_), channel_id=1, source_target_pairs={{0,4},{4,0},{8,12},{12,8},{16,20},{20,16},{24,28},{28,24},{1,5},{5... | collective-permute-start | bytes 3145736 | tf_op jit(solution)/shard_map/ppermute | solution.py:76
  35.3 13.5 %collective-permute-start.2 = (bf16[128,1536]{1,0:T(8,128)(2,1)}, bf16[128,1536]{1,0:T(8,128)(2,1)S(1)}, u32[]{:S(2)}, u32[]{:S(2)}) collective-permute-start(bf16[128,1536]{1,0:T(8,128)(2,1)} %copy-done.16), channel_id=1, source_target_pairs={{0,1},{1,2},{2,3},{3,0},{4,5},{5,6},{6,7},{7,4},{8,9},{9,10},{10,1... | collective-permute-start | bytes 1179656 | tf_op jit(solution)/shard_map/ppermute | solution.py:43
  38.2 17.0 %collective-permute-start.3 = (bf16[384,256]{1,0:T(8,128)(2,1)S(1)}, bf16[384,256]{1,0:T(8,128)(2,1)S(1)}, u32[]{:S(2)}, u32[]{:S(2)}) collective-permute-start(bf16[384,256]{1,0:T(8,128)(2,1)S(1)} %copy-done.21), channel_id=1, source_target_pairs={{0,4},{4,8},{8,12},{12,16},{16,20},{20,24},{24,28},{1,5},{5,9},{9,... | collective-permute-start | bytes 589832 | tf_op jit(solution)/shard_map/ppermute | solution.py:838
  52.7 6.1 %collective-permute-start.4 = (bf16[128,256]{1,0:T(8,128)(2,1)}, bf16[128,256]{1,0:T(8,128)(2,1)S(1)}, u32[]{:S(2)}, u32[]{:S(2)}) collective-permute-start(bf16[128,256]{1,0:T(8,128)(2,1)} %get-tuple-element.40.refs_5_), channel_id=1, source_target_pairs={{0,4},{4,8},{8,12},{12,16},{16,20},{20,24},{24,28},{1,5},{5,9},{9,... | collective-permute-start | bytes 196616 | tf_op jit(solution)/shard_map/ppermute | solution.py:838
  54.9 16.6 %collective-permute-start.14 = (bf16[48,1536]{1,0:T(8,128)(2,1)S(1)}, bf16[48,1536]{1,0:T(8,128)(2,1)S(1)}, u32[]{:S(2)}, u32[]{:S(2)}) collective-permute-start(bf16[48,1536]{1,0:T(8,128)(2,1)S(1)} %constant_dynamic-slice_fusion), channel_id=1, source_target_pairs={{0,1},{1,2},{2,3},{3,0},{4,5},{5,6},{6,7},{7,4},{8,9},{9,10},{10,1... | collective-permute-start | bytes 442376 | tf_op jit(solution)/shard_map/ppermute | solution.py:843
  54.9 16.6 %collective-permute-start.13 = (bf16[48,1536]{1,0:T(8,128)(2,1)S(1)}, bf16[48,1536]{1,0:T(8,128)(2,1)S(1)}, u32[]{:S(2)}, u32[]{:S(2)}) collective-permute-start(bf16[48,1536]{1,0:T(8,128)(2,1)S(1)} %constant_dynamic-slice_fusion), channel_id=1, source_target_pairs={{0,2},{1,3},{2,0},{3,1},{4,6},{5,7},{6,4},{7,5},{8,10},{9,11},{10,... | collective-permute-start | bytes 442376 | tf_op jit(solution)/shard_map/ppermute | solution.py:843
  55.1 16.4 %collective-permute-start.12 = (bf16[48,1536]{1,0:T(8,128)(2,1)S(1)}, bf16[48,1536]{1,0:T(8,128)(2,1)S(1)}, u32[]{:S(2)}, u32[]{:S(2)}) collective-permute-start(bf16[48,1536]{1,0:T(8,128)(2,1)S(1)} %constant_dynamic-slice_fusion), channel_id=1, source_target_pairs={{0,3},{1,0},{2,1},{3,2},{4,7},{5,4},{6,5},{7,6},{8,11},{9,8},{10,9... | collective-permute-start | bytes 442376 | tf_op jit(solution)/shard_map/ppermute | solution.py:843
  71.0 14.0 %collective-permute-start.9 = (bf16[128,384]{1,0:T(8,128)(2,1)}, bf16[128,384]{1,0:T(8,128)(2,1)S(1)}, u32[]{:S(2)}, u32[]{:S(2)}) collective-permute-start(bf16[128,384]{1,0:T(8,128)(2,1)} %get-tuple-element.46), channel_id=1, source_target_pairs={{0,3},{1,0},{2,1},{3,2},{4,7},{5,4},{6,5},{7,6},{8,11},{9,8},{10,9... | collective-permute-start | bytes 294920 | tf_op jit(solution)/shard_map/ppermute | solution.py:843
  71.7 13.3 %collective-permute-start.16 = (bf16[160,1536]{1,0:T(8,128)(2,1)S(1)}, bf16[160,1536]{1,0:T(8,128)(2,1)S(1)}, u32[]{:S(2)}, u32[]{:S(2)}) collective-permute-start(bf16[160,1536]{1,0:T(8,128)(2,1)S(1)} %pad_maximum_fusion.1), channel_id=1, source_target_pairs={{0,8},{4,20},{8,0},{12,28},{16,24},{20,4},{24,16},{28,12},{1,9},{5... | collective-permute-start | bytes 1474568 | tf_op jit(solution)/shard_map/ppermute | solution.py:81
  72.5 12.5 %collective-permute-start.15 = (bf16[160,1536]{1,0:T(8,128)(2,1)S(1)}, bf16[160,1536]{1,0:T(8,128)(2,1)S(1)}, u32[]{:S(2)}, u32[]{:S(2)}) collective-permute-start(bf16[160,1536]{1,0:T(8,128)(2,1)S(1)} %pad_maximum_fusion.1), channel_id=1, source_target_pairs={{0,16},{4,12},{8,24},{12,4},{16,0},{20,28},{24,8},{28,20},{1,17},{... | collective-permute-start | bytes 1474568 | tf_op jit(solution)/shard_map/ppermute | solution.py:80
  74.8 10.1 %collective-permute-start.10 = (bf16[128,384]{1,0:T(8,128)(2,1)S(1)}, bf16[128,384]{1,0:T(8,128)(2,1)S(1)}, u32[]{:S(2)}, u32[]{:S(2)}) collective-permute-start(bf16[128,384]{1,0:T(8,128)(2,1)S(1)} %copy-done.30), channel_id=1, source_target_pairs={{0,2},{1,3},{2,0},{3,1},{4,6},{5,7},{6,4},{7,5},{8,10},{9,11},{10,... | collective-permute-start | bytes 294920 | tf_op jit(solution)/shard_map/ppermute | solution.py:843
  85.0 9.4 %copy-start.29 = (bf16[128,384]{1,0:T(8,128)(2,1)S(1)}, bf16[128,384]{1,0:T(8,128)(2,1)}, u32[]{:S(2)}) copy-start(bf16[128,384]{1,0:T(8,128)(2,1)} %get-tuple-element.48) | copy-start | bytes 294916
  85.0 12.7 %copy-start.9 = (f32[1536]{0:T(1024)S(1)}, f32[1536]{0:T(1024)}, u32[]{:S(2)}) copy-start(f32[1536]{0:T(1024)} %param.26) | copy-start | bytes 18436
  85.1 16.4 %copy-start.7 = (bf16[480,1536]{1,0:T(8,128)(2,1)}, bf16[480,1536]{1,0:T(8,128)(2,1)S(1)}, u32[]{:S(2)}) copy-start(bf16[480,1536]{1,0:T(8,128)(2,1)S(1)} %constant_dynamic-update-slice_fusion.refs_5_.refs_0_) | copy-start | bytes 4423684
  85.1 16.4 %collective-permute-start.19 = (bf16[480,1536]{1,0:T(8,128)(2,1)S(1)}, bf16[480,1536]{1,0:T(8,128)(2,1)S(1)}, u32[]{:S(2)}, u32[]{:S(2)}) collective-permute-start(bf16[480,1536]{1,0:T(8,128)(2,1)S(1)} %constant_dynamic-update-slice_fusion.refs_5_.refs_0_), channel_id=1, source_target_pairs={{0,4},{4,0},{8,12},{12,8},{16,20},{20,16},{24,28},{28,24},{1,5},{5... | collective-permute-start | bytes 4423688 | tf_op jit(solution)/shard_map/ppermute | solution.py:76
  85.8 8.5 %collective-permute-start.17 = (bf16[80,1536]{1,0:T(8,128)(2,1)S(1)}, bf16[80,1536]{1,0:T(8,128)(2,1)S(1)}, u32[]{:S(2)}, u32[]{:S(2)}) collective-permute-start(bf16[80,1536]{1,0:T(8,128)(2,1)S(1)} %slice.63), channel_id=1, source_target_pairs={{0,8},{4,20},{8,0},{12,28},{16,24},{20,4},{24,16},{28,12},{1,9},{5... | collective-permute-start | bytes 737288 | tf_op jit(solution)/shard_map/ppermute | solution.py:85
  86.2 8.1 %collective-permute-start.18 = (bf16[80,1536]{1,0:T(8,128)(2,1)S(1)}, bf16[80,1536]{1,0:T(8,128)(2,1)S(1)}, u32[]{:S(2)}, u32[]{:S(2)}) collective-permute-start(bf16[80,1536]{1,0:T(8,128)(2,1)S(1)} %slice.64), channel_id=1, source_target_pairs={{0,16},{4,12},{8,24},{12,4},{16,0},{20,28},{24,8},{28,20},{1,17},{... | collective-permute-start | bytes 737288 | tf_op jit(solution)/shard_map/ppermute | solution.py:86
  94.4 7.1 %copy-start.4 = (bf16[160,1536]{1,0:T(8,128)(2,1)}, bf16[160,1536]{1,0:T(8,128)(2,1)S(1)}, u32[]{:S(2)}) copy-start(bf16[160,1536]{1,0:T(8,128)(2,1)S(1)} %constant_dynamic-update-slice_fusion.6.refs_6_.refs_1_) | copy-start | bytes 1474564
  94.4 7.1 %collective-permute-start.20 = (bf16[160,1536]{1,0:T(8,128)(2,1)S(1)}, bf16[160,1536]{1,0:T(8,128)(2,1)S(1)}, u32[]{:S(2)}, u32[]{:S(2)}) collective-permute-start(bf16[160,1536]{1,0:T(8,128)(2,1)S(1)} %constant_dynamic-update-slice_fusion.6.refs_6_.refs_1_), channel_id=1, source_target_pairs={{0,4},{4,0},{8,12},{12,8},{16,20},{20,16},{24,28},{28,24},{1,5},{5... | collective-permute-start | bytes 1474568 | tf_op jit(solution)/shard_map/ppermute | solution.py:76
  94.5 7.0 %collective-permute-start.11 = (bf16[128,384]{1,0:T(8,128)(2,1)S(1)}, bf16[128,384]{1,0:T(8,128)(2,1)S(1)}, u32[]{:S(2)}, u32[]{:S(2)}) collective-permute-start(bf16[128,384]{1,0:T(8,128)(2,1)S(1)} %copy-done.29), channel_id=1, source_target_pairs={{0,1},{1,2},{2,3},{3,0},{4,5},{5,6},{6,7},{7,4},{8,9},{9,10},{10,1... | collective-permute-start | bytes 294920 | tf_op jit(solution)/shard_map/ppermute | solution.py:843
  108.7 10.8 %collective-permute-start.22 = (bf16[128,1536]{1,0:T(8,128)(2,1)}, bf16[128,1536]{1,0:T(8,128)(2,1)S(1)}, u32[]{:S(2)}, u32[]{:S(2)}) collective-permute-start(bf16[128,1536]{1,0:T(8,128)(2,1)} %get-tuple-element.59.refs_0_), channel_id=1, source_target_pairs={{0,8},{4,20},{8,0},{12,28},{16,24},{20,4},{24,16},{28,12},{1,9},{5... | collective-permute-start | bytes 1179656 | tf_op jit(solution)/shard_map/ppermute | solution.py:81
  109.2 10.2 %collective-permute-start.21 = (bf16[128,1536]{1,0:T(8,128)(2,1)}, bf16[128,1536]{1,0:T(8,128)(2,1)S(1)}, u32[]{:S(2)}, u32[]{:S(2)}) collective-permute-start(bf16[128,1536]{1,0:T(8,128)(2,1)} %get-tuple-element.59.refs_0_), channel_id=1, source_target_pairs={{0,16},{4,12},{8,24},{12,4},{16,0},{20,28},{24,8},{28,20},{1,17},{... | collective-permute-start | bytes 1179656 | tf_op jit(solution)/shard_map/ppermute | solution.py:80
  110.1 17.4 %collective-permute-start.25 = (bf16[128,1536]{1,0:T(8,128)(2,1)}, bf16[128,1536]{1,0:T(8,128)(2,1)S(1)}, u32[]{:S(2)}, u32[]{:S(2)}) collective-permute-start(bf16[128,1536]{1,0:T(8,128)(2,1)} %get-tuple-element.59.refs_0_), channel_id=1, source_target_pairs={{0,4},{4,0},{8,12},{12,8},{16,20},{20,16},{24,28},{28,24},{1,5},{5... | collective-permute-start | bytes 1179656 | tf_op jit(solution)/shard_map/ppermute | solution.py:76
  119.5 9.2 %copy-start.5 = (bf16[128,1536]{1,0:T(8,128)(2,1)}, bf16[128,1536]{1,0:T(8,128)(2,1)S(1)}, u32[]{:S(2)}) copy-start(bf16[128,1536]{1,0:T(8,128)(2,1)S(1)} %collective-permute-done.22.refs_2_) | copy-start | bytes 1179652
  119.5 9.2 %copy-start.6 = (bf16[128,1536]{1,0:T(8,128)(2,1)}, bf16[128,1536]{1,0:T(8,128)(2,1)S(1)}, u32[]{:S(2)}) copy-start(bf16[128,1536]{1,0:T(8,128)(2,1)S(1)} %collective-permute-done.21.refs_1_) | copy-start | bytes 1179652
  119.5 7.5 %collective-permute-start.24 = (bf16[64,1536]{1,0:T(8,128)(2,1)S(1)}, bf16[64,1536]{1,0:T(8,128)(2,1)S(1)}, u32[]{:S(2)}, u32[]{:S(2)}) collective-permute-start(bf16[64,1536]{1,0:T(8,128)(2,1)S(1)} %slice.66), channel_id=1, source_target_pairs={{0,16},{4,12},{8,24},{12,4},{16,0},{20,28},{24,8},{28,20},{1,17},{... | collective-permute-start | bytes 589832 | tf_op jit(solution)/shard_map/ppermute | solution.py:86
  121.2 5.8 %collective-permute-start.23 = (bf16[64,1536]{1,0:T(8,128)(2,1)S(1)}, bf16[64,1536]{1,0:T(8,128)(2,1)S(1)}, u32[]{:S(2)}, u32[]{:S(2)}) collective-permute-start(bf16[64,1536]{1,0:T(8,128)(2,1)S(1)} %slice.65), channel_id=1, source_target_pairs={{0,8},{4,20},{8,0},{12,28},{16,24},{20,4},{24,16},{28,12},{1,9},{5... | collective-permute-start | bytes 589832 | tf_op jit(solution)/shard_map/ppermute | solution.py:85
  121.8 6.8 %collective-permute-start.26 = (bf16[128,1536]{1,0:T(8,128)(2,1)S(1)}, bf16[128,1536]{1,0:T(8,128)(2,1)S(1)}, u32[]{:S(2)}, u32[]{:S(2)}) collective-permute-start(bf16[128,1536]{1,0:T(8,128)(2,1)S(1)} %collective-permute-done.21.refs_1_), channel_id=1, source_target_pairs={{0,4},{4,0},{8,12},{12,8},{16,20},{20,16},{24,28},{28,24},{1,5},{5... | collective-permute-start | bytes 1179656 | tf_op jit(solution)/shard_map/ppermute | solution.py:76
  121.8 6.8 %collective-permute-start.27 = (bf16[128,1536]{1,0:T(8,128)(2,1)S(1)}, bf16[128,1536]{1,0:T(8,128)(2,1)S(1)}, u32[]{:S(2)}, u32[]{:S(2)}) collective-permute-start(bf16[128,1536]{1,0:T(8,128)(2,1)S(1)} %collective-permute-done.22.refs_2_), channel_id=1, source_target_pairs={{0,4},{4,0},{8,12},{12,8},{16,20},{20,16},{24,28},{28,24},{1,5},{5... | collective-permute-start | bytes 1179656 | tf_op jit(solution)/shard_map/ppermute | solution.py:76
  127.0 1.4 collective-permute-start.29
  127.0 1.7 collective-permute-start.28
  153.2 10.8 %copy-start = (bf16[512,1536]{1,0:T(8,128)(2,1)S(1)}, bf16[512,1536]{1,0:T(8,128)(2,1)}, u32[]{:S(2)}) copy-start(bf16[512,1536]{1,0:T(8,128)(2,1)} %get-tuple-element.65) | copy-start | bytes 4718596
  153.2 2.0 %collective-permute-start.31 = (bf16[128,1536]{1,0:T(8,128)(2,1)}, bf16[128,1536]{1,0:T(8,128)(2,1)S(1)}, u32[]{:S(2)}, u32[]{:S(2)}) collective-permute-start(bf16[128,1536]{1,0:T(8,128)(2,1)} %get-tuple-element.64), channel_id=1, source_target_pairs={{0,4},{4,0},{8,12},{12,8},{16,20},{20,16},{24,28},{28,24},{1,5},{5... | collective-permute-start | bytes 1179656 | tf_op jit(solution)/shard_map/ppermute | solution.py:143
  153.5 10.5 %collective-permute-start.30 = (bf16[384,1536]{1,0:T(8,128)(2,1)}, bf16[384,1536]{1,0:T(8,128)(2,1)S(1)}, u32[]{:S(2)}, u32[]{:S(2)}) collective-permute-start(bf16[384,1536]{1,0:T(8,128)(2,1)} %get-tuple-element.63), channel_id=1, source_target_pairs={{0,4},{4,0},{8,12},{12,8},{16,20},{20,16},{24,28},{28,24},{1,5},{5... | collective-permute-start | bytes 3538952 | tf_op jit(solution)/shard_map/ppermute | solution.py:144
  156.4 19.9 %copy-start.2 = (f32[128,1536]{1,0:T(8,128)S(1)}, f32[128,1536]{1,0:T(8,128)}, u32[]{:S(2)}) copy-start(f32[128,1536]{1,0:T(8,128)} %get-tuple-element.55) | copy-start | bytes 2359300
  156.4 7.7 %collective-permute-start.33 = (bf16[64,1536]{1,0:T(8,128)(2,1)S(1)}, bf16[64,1536]{1,0:T(8,128)(2,1)S(1)}, u32[]{:S(2)}, u32[]{:S(2)}) collective-permute-start(bf16[64,1536]{1,0:T(8,128)(2,1)S(1)} %get-tuple-element.71), channel_id=1, source_target_pairs={{0,16},{4,12},{8,24},{12,4},{16,0},{20,28},{24,8},{28,20},{1,17},{... | collective-permute-start | bytes 589832 | tf_op jit(solution)/shard_map/ppermute | solution.py:147
  157.6 6.4 %collective-permute-start.32 = (bf16[64,1536]{1,0:T(8,128)(2,1)S(1)}, bf16[64,1536]{1,0:T(8,128)(2,1)S(1)}, u32[]{:S(2)}, u32[]{:S(2)}) collective-permute-start(bf16[64,1536]{1,0:T(8,128)(2,1)S(1)} %get-tuple-element.72), channel_id=1, source_target_pairs={{0,8},{4,20},{8,0},{12,28},{16,24},{20,4},{24,16},{28,12},{1,9},{5... | collective-permute-start | bytes 589832 | tf_op jit(solution)/shard_map/ppermute | solution.py:146
  164.3 11.9 %collective-permute-start.34 = (bf16[128,1536]{1,0:T(8,128)(2,1)S(1)}, bf16[128,1536]{1,0:T(8,128)(2,1)S(1)}, u32[]{:S(2)}, u32[]{:S(2)}) collective-permute-start(bf16[128,1536]{1,0:T(8,128)(2,1)S(1)} %get-tuple-element.69), channel_id=1, source_target_pairs={{0,8},{4,20},{8,0},{12,28},{16,24},{20,4},{24,16},{28,12},{1,9},{5... | collective-permute-start | bytes 1179656 | tf_op jit(solution)/shard_map/ppermute | solution.py:158
  165.5 10.7 %collective-permute-start.35 = (bf16[128,1536]{1,0:T(8,128)(2,1)S(1)}, bf16[128,1536]{1,0:T(8,128)(2,1)S(1)}, u32[]{:S(2)}, u32[]{:S(2)}) collective-permute-start(bf16[128,1536]{1,0:T(8,128)(2,1)S(1)} %get-tuple-element.70), channel_id=1, source_target_pairs={{0,16},{4,12},{8,24},{12,4},{16,0},{20,28},{24,8},{28,20},{1,17},{... | collective-permute-start | bytes 1179656 | tf_op jit(solution)/shard_map/ppermute | solution.py:157
  (21 other events, 38.1 us)

commit v2 on v1

--- a/solution.py
+++ b/solution.py
@@ -35,13 +35,9 @@
     return jnp.sum(jnp.where(index[..., None] == entries, table, 0), axis=-1)
 
 
-def ring(block, axis, step):
+def next_turn(block, axis):
     count = lax.axis_size(axis)
-    route = [(i, (i + step) % count) for i in range(count)]
-    held = [block]
-    for _ in range(count - 1):
-        held.append(lax.ppermute(held[-1], axis, route))
-    return held
+    return lax.ppermute(block, axis, [(i, (i + 1) % count) for i in range(count)])
 
 
 def cube_routes():
@@ -91,16 +87,7 @@
         mine = [[block], [one], [two], three]
         every = mine + [[to_partner(piece) for piece in pieces] for pieces in mine]
         return [[(piece, 0, piece.shape[0]) for piece in pieces] for pieces in every]
-    if split:
-        head = jnp.concatenate([block, one, two], axis=0)
-        tail = jnp.concatenate(three, axis=0)
-        sides = [(head, tail), (to_partner(head), to_partner(tail))]
-        return [
-            [(side[0], i * rows, rows)] if i < 3 else [(side[1], 0, rows)]
-            for side in sides
-            for i in range(4)
-        ]
-    every = after(jnp.concatenate([block, one, two] + three, axis=0), ties[2])
+    every = jnp.concatenate(after([block, one, two] + three, ties[2]), axis=0)
     return [
         [(side, i * rows, rows)] for side in (every, to_partner(every)) for i in range(4)
     ]
@@ -228,20 +215,17 @@
     return list(outs[:-1]), outs[-1]
 
 
-def attend_kernel(
-    first, blocks, near_parts, slab_spec, q_local, near_list, reach, slab_list, slab_count, fill, slab_id, place, info, *refs
-):
+def attend_kernel(block, near_parts, slab_spec, q_local, *refs):
+    near_list, reach, read, slab_list, slab_count, fill, slab_id, place = refs[:8]
+    info, query = refs[8:10]
+    near_refs = refs[10 : 10 + near_parts]
+    slab_refs = refs[10 + near_parts : -16]
+    w_ref, out = refs[-16:-14]
+    near, far, scores, peak, total, accum, begin, owner, heads, mixed, w_all = refs[-14:-3]
+    near_sems, slab_sems, w_sem = refs[-3:]
     parts = near_list.shape[0]
-    total_in = blocks + near_parts + 1 + max(array for [(array, _, _)] in slab_spec)
-    q_refs = refs[:blocks]
-    near_refs = refs[blocks : blocks + near_parts]
-    slab_refs = refs[blocks + near_parts : total_in]
-    outs = refs[total_in : total_in + blocks]
-    q_all, near, far, scores, peak, total, accum, begin, owner, heads, sems, slab_sems = refs[
-        total_in + blocks :
-    ]
-    kv_local, stack, _ = q_refs[0].shape
-    rows_dev = info.shape[1]
+    kv_local, stack, _ = query.shape
+    rows_dev = info.shape[0]
     share = stack // rows_dev
     cuts = PREFIX // LANES
     window = parts + 1
@@ -251,9 +235,7 @@
     def lanes(ref, g, rows, start=0):
         return ref.at[pl.ds(start, rows), pl.ds(g * LANES, LANES)]
 
-    copies = [
-        pltpu.make_async_copy(ref, q_all.at[i], sems.at[i, 0]) for i, ref in enumerate(q_refs)
-    ]
+    copies = []
     base = 0
     for i, ref in enumerate(near_refs):
         for g in range(kv_local):
@@ -261,152 +243,153 @@
                 pltpu.make_async_copy(
                     lanes(ref, g, ref.shape[0]),
                     near.at[g, pl.ds(base, ref.shape[0])],
-                    sems.at[blocks + i, g],
+                    near_sems.at[i, g],
                 )
             )
         base += ref.shape[0]
-    slab_copies = [
-        pltpu.make_async_copy(
-            lanes(slab_refs[array], g, rows, start),
-            far.at[g, pl.ds(i * PREFIX, PREFIX)],
-            slab_sems.at[i, g],
+
+    def each_slab(act):
+        for i, [(array, start, _)] in enumerate(slab_spec):
+            @pl.when(read[block, i] != 0)
+            def _(i=i, array=array, start=start):
+                for g in range(kv_local):
+                    act(
+                        pltpu.make_async_copy(
+                            lanes(slab_refs[array], g, PREFIX, start),
+                            far.at[g, pl.ds(i * PREFIX, PREFIX)],
+                            slab_sems.at[i, g],
+                        )
+                    )
+
+    w_copy = pltpu.make_async_copy(w_ref, w_all, w_sem)
+    for copy in copies:
+        copy.start()
+    each_slab(lambda copy: copy.start())
+    w_copy.start()
+    for ref, column in ((owner, 0), (begin, 1)):
+        tall = jnp.concatenate([info[:, column : column + 1]] * share, axis=0)
+        ref[...] = jnp.broadcast_to(tall, wide)
+    row = lax.broadcasted_iota(jnp.int32, wide, 0)
+    order = row - lax.div(row, rows_dev) * rows_dev
+    for copy in copies:
+        copy.wait()
+
+    def rows_near(g, back):
+        unit = near_list[block, back]
+        return near[g, pl.ds(pl.multiple_of(unit * rows_dev, rows_dev), rows_dev), :]
+
+    def rows_window(g, backs):
+        return jnp.concatenate([rows_near(g, back) for back in backs], axis=0)
+
+    def rows_far(g, slab):
+        return far[g, pl.ds(pl.multiple_of(slab * PREFIX, PREFIX), PREFIX), :]
+
+    def score(g, rows):
+        return lax.dot_general(
+            query[g], rows, (((1,), (1,)), ((), ())), preferred_element_type=F32
         )
-        for i, [(array, start, rows)] in enumerate(slab_spec)
-        for g in range(kv_local)
-    ]
-    for copy in copies + slab_copies:
-        copy.start()
-    for copy in copies + slab_copies:
-        copy.wait()
-
-    @pl.loop(0, blocks)
-    def _(i):
-        block = lax.rem(first + i, parts)
-        columns = info[block]
-        for ref, column in ((owner, 0), (begin, 1)):
-            tall = jnp.concatenate([columns[:, column : column + 1]] * share, axis=0)
-            ref[...] = jnp.broadcast_to(tall, wide)
-        row = lax.broadcasted_iota(jnp.int32, wide, 0)
-        order = row - lax.div(row, rows_dev) * rows_dev
-
-        def rows_near(g, back):
-            unit = near_list[block, back]
-            return near[g, pl.ds(pl.multiple_of(unit * rows_dev, rows_dev), rows_dev), :]
-
-        def rows_window(g, backs):
-            return jnp.concatenate([rows_near(g, back) for back in backs], axis=0)
-
-        def rows_far(g, slab):
-            return far[g, pl.ds(pl.multiple_of(slab * PREFIX, PREFIX), PREFIX), :]
-
-        def score(g, rows):
-            return lax.dot_general(
-                q_all[i, g], rows, (((1,), (1,)), ((), ())), preferred_element_type=F32
-            )
-
-        def near_scores(backs, opening):
-            for g in range(kv_local):
-                every = score(g, rows_window(g, backs))
-                top = None if opening else peak[g]
-                for at, back in enumerate(backs):
-                    there = place[near_list[block, back]] + lane
-                    seen = there >= begin[...]
-                    if back == 0:
-                        seen = seen & (lane <= order)
-                    here = every[:, at * LANES : (at + 1) * LANES]
-                    here = jnp.where(seen, here, NEG_FILL)
-                    scores[g, back] = here
-                    top = here if top is None else jnp.maximum(top, here)
-                peak[g] = top
-
-        def far_scores(slab):
-            mine = owner[...] == slab_id[slab]
-            for g in range(kv_local):
-                every = score(g, rows_far(g, slab))
-                top = None
-                for c in range(cuts):
-                    here = every[:, c * LANES : (c + 1) * LANES]
-                    if (c + 1) * LANES > PREFIX // 2:
-                        here = jnp.where(lane + c * LANES < fill[slab], here, NEG_FILL)
-                    scores[g, window + slab * cuts + c] = here
-                    top = here if top is None else jnp.maximum(top, here)
-                old = peak[g]
-                peak[g] = jnp.where(mine, jnp.maximum(old, top), old)
-
-        def near_values(backs, opening):
-            for g in range(kv_local):
-                weights = [jnp.exp(scores[g, back] - peak[g]) for back in backs]
-                packed = jnp.concatenate([part.astype(BF16) for part in weights], axis=1)
-                summed = functools.reduce(jnp.add, weights)
-                mixed = jnp.dot(packed, rows_window(g, backs), preferred_element_type=F32)
-                if opening:
-                    total[g] = summed
-                    accum[g] = mixed
-                else:
-                    total[g] += summed
-                    accum[g] += mixed
-
-        def far_values(slab):
-            mine = owner[...] == slab_id[slab]
-            for g in range(kv_local):
-                shift = jnp.where(mine, peak[g], -NEG_FILL)
-                weights = [
-                    jnp.exp(scores[g, window + slab * cuts + c] - shift) for c in range(cuts)
-                ]
-                packed = jnp.concatenate([part.astype(BF16) for part in weights], axis=1)
-                total[g] += functools.reduce(jnp.add, weights)
-                accum[g] += jnp.dot(packed, rows_far(g, slab), preferred_element_type=F32)
-
-        def sweep(near_body, far_body):
-            near_body((0, 1), True)
-
-            @pl.when(reach[block] != 0)
-            def _():
-                near_body(tuple(range(2, window)), False)
-
-            @pl.loop(0, slab_count[block])
-            def _(turn):
-                far_body(slab_list[block, turn])
-
-        sweep(near_scores, far_scores)
+
+    def near_scores(backs, opening):
         for g in range(kv_local):
-            peak[g] = jnp.broadcast_to(jnp.max(peak[g], axis=1, keepdims=True), wide)
-        sweep(near_values, far_values)
+            every = score(g, rows_window(g, backs))
+            top = None if opening else peak[g]
+            for at, back in enumerate(backs):
+                there = place[near_list[block, back]] + lane
+                seen = there >= begin[...]
+                if back == 0:
+                    seen = seen & (lane <= order)
+                here = every[:, at * LANES : (at + 1) * LANES]
+                here = jnp.where(seen, here, NEG_FILL)
+                scores[g, back] = here
+                top = here if top is None else jnp.maximum(top, here)
+            peak[g] = top
+
+    def far_scores(slab):
+        mine = owner[...] == slab_id[slab]
         for g in range(kv_local):
-            result = accum[g] / jnp.sum(total[g], axis=1, keepdims=True)
-            for slot in range(share):
-                heads[g * share + slot] = result[slot * rows_dev : (slot + 1) * rows_dev]
-
-        low = lax.broadcasted_iota(jnp.int32, (rows_dev, LANES), 1) < HS
-        done = []
-        for pair in range((q_local + 1) // 2):
-            left = pltpu.roll(heads[2 * pair], HS, 1)
-            if 2 * pair + 1 < q_local:
-                done.append(jnp.where(low, left, heads[2 * pair + 1]).astype(BF16))
+            every = score(g, rows_far(g, slab))
+            top = None
+            for c in range(cuts):
+                here = every[:, c * LANES : (c + 1) * LANES]
+                if (c + 1) * LANES > PREFIX // 2:
+                    here = jnp.where(lane + c * LANES < fill[slab], here, NEG_FILL)
+                scores[g, window + slab * cuts + c] = here
+                top = here if top is None else jnp.maximum(top, here)
+            old = peak[g]
+            peak[g] = jnp.where(mine, jnp.maximum(old, top), old)
+
+    def near_values(backs, opening):
+        for g in range(kv_local):
+            weights = [jnp.exp(scores[g, back] - peak[g]) for back in backs]
+            packed = jnp.concatenate([part.astype(BF16) for part in weights], axis=1)
+            summed = functools.reduce(jnp.add, weights)
+            product = jnp.dot(packed, rows_window(g, backs), preferred_element_type=F32)
+            if opening:
+                total[g] = summed
+                accum[g] = product
             else:
-                done.append(left[:, :HS].astype(BF16))
-        for j in range(blocks):
-            @pl.when(i == j)
-            def _(j=j):
-                for pair, part in enumerate(done):
-                    outs[j][:, pair * LANES : pair * LANES + part.shape[1]] = part
-
-
-def attend(first, tables, info, queries, near, slabs, q_local):
-    blocks = len(queries)
+                total[g] += summed
+                accum[g] += product
+
+    def far_values(slab):
+        mine = owner[...] == slab_id[slab]
+        for g in range(kv_local):
+            shift = jnp.where(mine, peak[g], -NEG_FILL)
+            weights = [
+                jnp.exp(scores[g, window + slab * cuts + c] - shift) for c in range(cuts)
+            ]
+            packed = jnp.concatenate([part.astype(BF16) for part in weights], axis=1)
+            total[g] += functools.reduce(jnp.add, weights)
+            accum[g] += jnp.dot(packed, rows_far(g, slab), preferred_element_type=F32)
+
+    def sweep(near_body, far_body, between=None):
+        near_body((0, 1), True)
+
+        @pl.when(reach[block] != 0)
+        def _():
+            near_body(tuple(range(2, window)), False)
+
+        if between is not None:
+            between()
+
+        @pl.loop(0, slab_count[block])
+        def _(turn):
+            far_body(slab_list[block, turn])
+
+    sweep(near_scores, far_scores, lambda: each_slab(lambda copy: copy.wait()))
+    for g in range(kv_local):
+        peak[g] = jnp.broadcast_to(jnp.max(peak[g], axis=1, keepdims=True), wide)
+    sweep(near_values, far_values)
+    for g in range(kv_local):
+        result = accum[g] / jnp.sum(total[g], axis=1, keepdims=True)
+        for slot in range(share):
+            heads[g * share + slot] = result[slot * rows_dev : (slot + 1) * rows_dev]
+
+    low = lax.broadcasted_iota(jnp.int32, (rows_dev, LANES), 1) < HS
+    for pair in range((q_local + 1) // 2):
+        left = pltpu.roll(heads[2 * pair], HS, 1)
+        here = slice(pair * LANES, (pair + 1) * LANES)
+        if 2 * pair + 1 < q_local:
+            mixed[:, here] = jnp.where(low, left, heads[2 * pair + 1]).astype(BF16)
+        else:
+            mixed[:, pair * LANES :] = left[:, :HS].astype(BF16)
+    w_copy.wait()
+    out[...] = jnp.dot(mixed[...], w_all[...], preferred_element_type=F32).astype(out.dtype)
+
+
+def attend(block, tables, info, query, near, slabs, w_out, q_local, held_as):
     parts = info.shape[0]
-    kv_local, stack, _ = queries[0].shape
+    kv_local, stack, _ = query.shape
     rows_dev = info.shape[1]
     units = parts + 1 + len(slabs) * (PREFIX // LANES)
+    wide = (stack, LANES)
     arrays, slab_spec = flatten(slabs)
-    wide = (stack, LANES)
     return pl.pallas_call(
-        functools.partial(attend_kernel, first, blocks, len(near), slab_spec, q_local),
-        out_shape=[jax.ShapeDtypeStruct((rows_dev, q_local * HS), BF16)] * blocks,
-        in_specs=[SMEM] * 7 + [vmem()] + [ANY] * (blocks + len(near) + len(arrays)),
-        out_specs=[vmem()] * blocks,
+        functools.partial(attend_kernel, block, len(near), slab_spec, q_local),
+        out_shape=jax.ShapeDtypeStruct((rows_dev, w_out.shape[1]), held_as),
+        in_specs=[SMEM] * 8 + [vmem()] * 2 + [ANY] * (len(near) + len(arrays) + 1),
+        out_specs=vmem(),
         scratch_shapes=[
-            pltpu.VMEM((blocks,) + queries[0].shape, BF16),
             pltpu.VMEM((kv_local, 2 * parts * rows_dev, LANES), BF16),
             pltpu.VMEM((kv_local, len(slabs) * PREFIX, LANES), BF16),
             pltpu.VMEM((kv_local, units) + wide, F32),
@@ -416,95 +399,60 @@
             pltpu.VMEM(wide, jnp.int32),
             pltpu.VMEM(wide, jnp.int32),
             pltpu.VMEM((q_local, rows_dev, LANES), F32),
-            pltpu.SemaphoreType.DMA((blocks + len(near), kv_local)),
+            pltpu.VMEM((rows_dev, q_local * HS), BF16),
+            pltpu.VMEM(w_out.shape, BF16),
+            pltpu.SemaphoreType.DMA((len(near), kv_local)),
             pltpu.SemaphoreType.DMA((len(slabs), kv_local)),
+            pltpu.SemaphoreType.DMA,
         ],
         compiler_params=params(),
         cost_estimate=pl.CostEstimate(
-            flops=12 * 10**9, bytes_accessed=4 * 10**6, transcendentals=10**6
+            flops=8 * 10**9, bytes_accessed=4 * 10**6, transcendentals=10**6
         ),
         name="attend",
     )(
         tables["near_list"],
         tables["reach"],
+        tables["read"],
         tables["slab_list"],
         tables["slab_count"],
         tables["fill"],
         tables["slab_id"],
         tables["place"],
-        info,
-        *queries,
+        info[block],
+        query,
         *near,
         *arrays,
+        w_out,
     )
 
 
-def out_kernel(groups, cut, spec, origins, *refs):
-    pieces = refs[:groups]
-    w_own = refs[groups]
-    w_far = refs[groups + 1 : -7]
-    tokens, gain, hidden, expert_in, weights, sems, own_sem = refs[-7:]
-    own = pltpu.make_async_copy(w_own, weights.at[0], own_sem)
-    own.start()
-    copies = []
-    for k, pieces_k in enumerate(spec):
-        if cut:
-            first = pl.multiple_of(origins[k] * cut, 16)
-            for j in range(groups - 1):
-                for i, (array, there, offset, rows) in enumerate(
-                    row_ranges(pieces_k, j * cut, cut)
-                ):
-                    copies.append(
-                        pltpu.make_async_copy(
-                            w_far[array].at[pl.ds(there, rows)],
-                            weights.at[j + 1, pl.ds(first + offset, rows)],
-                            sems.at[k, 2 * j + i],
-                        )
-                    )
-        else:
-            copies.append(
-                pltpu.make_async_copy(w_far[pieces_k[0][0]], weights.at[k + 1], sems.at[k, 0])
-            )
-    for copy in copies:
-        copy.start()
-    own.wait()
-    total = tokens[...].astype(F32) + jnp.dot(
-        pieces[0][...], weights[0], preferred_element_type=F32
-    )
-    for copy in copies:
-        copy.wait()
-    for j in range(1, groups):
-        total += jnp.dot(pieces[j][...], weights[j], preferred_element_type=F32)
+def hidden_kernel(tokens, gain, own, *refs):
+    others = refs[:-2]
+    hidden, expert_in = refs[-2:]
+    total = tokens[...].astype(F32) + own[...]
+    for other in others:
+        total += other[...].astype(F32)
     hidden[...] = total
     spread = jnp.mean(total * total, axis=-1, keepdims=True)
     expert_in[...] = (total * lax.rsqrt(spread + NORM_EPS) * gain[...]).astype(BF16)
 
 
-def project_out(pieces, w_own, w_far, cut, origins, tokens, gain):
-    groups = len(pieces)
-    rows, width = tokens.shape
-    w_far, spec = flatten(w_far)
+def add_and_norm(tokens, gain, own, others):
     return pl.pallas_call(
-        functools.partial(out_kernel, groups, cut, spec),
+        hidden_kernel,
         out_shape=(
-            jax.ShapeDtypeStruct((rows, width), F32),
-            jax.ShapeDtypeStruct((rows, width), BF16),
-        ),
-        in_specs=[SMEM] + [vmem()] * groups + [ANY] * (1 + len(w_far)) + [vmem(), vmem()],
+            jax.ShapeDtypeStruct(tokens.shape, F32),
+            jax.ShapeDtypeStruct(tokens.shape, BF16),
+        ),
+        in_specs=[vmem()] * (3 + len(others)),
         out_specs=(vmem(), vmem()),
-        scratch_shapes=[
-            pltpu.VMEM((groups,) + w_own.shape, BF16),
-            pltpu.SemaphoreType.DMA((len(spec), 2 * groups)),
-            pltpu.SemaphoreType.DMA,
-        ],
         compiler_params=params(),
         cost_estimate=pl.CostEstimate(
-            flops=5 * 10**9,
-            bytes_accessed=2 * groups * w_own.size + 8 * rows * width,
-            transcendentals=rows,
-        ),
-        name="project_out_norm",
-    )(origins, *pieces, w_own, *w_far, tokens, gain)
+            flops=10**9, bytes_accessed=16 * tokens.size, transcendentals=tokens.shape[0]
+        ),
+        name="add_and_norm",
+    )(tokens, gain, own, *others)
 
 
 def expert_kernel(spec, rows, slot_row, gate_row, slot_col, *refs):
@@ -772,7 +720,9 @@
     q_local = w_query.shape[1] // HS
     origins = plane_origins()
 
-    turns = ring(tokens, "head", 1)
+    turns = [tokens]
+    for _ in range(groups // 2):
+        turns.append(next_turn(turns[-1], "head"))
 
     steps = jnp.arange(groups, dtype=jnp.int32)
     block_of = (me_head - steps) % groups
@@ -804,6 +754,7 @@
         "near_list": (steps[:, None] + backs[None, :]) % groups
         + jnp.where(block_of[:, None] >= backs[None, :], groups, 0),
         "reach": (begin[:, 0] < place - rows_dev).astype(jnp.int32),
+        "read": read,
         "slab_list": jnp.sum(
             jnp.where(
                 (rank[:, :, None] == spot[None, None, :]) & (read[:, :, None] != 0),
@@ -822,9 +773,11 @@
     if missing:
         w_query = jnp.pad(w_query, ((0, 0), (0, missing)))
     queries, own, prev = [], [], []
-    for some in (slice(0, groups - 1), slice(groups - 1, groups)):
+    for some in (slice(0, groups // 2), slice(groups // 2, groups)):
+        while len(turns) < some.stop:
+            turns.append(next_turn(after(turns[-1], own[0]), "head"))
         query, keyval = project(
-            after(turns[some], own[0]) if own else turns[some],
+            turns[some],
             attn_gain[None, :],
             w_query,
             w_keyval,
@@ -837,45 +790,44 @@
         own.append(keyval)
         prev.append(lax.ppermute(keyval, "tok", [(i, i + 1) for i in range(tok_count - 1)]))
 
-    cached = plane_gather(prefix_cache, False, True, [turns[1], None, own[0]])
-
     def exchanged(block, j):
         return lax.ppermute(block, "head", [(i, (i - j) % groups) for i in range(groups)])
 
+    lanes = prefix_cache.shape[1]
+    packed = packed_routes(routes, route_gates, lanes)
+    cached = plane_gather(
+        jnp.concatenate([prefix_cache, packed], axis=0), False, True, [own[0], None, turns[-1]]
+    )
+
     near = prev + own
-    cut = w_out.shape[0] // tok_count if tok_count == 8 else 0
-    share = lax.dynamic_slice_in_dim(w_out, me_tok * cut, cut, 0) if cut else w_out
-    share = after(share, own[-1])
-    w_far = [exchanged(share, s) for s in range(1, groups)]
-    middle = groups // 2
-    early = attend(1, tables, info, queries[1 : middle + 1], near, cached, q_local)
-    late = attend(
-        middle + 1, tables, info, queries[middle + 1 :] + queries[:1], near, cached, q_local
-    )
-    mixed = [exchanged(block, 1 + i) for i, block in enumerate(early)]
-    packed = packed_routes(routes, route_gates, 2 * LANES)
-    if cut:
-        w_far = after(w_far, early[0])
-        packed = jnp.pad(packed, ((0, 0), (0, width - packed.shape[1])))
-        w_far = plane_gather(
-            jnp.concatenate(w_far + [packed], axis=0), True, True, [None, (late[0], mixed), None]
-        )
-        route_parts = w_far
-    else:
-        route_parts = plane_gather(packed, False, False)
-        w_far = [[(block, 0, block.shape[0])] for block in w_far]
+
+    def term(j, held_as):
+        return attend(j, tables, info, queries[j], near, cached, w_out, q_local, held_as)
+
+    down = groups // 2
+    up = groups - 1 - down
+    lower = upper = None
+    for turn in range(down):
+        here = term(down - turn, BF16)
+        if lower is not None:
+            here = (here.astype(F32) + lower.astype(F32)).astype(BF16)
+        lower = exchanged(here, 1)
+        if turn < up:
+            here = term(groups - up + turn, BF16)
+            if upper is not None:
+                here = (here.astype(F32) + upper.astype(F32)).astype(BF16)
+            upper = exchanged(here, groups - 1)
+    terms = [lower] if upper is None else [lower, upper]
+    own_term = term(0, F32)
+    hidden, expert_in = add_and_norm(tokens, ffn_gain[None, :], own_term, terms)
+
     exp_local = w_gate.shape[0]
     route = route_tables(
-        route_parts,
+        cached,
         packed.shape[0],
-        2 * LANES,
+        lanes,
         (me_tok * exp_local).astype(jnp.int32).reshape(1),
         exp_local,
-    )
-    mixed += [exchanged(block, middle + 1 + i) for i, block in enumerate(late[:-1])]
-    mixed = [late[-1]] + mixed
-    hidden, expert_in = project_out(
-        mixed, w_out, w_far, cut, origins, tokens, ffn_gain[None, :]
     )
     blocks = plane_gather(expert_in, True, False, [None, route[0], None])
     near, far, last = experts(blocks, *route, w_gate, w_up, w_down)

time: 178 us -> 166 us (0.933)
  waiting for transfers between devices: 59.1 us -> 52.6 us
  local copies, waits for them, and re-layouts: 9.78 us -> 7.7 us
  starting transfers between devices: 33.8 us -> 31.9 us
    ppermute x2 -> x1, waiting for transfers between devices: 7.55 us -> 0.04 us  [plane_gather(): lax.ppermute(one[:half], 'tok', second)]
    ppermute x3 -> x2, starting transfers between devices: 1.96 us -> 5.33 us  [plane_gather(): two = lax.ppermute(block, 'tok', second)]
    ppermute x3 -> x2, starting transfers between devices: 3.66 us -> 0.76 us  [plane_gather(): one = lax.ppermute(block, 'tok', first)]
    ppermute x1, waiting for transfers between devices: 3.1 us -> 5.5 us  [plane_gather(): three = [lax.ppermute(block, 'tok', [(t, t ^ 6) for t in range(8)])]]
    ppermute x3, waiting for transfers between devices: 12.1 us -> 9.79 us  [next_turn(): lax.ppermute(block, axis, [(i, (i + 1) % count) for i in range(count)])]
    unnamed x71 -> x59, local copies, waits for them, and re-layouts: 4.85 us -> 2.88 us
    ppermute x3 -> x2, waiting for transfers between devices: 11 us -> 9.73 us  [plane_gather(): two = lax.ppermute(block, 'tok', second)]
    ppermute x6 -> x3, starting transfers between devices: 8.24 us -> 7.74 us  [exchanged(): lax.ppermute(block, 'head', [(i, (i - j) % groups) for i in range(groups)])]
  transfers between devices with their start and end apart: 36 -> 27, of which waited for: 15 -> 14; matrix products, arithmetic and copies ran while one was open for 10% -> 10% of each run, Pallas kernels for 15% -> 17%
where the time goes in v2:
time: 166 us; the launch traced here: 167 us
  Pallas kernels  60.1 us (36%)
  waiting for transfers between devices  52.6 us (32%)
  starting transfers between devices  31.9 us (19%)
  other arithmetic  13.8 us (8%)
  local copies, waits for them, and re-layouts  7.7 us (5%)
    pallas_call x4, Pallas kernels, attend(): pl.pallas_call(functools.partial(attend_kernel, block, len(near), slab_sp...  24.1 us
    pallas_call x1, Pallas kernels, experts(): pl.pallas_call(functools.partial(expert_kernel, spec, rows), out_shape=tu...  23.6 us
    ppermute x3, waiting for transfers between devices, next_turn(): lax.ppermute(block, axis, [(i, (i + 1) % count) for i in range(count)])  9.79 us
    ppermute x2, waiting for transfers between devices, plane_gather(): two = lax.ppermute(block, 'tok', second)  9.73 us
    ppermute x1, waiting for transfers between devices, plane_sum(): beside = lax.ppermute((pair(2) + add_lower).astype(BF16), 'tok', second)  9.68 us
    ppermute x3, starting transfers between devices, exchanged(): lax.ppermute(block, 'head', [(i, (i - j) % groups) for i in range(groups)])  7.74 us
    pallas_call x2, Pallas kernels, project(): pl.pallas_call(functools.partial(project_kernel, blocks, kv_local, q_loca...  7.64 us
    ppermute x1, waiting for transfers between devices, plane_sum(): across_lower = lax.ppermute(three[half:], 'tok', first)  5.66 us
  transfers between devices with their start and end apart: 27, of which 14 were waited for; matrix products, arithmetic and copies ran while one was open for 10% of the time, Pallas kernels for 17%

profile of v2, /device:TPU:0, one launch (start us, length us, event | category | flops | bytes accessed | tf_op | source)
XLA Modules:
  0.0 166.7 jit_solution(3117234928515600163)
XLA Ops:
  0.0 3.0 %collective-permute-start = (bf16[128,1536]{1,0:T(8,128)(2,1)}, bf16[128,1536]{1,0:T(8,128)(2,1)S(1)}, u32[]{:S(2)}, u32[]{:S(2)}) collective-permute-start(bf16[128,1536]{1,0:T(8,128)(2,1)} %tokens.1), channel_id=1, source_target_pairs={{0,1},{1,2},{2,3},{3,0},{4,5},{5,6},{6,7},{7,4},{8,9},{9,10},{10,1... | collective-permute-start | bytes 1179656 | tf_op jit(solution)/shard_map/ppermute | solution.py:40
  3.1 0.9 convert_reduce_fusion
  4.1 0.8 dynamic-slice_bitcast_fusion
  4.8 0.8 select_reduce_fusion.7
  6.1 0.7 select_reduce_fusion.2
  8.9 1.0 fusion
  10.4 0.7 fusion.9
  11.4 0.7 fusion.8
  12.1 2.2 %collective-permute-done.refs_1_ = bf16[128,1536]{1,0:T(8,128)(2,1)S(1)} collective-permute-done((bf16[128,1536]{1,0:T(8,128)(2,1)}, bf16[128,1536]{1,0:T(8,128)(2,1)S(1)}, u32[]{:S(2)}, u32[]{:S(2)}) %collective-permute-start) | collective-permute-done | bytes 393248 | tf_op jit(solution)/shard_map/ppermute | solution.py:40
  14.4 0.7 broadcast_in_dim.147.refs_2_
  15.1 3.8 %norm_project_rotate.2 = (bf16[2,384,128]{2,1,0:T(8,128)(2,1)}, bf16[2,384,128]{2,1,0:T(8,128)(2,1)}, bf16[256,256]{1,0:T(8,128)(2,1)}) custom-call(bf16[128,1536]{1,0:T(8,128)(2,1)} %tokens.1, bf16[128,1536]{1,0:T(8,128)(2,1)} %copy-done.12, f32[1,1536]{1,0:T(1,128)} %broadcast_in_dim.147.refs_2_, bf16[1536,384]{1,0:T(8,128)(2,1)} %refs_3_.3, ...), custom_call_target="tpu_custom_call" | custom-call | flops 4000000000 | bytes 4000000 | tf_op jit(solution)/shard_map/norm_project_rotate/pallas_call | solution.py:202
  18.9 7.5 %collective-permute-done.2.refs_0_ = bf16[128,1536]{1,0:T(8,128)(2,1)S(1)} collective-permute-done((bf16[128,1536]{1,0:T(8,128)(2,1)S(1)}, bf16[128,1536]{1,0:T(8,128)(2,1)S(1)}, u32[]{:S(2)}, u32[]{:S(2)}) %collective-permute-start.2) | collective-permute-done | bytes 393248 | tf_op jit(solution)/shard_map/ppermute | solution.py:40
  26.6 2.2 %collective-permute-start.7 = (bf16[528,256]{1,0:T(8,128)(2,1)S(1)}, bf16[528,256]{1,0:T(8,128)(2,1)S(1)}, u32[]{:S(2)}, u32[]{:S(2)}) collective-permute-start(bf16[528,256]{1,0:T(8,128)(2,1)S(1)} %maximum_maximum_fusion), channel_id=1, source_target_pairs={{0,24},{4,28},{8,16},{12,20},{16,8},{20,12},{24,0},{28,4},{1,25},{... | collective-permute-start | bytes 811016 | tf_op jit(solution)/shard_map/ppermute | solution.py:85
  29.3 0.8 collective-permute-start.5
  30.1 0.8 select_reduce_fusion.6.refs_5_
  31.4 5.5 %collective-permute-done.7 = bf16[528,256]{1,0:T(8,128)(2,1)S(1)} collective-permute-done((bf16[528,256]{1,0:T(8,128)(2,1)S(1)}, bf16[528,256]{1,0:T(8,128)(2,1)S(1)}, u32[]{:S(2)}, u32[]{:S(2)}) %collective-permute-start.7) | collective-permute-done | bytes 270368 | tf_op jit(solution)/shard_map/ppermute | solution.py:85
  36.9 2.7 %collective-permute-done.6 = bf16[528,256]{1,0:T(8,128)(2,1)S(1)} collective-permute-done((bf16[528,256]{1,0:T(8,128)(2,1)S(1)}, bf16[528,256]{1,0:T(8,128)(2,1)S(1)}, u32[]{:S(2)}, u32[]{:S(2)}) %collective-permute-start.6) | collective-permute-done | bytes 270368 | tf_op jit(solution)/shard_map/ppermute | solution.py:77
  40.3 0.8 convert_reduce_fusion.1.refs_4_
  41.7 0.7 slice_bitcast_fusion
  42.4 2.3 %collective-permute-start.1 = (bf16[256,256]{1,0:T(8,128)(2,1)S(1)}, bf16[256,256]{1,0:T(8,128)(2,1)S(1)}, u32[]{:S(2)}, u32[]{:S(2)}) collective-permute-start(bf16[256,256]{1,0:T(8,128)(2,1)S(1)} %copy-done.25), channel_id=1, source_target_pairs={{0,4},{4,8},{8,12},{12,16},{16,20},{20,24},{24,28},{1,5},{5,9},{9,... | collective-permute-start | bytes 393224 | tf_op jit(solution)/shard_map/ppermute | solution.py:791
  44.7 3.8 %norm_project_rotate.3 = (bf16[2,384,128]{2,1,0:T(8,128)(2,1)}, bf16[2,384,128]{2,1,0:T(8,128)(2,1)}, bf16[256,256]{1,0:T(8,128)(2,1)}) custom-call(bf16[128,1536]{1,0:T(8,128)(2,1)} %copy-done.14, bf16[128,1536]{1,0:T(8,128)(2,1)} %copy-done.15, f32[1,1536]{1,0:T(1,128)} %broadcast_in_dim.147.refs_2_, bf16[1536,384]{1,0:T(8,128)(2,1)} %refs_3_.3, ...), custom_call_target="tpu_custom_call" | custom-call | flops 4000000000 | bytes 4000000 | tf_op jit(solution)/shard_map/norm_project_rotate/pallas_call | solution.py:202
  48.6 2.8 %collective-permute-start.4 = (bf16[256,256]{1,0:T(8,128)(2,1)}, bf16[256,256]{1,0:T(8,128)(2,1)S(1)}, u32[]{:S(2)}, u32[]{:S(2)}) collective-permute-start(bf16[256,256]{1,0:T(8,128)(2,1)} %get-tuple-element.32.refs_13_), channel_id=1, source_target_pairs={{0,4},{4,8},{8,12},{12,16},{16,20},{20,24},{24,28},{1,5},{5,9},{9,... | collective-permute-start | bytes 393224 | tf_op jit(solution)/shard_map/ppermute | solution.py:791
  54.3 5.1 %attend.6 = bf16[128,1536]{1,0:T(8,128)(2,1)} custom-call(s32[4,5]{1,0:T(4,128)} %fusion.5.refs_0_, s32[4]{0:T(128)} %compare_convert_fusion.refs_1_, s32[4,8]{1,0:T(4,128)} %copy-done.8, s32[4,8]{1,0:T(4,128)} %select_reduce_fusion.3.refs_3_, s32[4]{0:T(128)} %convert_reduce_fusion.1.refs_4_, s32[8]{0:T(128)} %select_reduce_fusion.6.refs_5_, s32[8]{0:T(128)} %copy-done.9, ...), custom_call_target="tpu_custom_call" | custom-call | flops 8000000000 | bytes 4000000 | tf_op jit(solution)/shard_map/attend/pallas_call | solution.py:387
  59.4 4.5 %collective-permute-start.9 = (bf16[128,1536]{1,0:T(8,128)(2,1)}, bf16[128,1536]{1,0:T(8,128)(2,1)S(1)}, u32[]{:S(2)}, u32[]{:S(2)}) collective-permute-start(bf16[128,1536]{1,0:T(8,128)(2,1)} %attend.6), channel_id=1, source_target_pairs={{0,3},{1,0},{2,1},{3,2},{4,7},{5,4},{6,5},{7,6},{8,11},{9,8},{10,9... | collective-permute-start | bytes 1179656 | tf_op jit(solution)/shard_map/ppermute | solution.py:794
  63.9 6.0 %attend.7 = bf16[128,1536]{1,0:T(8,128)(2,1)} custom-call(s32[4,5]{1,0:T(4,128)} %fusion.5.refs_0_, s32[4]{0:T(128)} %compare_convert_fusion.refs_1_, s32[4,8]{1,0:T(4,128)} %copy-done.8, s32[4,8]{1,0:T(4,128)} %select_reduce_fusion.3.refs_3_, s32[4]{0:T(128)} %convert_reduce_fusion.1.refs_4_, s32[8]{0:T(128)} %select_reduce_fusion.6.refs_5_, s32[8]{0:T(128)} %copy-done.9, ...), custom_call_target="tpu_custom_call" | custom-call | flops 8000000000 | bytes 4000000 | tf_op jit(solution)/shard_map/attend/pallas_call | solution.py:387
  70.0 5.9 %attend.5 = bf16[128,1536]{1,0:T(8,128)(2,1)} custom-call(s32[4,5]{1,0:T(4,128)} %fusion.5.refs_0_, s32[4]{0:T(128)} %compare_convert_fusion.refs_1_, s32[4,8]{1,0:T(4,128)} %copy-done.8, s32[4,8]{1,0:T(4,128)} %select_reduce_fusion.3.refs_3_, s32[4]{0:T(128)} %convert_reduce_fusion.1.refs_4_, s32[8]{0:T(128)} %select_reduce_fusion.6.refs_5_, s32[8]{0:T(128)} %copy-done.9, ...), custom_call_target="tpu_custom_call" | custom-call | flops 8000000000 | bytes 4000000 | tf_op jit(solution)/shard_map/attend/pallas_call | solution.py:387
  75.9 1.1 add_convert_fusion.4
  77.0 3.2 %collective-permute-start.10 = (bf16[128,1536]{1,0:T(8,128)(2,1)S(1)}, bf16[128,1536]{1,0:T(8,128)(2,1)S(1)}, u32[]{:S(2)}, u32[]{:S(2)}) collective-permute-start(bf16[128,1536]{1,0:T(8,128)(2,1)S(1)} %add_convert_fusion.4), channel_id=1, source_target_pairs={{0,3},{1,0},{2,1},{3,2},{4,7},{5,4},{6,5},{7,6},{8,11},{9,8},{10,9... | collective-permute-start | bytes 1179656 | tf_op jit(solution)/shard_map/ppermute | solution.py:794
  80.2 7.1 %attend.4.own = f32[128,1536]{1,0:T(8,128)} custom-call(s32[4,5]{1,0:T(4,128)} %fusion.5.refs_0_, s32[4]{0:T(128)} %compare_convert_fusion.refs_1_, s32[4,8]{1,0:T(4,128)} %copy-done.8, s32[4,8]{1,0:T(4,128)} %select_reduce_fusion.3.refs_3_, s32[4]{0:T(128)} %convert_reduce_fusion.1.refs_4_, s32[8]{0:T(128)} %select_reduce_fusion.6.refs_5_, s32[8]{0:T(128)} %copy-done.9, ...), custom_call_target="tpu_custom_call" | custom-call | flops 8000000000 | bytes 4000000 | tf_op jit(solution)/shard_map/attend/pallas_call | solution.py:387
  87.3 3.6 %collective-permute-done.10.refs_0_ = bf16[128,1536]{1,0:T(8,128)(2,1)S(1)} collective-permute-done((bf16[128,1536]{1,0:T(8,128)(2,1)S(1)}, bf16[128,1536]{1,0:T(8,128)(2,1)S(1)}, u32[]{:S(2)}, u32[]{:S(2)}) %collective-permute-start.10) | collective-permute-done | bytes 393248 | tf_op jit(solution)/shard_map/ppermute | solution.py:794
  90.9 0.7 copy-done.20
  91.6 2.8 %add_and_norm.1 = (f32[128,1536]{1,0:T(8,128)}, bf16[128,1536]{1,0:T(8,128)(2,1)}) custom-call(bf16[128,1536]{1,0:T(8,128)(2,1)} %tokens.1, f32[1,1536]{1,0:T(1,128)} %broadcast_in_dim.130.gain, f32[128,1536]{1,0:T(8,128)} %attend.4.own, bf16[128,1536]{1,0:T(8,128)(2,1)} %copy-done.20, bf16[128,1536]{1,0:T(8,128)(2,1)} %copy-done.19), custom_call_target="tpu_custom_call" | custom-call | flops 1000000000 | bytes 3145728 | tf_op jit(solution)/shard_map/add_and_norm/pallas_call | solution.py:442
  94.4 4.8 %collective-permute-start.13 = (bf16[128,1536]{1,0:T(8,128)(2,1)}, bf16[128,1536]{1,0:T(8,128)(2,1)S(1)}, u32[]{:S(2)}, u32[]{:S(2)}) collective-permute-start(bf16[128,1536]{1,0:T(8,128)(2,1)} %get-tuple-element.45.refs_0_), channel_id=1, source_target_pairs={{0,8},{4,20},{8,0},{12,28},{16,24},{20,4},{24,16},{28,12},{1,9},{5... | collective-permute-start | bytes 1179656 | tf_op jit(solution)/shard_map/ppermute | solution.py:77
  99.2 2.1 %route_tables.1 = (s32[4,1024]{1,0:T(4,128)}, f32[4,1024]{1,0:T(4,128)}, s32[1024,8]{1,0:T(8,128)}) custom-call(s32[1]{0:T(128)} %bitcast.21.first_expert, bf16[2112,256]{1,0:T(8,128)(2,1)} %copy-done.5, bf16[2112,256]{1,0:T(8,128)(2,1)} %copy-done.11), custom_call_target="tpu_custom_call" | custom-call | flops 3000000000 | bytes 1000000 | tf_op jit(solution)/shard_map/route_tables/pallas_call | solution.py:673
  101.5 7.0 %collective-permute-done.13.refs_2_ = bf16[128,1536]{1,0:T(8,128)(2,1)S(1)} collective-permute-done((bf16[128,1536]{1,0:T(8,128)(2,1)}, bf16[128,1536]{1,0:T(8,128)(2,1)S(1)}, u32[]{:S(2)}, u32[]{:S(2)}) %collective-permute-start.13) | collective-permute-done | bytes 393248 | tf_op jit(solution)/shard_map/ppermute | solution.py:77
  109.2 1.8 %collective-permute-start.15 = (bf16[64,1536]{1,0:T(8,128)(2,1)S(1)}, bf16[64,1536]{1,0:T(8,128)(2,1)S(1)}, u32[]{:S(2)}, u32[]{:S(2)}) collective-permute-start(bf16[64,1536]{1,0:T(8,128)(2,1)S(1)} %slice.74), channel_id=1, source_target_pairs={{0,16},{4,12},{8,24},{12,4},{16,0},{20,28},{24,8},{28,20},{1,17},{... | collective-permute-start | bytes 589832 | tf_op jit(solution)/shard_map/ppermute | solution.py:82
  111.6 5.0 %collective-permute-done.15.refs_4_ = bf16[64,1536]{1,0:T(8,128)(2,1)S(1)} collective-permute-done((bf16[64,1536]{1,0:T(8,128)(2,1)S(1)}, bf16[64,1536]{1,0:T(8,128)(2,1)S(1)}, u32[]{:S(2)}, u32[]{:S(2)}) %collective-permute-start.15) | collective-permute-done | bytes 196640 | tf_op jit(solution)/shard_map/ppermute | solution.py:82
  117.2 0.9 collective-permute-done.20.refs_9_
  119.4 23.6 %experts.1 = (bf16[512,1536]{1,0:T(8,128)(2,1)}, bf16[384,1536]{1,0:T(8,128)(2,1)}, bf16[128,1536]{1,0:T(8,128)(2,1)}) custom-call(s32[4,1024]{1,0:T(4,128)} %get-tuple-element.42.slot_row, f32[4,1024]{1,0:T(4,128)} %get-tuple-element.43.gate_row, s32[1024,8]{1,0:T(8,128)} %get-tuple-element.44.slot_col, bf16[128,1536]{1,0:T(8,128)(2,1)} %get-tuple-element.45.refs_0_, ...), custom_call_target="tpu_custom_call" | custom-call | flops 12884901888 | bytes 25165824 | tf_op jit(solution)/shard_map/experts/pallas_call | solution.py:581
  143.6 1.4 collective-permute-done.22
  145.0 1.1 add_convert_fusion.3
  146.1 1.0 collective-permute-start.24
  147.1 0.9 collective-permute-start.23
  148.0 5.7 %collective-permute-done.24 = bf16[64,1536]{1,0:T(8,128)(2,1)S(1)} collective-permute-done((bf16[64,1536]{1,0:T(8,128)(2,1)S(1)}, bf16[64,1536]{1,0:T(8,128)(2,1)S(1)}, u32[]{:S(2)}, u32[]{:S(2)}) %collective-permute-start.24) | collective-permute-done | bytes 196640 | tf_op jit(solution)/shard_map/ppermute | solution.py:134
  153.9 1.4 collective-permute-start.25
  155.3 0.7 collective-permute-start.26
  156.0 9.7 %collective-permute-done.25 = bf16[128,1536]{1,0:T(8,128)(2,1)S(1)} collective-permute-done((bf16[128,1536]{1,0:T(8,128)(2,1)S(1)}, bf16[128,1536]{1,0:T(8,128)(2,1)S(1)}, u32[]{:S(2)}, u32[]{:S(2)}) %collective-permute-start.25) | collective-permute-done | bytes 393248 | tf_op jit(solution)/shard_map/ppermute | solution.py:145
  165.7 1.0 add_convert_fusion
  (120 shorter events, 13.0 us)
Async XLA Ops:
  0.0 14.4 %collective-permute-start = (bf16[128,1536]{1,0:T(8,128)(2,1)}, bf16[128,1536]{1,0:T(8,128)(2,1)S(1)}, u32[]{:S(2)}, u32[]{:S(2)}) collective-permute-start(bf16[128,1536]{1,0:T(8,128)(2,1)} %tokens.1), channel_id=1, source_target_pairs={{0,1},{1,2},{2,3},{3,0},{4,5},{5,6},{6,7},{7,4},{8,9},{9,10},{10,1... | collective-permute-start | bytes 1179656 | tf_op jit(solution)/shard_map/ppermute | solution.py:40
  5.9 24.2 %copy-start.9 = (s32[8]{0:T(128)}, s32[8]{0:T(128)S(1)}, u32[]{:S(2)}) copy-start(s32[8]{0:T(128)S(1)} %stack.44.refs_6_) | copy-start | bytes 100
  7.9 18.6 %copy-start.8 = (s32[4,8]{1,0:T(4,128)}, s32[4,8]{1,0:T(4,128)S(1)}, u32[]{:S(2)}) copy-start(s32[4,8]{1,0:T(4,128)S(1)} %get-tuple-element.76.refs_2_) | copy-start | bytes 388
  9.9 1.5 copy-start.2
  11.1 3.3 %copy-start.6 = (f32[1536]{0:T(1024)S(1)}, f32[1536]{0:T(1024)}, u32[]{:S(2)}) copy-start(f32[1536]{0:T(1024)} %param.22) | copy-start | bytes 18436
  14.4 12.1 %collective-permute-start.2 = (bf16[128,1536]{1,0:T(8,128)(2,1)S(1)}, bf16[128,1536]{1,0:T(8,128)(2,1)S(1)}, u32[]{:S(2)}, u32[]{:S(2)}) collective-permute-start(bf16[128,1536]{1,0:T(8,128)(2,1)S(1)} %collective-permute-done.refs_1_), channel_id=1, source_target_pairs={{0,1},{1,2},{2,3},{3,0},{4,5},{5,6},{6,7},{7,4},{8,9},{9,10},{10,1... | collective-permute-start | bytes 1179656 | tf_op jit(solution)/shard_map/ppermute | solution.py:40
  15.1 15.0 %copy-start.10 = (s32[8]{0:T(128)S(1)}, s32[8]{0:T(128)}, u32[]{:S(2)}) copy-start(s32[8]{0:T(128)} %param.20) | copy-start | bytes 100
  26.5 16.0 %copy-start.14 = (bf16[128,1536]{1,0:T(8,128)(2,1)}, bf16[128,1536]{1,0:T(8,128)(2,1)S(1)}, u32[]{:S(2)}) copy-start(bf16[128,1536]{1,0:T(8,128)(2,1)S(1)} %collective-permute-done.2.refs_0_) | copy-start | bytes 1179652
  26.5 13.6 %collective-permute-start.3 = (bf16[128,1536]{1,0:T(8,128)(2,1)S(1)}, bf16[128,1536]{1,0:T(8,128)(2,1)S(1)}, u32[]{:S(2)}, u32[]{:S(2)}) collective-permute-start(bf16[128,1536]{1,0:T(8,128)(2,1)S(1)} %collective-permute-done.2.refs_0_), channel_id=1, source_target_pairs={{0,1},{1,2},{2,3},{3,0},{4,5},{5,6},{6,7},{7,4},{8,9},{9,10},{10,1... | collective-permute-start | bytes 1179656 | tf_op jit(solution)/shard_map/ppermute | solution.py:40
  26.6 10.4 %collective-permute-start.7 = (bf16[528,256]{1,0:T(8,128)(2,1)S(1)}, bf16[528,256]{1,0:T(8,128)(2,1)S(1)}, u32[]{:S(2)}, u32[]{:S(2)}) collective-permute-start(bf16[528,256]{1,0:T(8,128)(2,1)S(1)} %maximum_maximum_fusion), channel_id=1, source_target_pairs={{0,24},{4,28},{8,16},{12,20},{16,8},{20,12},{24,0},{28,4},{1,25},{... | collective-permute-start | bytes 811016 | tf_op jit(solution)/shard_map/ppermute | solution.py:85
  28.8 10.8 %collective-permute-start.6 = (bf16[528,256]{1,0:T(8,128)(2,1)S(1)}, bf16[528,256]{1,0:T(8,128)(2,1)S(1)}, u32[]{:S(2)}, u32[]{:S(2)}) collective-permute-start(bf16[528,256]{1,0:T(8,128)(2,1)S(1)} %maximum_maximum_fusion), channel_id=1, source_target_pairs={{0,8},{4,20},{8,0},{12,28},{16,24},{20,4},{24,16},{28,12},{1,9},{5... | collective-permute-start | bytes 811016 | tf_op jit(solution)/shard_map/ppermute | solution.py:77
  29.3 10.7 %collective-permute-start.5 = (bf16[528,256]{1,0:T(8,128)(2,1)S(1)}, bf16[528,256]{1,0:T(8,128)(2,1)S(1)}, u32[]{:S(2)}, u32[]{:S(2)}) collective-permute-start(bf16[528,256]{1,0:T(8,128)(2,1)S(1)} %maximum_maximum_fusion), channel_id=1, source_target_pairs={{0,16},{4,12},{8,24},{12,4},{16,0},{20,28},{24,8},{28,20},{1,17},{... | collective-permute-start | bytes 811016 | tf_op jit(solution)/shard_map/ppermute | solution.py:76
  40.1 2.4 %copy-start.15 = (bf16[128,1536]{1,0:T(8,128)(2,1)}, bf16[128,1536]{1,0:T(8,128)(2,1)S(1)}, u32[]{:S(2)}) copy-start(bf16[128,1536]{1,0:T(8,128)(2,1)S(1)} %collective-permute-done.3.refs_1_) | copy-start | bytes 1179652
  40.1 2.4 %copy-start.25 = (bf16[256,256]{1,0:T(8,128)(2,1)S(1)}, bf16[256,256]{1,0:T(8,128)(2,1)}, u32[]{:S(2)}) copy-start(bf16[256,256]{1,0:T(8,128)(2,1)} %get-tuple-element.30.refs_12_) | copy-start | bytes 393220
  40.2 8.4 %copy-start.5 = (bf16[2112,256]{1,0:T(8,128)(2,1)}, bf16[2112,256]{1,0:T(8,128)(2,1)S(1)}, u32[]{:S(2)}) copy-start(bf16[2112,256]{1,0:T(8,128)(2,1)S(1)} %constant_dynamic-update-slice_fusion.refs_14_.refs_0_) | copy-start | bytes 3244036
  40.2 13.1 %collective-permute-start.8 = (bf16[2112,256]{1,0:T(8,128)(2,1)S(1)}, bf16[2112,256]{1,0:T(8,128)(2,1)S(1)}, u32[]{:S(2)}, u32[]{:S(2)}) collective-permute-start(bf16[2112,256]{1,0:T(8,128)(2,1)S(1)} %constant_dynamic-update-slice_fusion.refs_14_.refs_0_), channel_id=1, source_target_pairs={{0,4},{4,0},{8,12},{12,8},{16,20},{20,16},{24,28},{28,24},{1,5},{5... | collective-permute-start | bytes 3244040 | tf_op jit(solution)/shard_map/ppermute | solution.py:72
  42.4 10.8 %collective-permute-start.1 = (bf16[256,256]{1,0:T(8,128)(2,1)S(1)}, bf16[256,256]{1,0:T(8,128)(2,1)S(1)}, u32[]{:S(2)}, u32[]{:S(2)}) collective-permute-start(bf16[256,256]{1,0:T(8,128)(2,1)S(1)} %copy-done.25), channel_id=1, source_target_pairs={{0,4},{4,8},{8,12},{12,16},{16,20},{20,24},{24,28},{1,5},{5,9},{9,... | collective-permute-start | bytes 393224 | tf_op jit(solution)/shard_map/ppermute | solution.py:791
  44.7 7.3 %copy-start.7 = (f32[1536]{0:T(1024)S(1)}, f32[1536]{0:T(1024)}, u32[]{:S(2)}) copy-start(f32[1536]{0:T(1024)} %param.26) | copy-start | bytes 18436
  48.6 4.7 %collective-permute-start.4 = (bf16[256,256]{1,0:T(8,128)(2,1)}, bf16[256,256]{1,0:T(8,128)(2,1)S(1)}, u32[]{:S(2)}, u32[]{:S(2)}) collective-permute-start(bf16[256,256]{1,0:T(8,128)(2,1)} %get-tuple-element.32.refs_13_), channel_id=1, source_target_pairs={{0,4},{4,8},{8,12},{12,16},{16,20},{20,24},{24,28},{1,5},{5,9},{9,... | collective-permute-start | bytes 393224 | tf_op jit(solution)/shard_map/ppermute | solution.py:791
  53.3 1.1 copy-start.11
  59.4 16.5 %collective-permute-start.9 = (bf16[128,1536]{1,0:T(8,128)(2,1)}, bf16[128,1536]{1,0:T(8,128)(2,1)S(1)}, u32[]{:S(2)}, u32[]{:S(2)}) collective-permute-start(bf16[128,1536]{1,0:T(8,128)(2,1)} %attend.6), channel_id=1, source_target_pairs={{0,3},{1,0},{2,1},{3,2},{4,7},{5,4},{6,5},{7,6},{8,11},{9,8},{10,9... | collective-permute-start | bytes 1179656 | tf_op jit(solution)/shard_map/ppermute | solution.py:794
  69.9 17.4 %collective-permute-start.11 = (bf16[128,1536]{1,0:T(8,128)(2,1)}, bf16[128,1536]{1,0:T(8,128)(2,1)S(1)}, u32[]{:S(2)}, u32[]{:S(2)}) collective-permute-start(bf16[128,1536]{1,0:T(8,128)(2,1)} %attend.7), channel_id=1, source_target_pairs={{0,1},{1,2},{2,3},{3,0},{4,5},{5,6},{6,7},{7,4},{8,9},{9,10},{10,1... | collective-permute-start | bytes 1179656 | tf_op jit(solution)/shard_map/ppermute | solution.py:794
  77.0 13.9 %collective-permute-start.10 = (bf16[128,1536]{1,0:T(8,128)(2,1)S(1)}, bf16[128,1536]{1,0:T(8,128)(2,1)S(1)}, u32[]{:S(2)}, u32[]{:S(2)}) collective-permute-start(bf16[128,1536]{1,0:T(8,128)(2,1)S(1)} %add_convert_fusion.4), channel_id=1, source_target_pairs={{0,3},{1,0},{2,1},{3,2},{4,7},{5,4},{6,5},{7,6},{8,11},{9,8},{10,9... | collective-permute-start | bytes 1179656 | tf_op jit(solution)/shard_map/ppermute | solution.py:794
  87.3 3.6 %copy-start.19 = (bf16[128,1536]{1,0:T(8,128)(2,1)}, bf16[128,1536]{1,0:T(8,128)(2,1)S(1)}, u32[]{:S(2)}) copy-start(bf16[128,1536]{1,0:T(8,128)(2,1)S(1)} %collective-permute-done.11.refs_1_) | copy-start | bytes 1179652
  94.4 14.1 %collective-permute-start.13 = (bf16[128,1536]{1,0:T(8,128)(2,1)}, bf16[128,1536]{1,0:T(8,128)(2,1)S(1)}, u32[]{:S(2)}, u32[]{:S(2)}) collective-permute-start(bf16[128,1536]{1,0:T(8,128)(2,1)} %get-tuple-element.45.refs_0_), channel_id=1, source_target_pairs={{0,8},{4,20},{8,0},{12,28},{16,24},{20,4},{24,16},{28,12},{1,9},{5... | collective-permute-start | bytes 1179656 | tf_op jit(solution)/shard_map/ppermute | solution.py:77
  99.2 9.9 %collective-permute-start.12 = (bf16[128,1536]{1,0:T(8,128)(2,1)}, bf16[128,1536]{1,0:T(8,128)(2,1)S(1)}, u32[]{:S(2)}, u32[]{:S(2)}) collective-permute-start(bf16[128,1536]{1,0:T(8,128)(2,1)} %get-tuple-element.45.refs_0_), channel_id=1, source_target_pairs={{0,16},{4,12},{8,24},{12,4},{16,0},{20,28},{24,8},{28,20},{1,17},{... | collective-permute-start | bytes 1179656 | tf_op jit(solution)/shard_map/ppermute | solution.py:76
  99.2 2.1 %copy-start.13 = (bf16[128,1536]{1,0:T(8,128)(2,1)S(1)}, bf16[128,1536]{1,0:T(8,128)(2,1)}, u32[]{:S(2)}) copy-start(bf16[128,1536]{1,0:T(8,128)(2,1)} %get-tuple-element.45.refs_0_) | copy-start | bytes 1179652
  101.3 15.9 %collective-permute-start.16 = (bf16[128,1536]{1,0:T(8,128)(2,1)S(1)}, bf16[128,1536]{1,0:T(8,128)(2,1)S(1)}, u32[]{:S(2)}, u32[]{:S(2)}) collective-permute-start(bf16[128,1536]{1,0:T(8,128)(2,1)S(1)} %copy-done.13), channel_id=1, source_target_pairs={{0,4},{4,0},{8,12},{12,8},{16,20},{20,16},{24,28},{28,24},{1,5},{5... | collective-permute-start | bytes 1179656 | tf_op jit(solution)/shard_map/ppermute | solution.py:72
  108.5 9.9 %copy-start.3 = (bf16[128,1536]{1,0:T(8,128)(2,1)}, bf16[128,1536]{1,0:T(8,128)(2,1)S(1)}, u32[]{:S(2)}) copy-start(bf16[128,1536]{1,0:T(8,128)(2,1)S(1)} %collective-permute-done.13.refs_2_) | copy-start | bytes 1179652
  109.1 9.3 %copy-start.4 = (bf16[128,1536]{1,0:T(8,128)(2,1)}, bf16[128,1536]{1,0:T(8,128)(2,1)S(1)}, u32[]{:S(2)}) copy-start(bf16[128,1536]{1,0:T(8,128)(2,1)S(1)} %collective-permute-done.12.refs_1_) | copy-start | bytes 1179652
  109.2 7.5 %collective-permute-start.15 = (bf16[64,1536]{1,0:T(8,128)(2,1)S(1)}, bf16[64,1536]{1,0:T(8,128)(2,1)S(1)}, u32[]{:S(2)}, u32[]{:S(2)}) collective-permute-start(bf16[64,1536]{1,0:T(8,128)(2,1)S(1)} %slice.74), channel_id=1, source_target_pairs={{0,16},{4,12},{8,24},{12,4},{16,0},{20,28},{24,8},{28,20},{1,17},{... | collective-permute-start | bytes 589832 | tf_op jit(solution)/shard_map/ppermute | solution.py:82
  111.0 5.7 %collective-permute-start.14 = (bf16[64,1536]{1,0:T(8,128)(2,1)S(1)}, bf16[64,1536]{1,0:T(8,128)(2,1)S(1)}, u32[]{:S(2)}, u32[]{:S(2)}) collective-permute-start(bf16[64,1536]{1,0:T(8,128)(2,1)S(1)} %slice.73), channel_id=1, source_target_pairs={{0,8},{4,20},{8,0},{12,28},{16,24},{20,4},{24,16},{28,12},{1,9},{5... | collective-permute-start | bytes 589832 | tf_op jit(solution)/shard_map/ppermute | solution.py:81
  111.1 7.3 %collective-permute-start.17 = (bf16[128,1536]{1,0:T(8,128)(2,1)S(1)}, bf16[128,1536]{1,0:T(8,128)(2,1)S(1)}, u32[]{:S(2)}, u32[]{:S(2)}) collective-permute-start(bf16[128,1536]{1,0:T(8,128)(2,1)S(1)} %collective-permute-done.12.refs_1_), channel_id=1, source_target_pairs={{0,4},{4,0},{8,12},{12,8},{16,20},{20,16},{24,28},{28,24},{1,5},{5... | collective-permute-start | bytes 1179656 | tf_op jit(solution)/shard_map/ppermute | solution.py:72
  111.1 7.3 %collective-permute-start.18 = (bf16[128,1536]{1,0:T(8,128)(2,1)S(1)}, bf16[128,1536]{1,0:T(8,128)(2,1)S(1)}, u32[]{:S(2)}, u32[]{:S(2)}) collective-permute-start(bf16[128,1536]{1,0:T(8,128)(2,1)S(1)} %collective-permute-done.13.refs_2_), channel_id=1, source_target_pairs={{0,4},{4,0},{8,12},{12,8},{16,20},{20,16},{24,28},{28,24},{1,5},{5... | collective-permute-start | bytes 1179656 | tf_op jit(solution)/shard_map/ppermute | solution.py:72
  116.7 1.8 %copy-start.21 = (bf16[64,1536]{1,0:T(8,128)(2,1)}, bf16[64,1536]{1,0:T(8,128)(2,1)S(1)}, u32[]{:S(2)}) copy-start(bf16[64,1536]{1,0:T(8,128)(2,1)S(1)} %collective-permute-done.15.refs_4_) | copy-start | bytes 589828
  116.7 1.4 collective-permute-start.20
  116.7 1.7 %copy-start.22 = (bf16[64,1536]{1,0:T(8,128)(2,1)}, bf16[64,1536]{1,0:T(8,128)(2,1)S(1)}, u32[]{:S(2)}) copy-start(bf16[64,1536]{1,0:T(8,128)(2,1)S(1)} %collective-permute-done.14.refs_3_) | copy-start | bytes 589828
  116.7 1.7 %collective-permute-start.19 = (bf16[64,1536]{1,0:T(8,128)(2,1)S(1)}, bf16[64,1536]{1,0:T(8,128)(2,1)S(1)}, u32[]{:S(2)}, u32[]{:S(2)}) collective-permute-start(bf16[64,1536]{1,0:T(8,128)(2,1)S(1)} %collective-permute-done.14.refs_3_), channel_id=1, source_target_pairs={{0,4},{4,0},{8,12},{12,8},{16,20},{20,16},{24,28},{28,24},{1,5},{5... | collective-permute-start | bytes 589832 | tf_op jit(solution)/shard_map/ppermute | solution.py:72
  117.2 1.3 copy-start.16
  118.4 1.0 copy-start.18
  143.0 10.7 %copy-start = (bf16[512,1536]{1,0:T(8,128)(2,1)S(1)}, bf16[512,1536]{1,0:T(8,128)(2,1)}, u32[]{:S(2)}) copy-start(bf16[512,1536]{1,0:T(8,128)(2,1)} %get-tuple-element.51) | copy-start | bytes 4718596
  143.0 2.0 %collective-permute-start.22 = (bf16[128,1536]{1,0:T(8,128)(2,1)}, bf16[128,1536]{1,0:T(8,128)(2,1)S(1)}, u32[]{:S(2)}, u32[]{:S(2)}) collective-permute-start(bf16[128,1536]{1,0:T(8,128)(2,1)} %get-tuple-element.50), channel_id=1, source_target_pairs={{0,4},{4,0},{8,12},{12,8},{16,20},{20,16},{24,28},{28,24},{1,5},{5... | collective-permute-start | bytes 1179656 | tf_op jit(solution)/shard_map/ppermute | solution.py:130
  143.3 10.4 %collective-permute-start.21 = (bf16[384,1536]{1,0:T(8,128)(2,1)}, bf16[384,1536]{1,0:T(8,128)(2,1)S(1)}, u32[]{:S(2)}, u32[]{:S(2)}) collective-permute-start(bf16[384,1536]{1,0:T(8,128)(2,1)} %get-tuple-element.49), channel_id=1, source_target_pairs={{0,4},{4,0},{8,12},{12,8},{16,20},{20,16},{24,28},{28,24},{1,5},{5... | collective-permute-start | bytes 3538952 | tf_op jit(solution)/shard_map/ppermute | solution.py:131
  146.1 7.6 %collective-permute-start.24 = (bf16[64,1536]{1,0:T(8,128)(2,1)S(1)}, bf16[64,1536]{1,0:T(8,128)(2,1)S(1)}, u32[]{:S(2)}, u32[]{:S(2)}) collective-permute-start(bf16[64,1536]{1,0:T(8,128)(2,1)S(1)} %get-tuple-element.57), channel_id=1, source_target_pairs={{0,16},{4,12},{8,24},{12,4},{16,0},{20,28},{24,8},{28,20},{1,17},{... | collective-permute-start | bytes 589832 | tf_op jit(solution)/shard_map/ppermute | solution.py:134
  147.1 18.6 %copy-start.1 = (f32[128,1536]{1,0:T(8,128)S(1)}, f32[128,1536]{1,0:T(8,128)}, u32[]{:S(2)}) copy-start(f32[128,1536]{1,0:T(8,128)} %get-tuple-element.41) | copy-start | bytes 2359300
  147.1 6.6 %collective-permute-start.23 = (bf16[64,1536]{1,0:T(8,128)(2,1)S(1)}, bf16[64,1536]{1,0:T(8,128)(2,1)S(1)}, u32[]{:S(2)}, u32[]{:S(2)}) collective-permute-start(bf16[64,1536]{1,0:T(8,128)(2,1)S(1)} %get-tuple-element.58), channel_id=1, source_target_pairs={{0,8},{4,20},{8,0},{12,28},{16,24},{20,4},{24,16},{28,12},{1,9},{5... | collective-permute-start | bytes 589832 | tf_op jit(solution)/shard_map/ppermute | solution.py:133
  153.9 11.7 %collective-permute-start.25 = (bf16[128,1536]{1,0:T(8,128)(2,1)S(1)}, bf16[128,1536]{1,0:T(8,128)(2,1)S(1)}, u32[]{:S(2)}, u32[]{:S(2)}) collective-permute-start(bf16[128,1536]{1,0:T(8,128)(2,1)S(1)} %get-tuple-element.55), channel_id=1, source_target_pairs={{0,8},{4,20},{8,0},{12,28},{16,24},{20,4},{24,16},{28,12},{1,9},{5... | collective-permute-start | bytes 1179656 | tf_op jit(solution)/shard_map/ppermute | solution.py:145
  155.3 10.4 %collective-permute-start.26 = (bf16[128,1536]{1,0:T(8,128)(2,1)S(1)}, bf16[128,1536]{1,0:T(8,128)(2,1)S(1)}, u32[]{:S(2)}, u32[]{:S(2)}) collective-permute-start(bf16[128,1536]{1,0:T(8,128)(2,1)S(1)} %get-tuple-element.56), channel_id=1, source_target_pairs={{0,16},{4,12},{8,24},{12,4},{16,0},{20,28},{24,8},{28,20},{1,17},{... | collective-permute-start | bytes 1179656 | tf_op jit(solution)/shard_map/ppermute | solution.py:144
  (7 other events, 5.0 us)

commit v3 on v2

--- a/solution.py
+++ b/solution.py
@@ -60,36 +60,26 @@
     ).astype(jnp.int32)
 
 
-def plane_gather(block, split, joined, ties=(None, None, None)):
+def to_neighbours(block):
+    if lax.axis_size("tok") != 8:
+        return []
+    first, second, _ = cube_routes()
+    return [lax.ppermute(block, "tok", first), lax.ppermute(block, "tok", second)]
+
+
+def to_plane(block, neighbours, tie):
     count = lax.axis_size("tok")
     rows = block.shape[0]
     if count != 8:
         whole = lax.all_gather(block, "tok", axis=0, tiled=True)
         return [[(whole, i * rows, rows)] for i in range(count)]
-    first, second, partner = cube_routes()
-
-    def to_partner(array):
-        return lax.ppermute(array, "tok", partner)
-
-    block = after(block, ties[0])
-    half = rows // 2
-    one = lax.ppermute(block, "tok", first)
-    two = lax.ppermute(block, "tok", second)
-    one, two = after((one, two), ties[1])
-    if split:
-        three = [
-            lax.ppermute(one[:half], "tok", second),
-            lax.ppermute(two[half:], "tok", first),
-        ]
-    else:
-        three = [lax.ppermute(block, "tok", [(t, t ^ 6) for t in range(8)])]
-    if not joined:
-        mine = [[block], [one], [two], three]
-        every = mine + [[to_partner(piece) for piece in pieces] for pieces in mine]
-        return [[(piece, 0, piece.shape[0]) for piece in pieces] for pieces in every]
-    every = jnp.concatenate(after([block, one, two] + three, ties[2]), axis=0)
+    _, second, partner = cube_routes()
+    across = lax.ppermute(neighbours[0], "tok", second)
+    every = jnp.concatenate(after([block, *neighbours, across], tie), axis=0)
     return [
-        [(side, i * rows, rows)] for side in (every, to_partner(every)) for i in range(4)
+        [(side, i * rows, rows)]
+        for side in (every, lax.ppermute(every, "tok", partner))
+        for i in range(4)
     ]
 
 
@@ -121,10 +111,6 @@
 
 
 def plane_sum(near, far, last, rows):
-    count = lax.axis_size("tok")
-    if count != 8:
-        every = jnp.concatenate([near, far, last], axis=0)
-        return lax.psum_scatter(every, "tok", scatter_dimension=0, tiled=True).astype(F32)
     first, second, partner = cube_routes()
     half = rows // 2
     got_last = lax.ppermute(last, "tok", partner)
@@ -147,10 +133,10 @@
 
 
 def project_kernel(blocks, kv_local, q_local, *refs):
-    pieces = refs[:blocks]
-    gain, wq, wkv, cos, sin = refs[blocks : blocks + 5]
-    q_outs = refs[blocks + 5 : 2 * blocks + 5]
-    kv_out, normed = refs[2 * blocks + 5 :]
+    pieces = refs[: 2 * blocks]
+    gain, wq, wkv, cos, sin = refs[2 * blocks : 2 * blocks + 5]
+    q_outs = refs[2 * blocks + 5 : 3 * blocks + 5]
+    kv_out, normed = refs[3 * blocks + 5 :]
     half = pieces[0].shape[0]
     for i, piece in enumerate(pieces):
         wide = piece[...].astype(F32)
@@ -196,14 +182,14 @@
 
 
 def project(pieces, gain, w_query, w_keyval, cos, sin, kv_local, q_local):
-    blocks = len(pieces)
-    rows_dev, width = pieces[0].shape
+    blocks = len(pieces) // 2
+    rows_dev, width = 2 * pieces[0].shape[0], pieces[0].shape[1]
     share = q_local // kv_local
     outs = pl.pallas_call(
         functools.partial(project_kernel, blocks, kv_local, q_local),
         out_shape=[jax.ShapeDtypeStruct((kv_local, share * rows_dev, LANES), BF16)] * blocks
         + [jax.ShapeDtypeStruct((blocks * rows_dev, kv_local * LANES), BF16)],
-        in_specs=[vmem()] * (blocks + 5),
+        in_specs=[vmem()] * (2 * blocks + 5),
         out_specs=[vmem()] * (blocks + 1),
         scratch_shapes=[pltpu.VMEM((blocks * rows_dev, width), BF16)],
         compiler_params=params(),
@@ -455,12 +441,13 @@
     )(tokens, gain, own, *others)
 
 
-def expert_kernel(spec, rows, slot_row, gate_row, slot_col, *refs):
+def expert_kernel(spec, rows, layout, slot_row, gate_row, slot_col, *refs):
     count = len(spec)
-    many = len(refs) - 15
-    x_refs = refs[:many]
-    wg_ref, wu_ref, wd_ref, near, far, last = refs[many : many + 6]
-    x_all, wg, wu, wd, picked, answered, inner, x_sem, w_sem = refs[many + 6 :]
+    x_refs = refs[: -12 - len(layout)]
+    wg_ref, wu_ref, wd_ref = refs[-12 - len(layout) : -9 - len(layout)]
+    outs = refs[-9 - len(layout) : -9]
+    x_all, wg, wu, wd, picked, answered, inner, x_sem, w_sem = refs[-9:]
+    targets = [(out, i) for out, many in zip(outs, layout) for i in range(many)]
     exp_local = wg.shape[0]
     width = x_all.shape[1]
     span = 2 * rows
@@ -527,7 +514,9 @@
             [
                 jnp.sum(
                     jnp.where(
-                        pair_hits(e, b), gate_row[pl.ds(e, 1), b * span : (b + 1) * span], 0.0
+                        pair_hits(e, b),
+                        gate_row[pl.ds(e, 1), b * span : (b + 1) * span],
+                        0.0,
                     ),
                     axis=1,
                     keepdims=True,
@@ -559,17 +548,14 @@
             sums = jnp.dot(
                 spreader, answered[b, :, c : c + chunk], preferred_element_type=F32
             ).astype(BF16)
-            base = (b - pairs // 2) * span
-            if b < pairs // 2:
-                near[b * span : (b + 1) * span, c : c + chunk] = sums
-            elif b < pairs - 1:
-                far[base : base + span, c : c + chunk] = sums
-            else:
-                far[base : base + rows, c : c + chunk] = sums[:rows]
-                last[:, c : c + chunk] = sums[rows:]
-
-
-def experts(blocks, slot_row, gate_row, slot_col, w_gate, w_up, w_down):
+            for side in range(2):
+                out, at = targets[2 * b + side]
+                out[at * rows : (at + 1) * rows, c : c + chunk] = sums[
+                    side * rows : (side + 1) * rows
+                ]
+
+
+def experts(blocks, layout, route, w_gate, w_up, w_down):
     count = len(blocks)
     pieces, spec = flatten(blocks)
     parts = sum(len(one) for one in spec)
@@ -579,13 +565,13 @@
     slots = 2 * CAP
     work = exp_local * pairs * slots
     return pl.pallas_call(
-        functools.partial(expert_kernel, spec, rows),
+        functools.partial(expert_kernel, spec, rows, layout),
         out_shape=tuple(
             jax.ShapeDtypeStruct((many * rows, width), BF16)
-            for many in (count // 2, count // 2 - 1, 1)
+            for many in layout
         ),
         in_specs=[vmem()] * 3 + [ANY] * (len(pieces) + 3),
-        out_specs=(vmem(), vmem(), vmem()),
+        out_specs=(vmem(),) * len(layout),
         scratch_shapes=[
             pltpu.VMEM((count * rows, width), BF16),
             pltpu.VMEM(w_gate.shape, BF16),
@@ -604,7 +590,7 @@
             transcendentals=work * hidden,
         ),
         name="experts",
-    )(slot_row, gate_row, slot_col, *pieces, w_gate, w_up, w_down)
+    )(*route, *pieces, w_gate, w_up, w_down)
 
 
 def packed_routes(routes, route_gates, lanes):
@@ -720,9 +706,14 @@
     q_local = w_query.shape[1] // HS
     origins = plane_origins()
 
-    turns = [tokens]
+    half = rows_dev // 2
+    turns = [(tokens[:half], tokens[half:])]
+
+    def turn_on(tie):
+        turns.append(tuple(next_turn(after(part, tie), "head") for part in turns[-1]))
+
     for _ in range(groups // 2):
-        turns.append(next_turn(turns[-1], "head"))
+        turn_on(None)
 
     steps = jnp.arange(groups, dtype=jnp.int32)
     block_of = (me_head - steps) % groups
@@ -772,12 +763,18 @@
     missing = -w_query.shape[1] % LANES
     if missing:
         w_query = jnp.pad(w_query, ((0, 0), (0, missing)))
+    lanes = prefix_cache.shape[1]
+    packed = packed_routes(routes, route_gates, lanes)
+    prefix_rows = after(jnp.concatenate([prefix_cache, packed], axis=0), turns[1][0])
+    neighbours = to_neighbours(prefix_rows)
+
     queries, own, prev = [], [], []
     for some in (slice(0, groups // 2), slice(groups // 2, groups)):
         while len(turns) < some.stop:
-            turns.append(next_turn(after(turns[-1], own[0]), "head"))
+            turn_on((own[0], tables, info, neighbours))
+        pieces = [piece for parts in turns[some] for piece in parts]
         query, keyval = project(
-            turns[some],
+            after(pieces, prev[0]) if prev else pieces,
             attn_gain[None, :],
             w_query,
             w_keyval,
@@ -793,11 +790,7 @@
     def exchanged(block, j):
         return lax.ppermute(block, "head", [(i, (i - j) % groups) for i in range(groups)])
 
-    lanes = prefix_cache.shape[1]
-    packed = packed_routes(routes, route_gates, lanes)
-    cached = plane_gather(
-        jnp.concatenate([prefix_cache, packed], axis=0), False, True, [own[0], None, turns[-1]]
-    )
+    cached = to_plane(prefix_rows, neighbours, own[1])
 
     near = prev + own
 
@@ -819,8 +812,6 @@
             upper = exchanged(here, groups - 1)
     terms = [lower] if upper is None else [lower, upper]
     own_term = term(0, F32)
-    hidden, expert_in = add_and_norm(tokens, ffn_gain[None, :], own_term, terms)
-
     exp_local = w_gate.shape[0]
     route = route_tables(
         cached,
@@ -829,8 +820,35 @@
         (me_tok * exp_local).astype(jnp.int32).reshape(1),
         exp_local,
     )
-    blocks = plane_gather(expert_in, True, False, [None, route[0], None])
-    near, far, last = experts(blocks, *route, w_gate, w_up, w_down)
+    hidden, expert_in = add_and_norm(tokens, ffn_gain[None, :], own_term, after(terms, route))
+
+    def chosen(blocks, layout):
+        return experts(blocks, layout, route, w_gate, w_up, w_down)
+
+    if tok_count != 8:
+        every = lax.all_gather(expert_in, "tok", axis=0, tiled=True)
+        blocks = [[(every, k * rows_dev, rows_dev)] for k in range(tok_count)]
+        (sums,) = chosen(blocks, (tok_count,))
+        summed = lax.psum_scatter(sums, "tok", scatter_dimension=0, tiled=True).astype(F32)
+        return (hidden + summed).astype(BF16)
+
+    first, second, partner = cube_routes()
+
+    def to_partner(array):
+        return lax.ppermute(array, "tok", partner)
+
+    one = lax.ppermute(expert_in, "tok", first)
+    two = lax.ppermute(expert_in, "tok", second)
+    three = [
+        lax.ppermute(one[:half], "tok", second),
+        lax.ppermute(two[half:], "tok", first),
+    ]
+    mine = [[expert_in], [one], [two], three]
+    blocks = [
+        [(piece, 0, piece.shape[0]) for piece in pieces]
+        for pieces in mine + [[to_partner(piece) for piece in pieces] for pieces in mine]
+    ]
+    near, far, last = chosen(blocks, (4, 3, 1))
     return (hidden + plane_sum(near, far, last, rows_dev)).astype(BF16)
 
 

time: 166 us -> 167 us (level)
  waiting for transfers between devices: 52.6 us -> 48 us
  Pallas kernels: 60.1 us -> 63.7 us
  local copies, waits for them, and re-layouts: 7.7 us -> 10.7 us
    ppermute x7 -> x8, waiting for transfers between devices: 21.3 us -> 11.7 us  [the longest x1 7.83 us: local(): two = lax.ppermute(expert_in, 'tok', second)]
    ppermute x3, starting transfers between devices: 7.74 us -> 3.63 us  [exchanged(): lax.ppermute(block, 'head', [(i, (i - j) % groups) for i in range(groups)])]
    ppermute x3 -> x6, starting transfers between devices: 3.03 us -> 6.62 us  [next_turn(): lax.ppermute(block, axis, [(i, (i + 1) % count) for i in range(count)])]
    ppermute x3 -> x6, waiting for transfers between devices: 9.79 us -> 13.3 us  [next_turn(): lax.ppermute(block, axis, [(i, (i + 1) % count) for i in range(count)])]
    pallas_call x4, Pallas kernels: 24.1 us -> 27.5 us  [attend(): pl.pallas_call(functools.partial(attend_kernel, block, len(near), slab_sp...]
    unnamed x59 -> x67, local copies, waits for them, and re-layouts: 2.88 us -> 4.89 us
    ppermute x2, starting transfers between devices: 5.03 us -> 3.21 us  [local(): lax.ppermute(keyval, 'tok', [(i, i + 1) for i in range(tok_count - 1)])]
    ppermute x7 -> x8, starting transfers between devices: 10.3 us -> 11.8 us  [the longest x1 2.35 us: local(): lax.ppermute(two[half:], 'tok', first)]
  transfers between devices with their start and end apart: 27 -> 30, of which waited for: 14 -> 14; matrix products, arithmetic and copies ran while one was open for 10% -> 10% of each run, Pallas kernels for 17% -> 19%
where the time goes in v3:
time: 167 us
  Pallas kernels  63.7 us (38%)
  waiting for transfers between devices  48 us (29%)
  starting transfers between devices  30.3 us (18%)
  other arithmetic  13.6 us (8%)
  local copies, waits for them, and re-layouts  10.7 us (6%)
    pallas_call x4, Pallas kernels, attend(): pl.pallas_call(functools.partial(attend_kernel, block, len(near), slab_sp...  27.5 us
    pallas_call x1, Pallas kernels, experts(): pl.pallas_call(functools.partial(expert_kernel, spec, rows, layout), out_...  23.6 us
    ppermute x6, waiting for transfers between devices, next_turn(): lax.ppermute(block, axis, [(i, (i + 1) % count) for i in range(count)])  13.3 us
    ppermute x1, waiting for transfers between devices, plane_sum(): beside = lax.ppermute((pair(2) + add_lower).astype(BF16), 'tok', second)  9.54 us
    ppermute x1, waiting for transfers between devices, local(): two = lax.ppermute(expert_in, 'tok', second)  7.83 us
    pallas_call x2, Pallas kernels, project(): pl.pallas_call(functools.partial(project_kernel, blocks, kv_local, q_loca...  7.79 us
    ppermute x6, starting transfers between devices, next_turn(): lax.ppermute(block, axis, [(i, (i + 1) % count) for i in range(count)])  6.62 us
    ppermute x1, waiting for transfers between devices, plane_sum(): across_lower = lax.ppermute(three[half:], 'tok', first)  5.34 us
  transfers between devices with their start and end apart: 30, of which 14 were waited for; matrix products, arithmetic and copies ran while one was open for 10% of the time, Pallas kernels for 19%

profile of v3, /device:TPU:0, one launch (start us, length us, event | category | flops | bytes accessed | tf_op | source)
XLA Modules:
  0.0 166.7 jit_solution(17017974919975520015)
XLA Ops:
  0.0 1.1 fusion.8
  1.1 3.1 %collective-permute-start.1 = (bf16[64,1536]{1,0:T(8,128)(2,1)S(1)}, bf16[64,1536]{1,0:T(8,128)(2,1)S(1)}, u32[]{:S(2)}, u32[]{:S(2)}) collective-permute-start(bf16[64,1536]{1,0:T(8,128)(2,1)S(1)} %get-tuple-element.69.refs_1_), channel_id=1, source_target_pairs={{0,1},{1,2},{2,3},{3,0},{4,5},{5,6},{6,7},{7,4},{8,9},{9,10},{10,1... | collective-permute-start | bytes 589832 | tf_op jit(solution)/shard_map/ppermute | solution.py:40
  4.2 1.6 collective-permute-start
  6.5 0.9 convert_reduce_fusion
  7.5 0.8 dynamic-slice_bitcast_fusion
  8.3 1.4 select_reduce_fusion.6.refs_5_
  9.7 0.8 select_reduce_fusion.7
  10.9 0.7 select_reduce_fusion.2
  14.8 1.0 fusion
  16.3 0.7 fusion.10
  19.4 1.5 collective-permute-start.6
  20.9 1.5 collective-permute-start.5
  22.4 1.6 collective-permute-start.3
  24.7 3.9 %norm_project_rotate.2 = (bf16[2,384,128]{2,1,0:T(8,128)(2,1)}, bf16[2,384,128]{2,1,0:T(8,128)(2,1)}, bf16[256,256]{1,0:T(8,128)(2,1)}) custom-call(bf16[64,1536]{1,0:T(8,128)(2,1)} %copy-done.4, bf16[64,1536]{1,0:T(8,128)(2,1)} %copy-done.3, bf16[64,1536]{1,0:T(8,128)(2,1)} %copy-done.19, bf16[64,1536]{1,0:T(8,128)(2,1)} %copy-done.20, ...), custom_call_target="tpu_custom_call" | custom-call | flops 4000000000 | bytes 4000000 | tf_op jit(solution)/shard_map/norm_project_rotate/pallas_call | solution.py:188
  28.6 5.4 %collective-permute-done.4.refs_1_ = bf16[64,1536]{1,0:T(8,128)(2,1)S(1)} collective-permute-done((bf16[64,1536]{1,0:T(8,128)(2,1)S(1)}, bf16[64,1536]{1,0:T(8,128)(2,1)S(1)}, u32[]{:S(2)}, u32[]{:S(2)}) %collective-permute-start.4) | collective-permute-done | bytes 196640 | tf_op jit(solution)/shard_map/ppermute | solution.py:40
  34.1 1.3 collective-permute-start.2
  35.4 1.2 collective-permute-start.10
  36.7 5.9 %collective-permute-done.7.refs_2_ = bf16[64,1536]{1,0:T(8,128)(2,1)S(1)} collective-permute-done((bf16[64,1536]{1,0:T(8,128)(2,1)S(1)}, bf16[64,1536]{1,0:T(8,128)(2,1)S(1)}, u32[]{:S(2)}, u32[]{:S(2)}) %collective-permute-start.7) | collective-permute-done | bytes 196640 | tf_op jit(solution)/shard_map/ppermute | solution.py:40
  42.5 2.1 %collective-permute-done.8.refs_3_ = bf16[64,1536]{1,0:T(8,128)(2,1)S(1)} collective-permute-done((bf16[64,1536]{1,0:T(8,128)(2,1)S(1)}, bf16[64,1536]{1,0:T(8,128)(2,1)S(1)}, u32[]{:S(2)}, u32[]{:S(2)}) %collective-permute-start.8) | collective-permute-done | bytes 196640 | tf_op jit(solution)/shard_map/ppermute | solution.py:40
  45.3 3.9 %norm_project_rotate.3 = (bf16[2,384,128]{2,1,0:T(8,128)(2,1)}, bf16[2,384,128]{2,1,0:T(8,128)(2,1)}, bf16[256,256]{1,0:T(8,128)(2,1)}) custom-call(bf16[64,1536]{1,0:T(8,128)(2,1)} %copy-done.21, bf16[64,1536]{1,0:T(8,128)(2,1)} %copy-done.23, bf16[64,1536]{1,0:T(8,128)(2,1)} %copy-done.26, bf16[64,1536]{1,0:T(8,128)(2,1)} %copy-done.28, ...), custom_call_target="tpu_custom_call" | custom-call | flops 4000000000 | bytes 4000000 | tf_op jit(solution)/shard_map/norm_project_rotate/pallas_call | solution.py:188
  50.5 1.9 %collective-permute-start.9 = (bf16[256,256]{1,0:T(8,128)(2,1)S(1)}, bf16[256,256]{1,0:T(8,128)(2,1)S(1)}, u32[]{:S(2)}, u32[]{:S(2)}) collective-permute-start(bf16[256,256]{1,0:T(8,128)(2,1)S(1)} %copy-done.30), channel_id=1, source_target_pairs={{0,4},{4,8},{8,12},{12,16},{16,20},{20,24},{24,28},{1,5},{5,9},{9,... | collective-permute-start | bytes 393224 | tf_op jit(solution)/shard_map/ppermute | solution.py:788
  54.4 5.8 %attend.6 = bf16[128,1536]{1,0:T(8,128)(2,1)} custom-call(s32[4,5]{1,0:T(4,128)} %fusion.5.refs_0_, s32[4]{0:T(128)} %compare_convert_fusion.refs_1_, s32[4,8]{1,0:T(4,128)} %copy-done.10, s32[4,8]{1,0:T(4,128)} %select_reduce_fusion.3.refs_3_, s32[4]{0:T(128)} %convert_reduce_fusion.1.refs_4_, s32[8]{0:T(128)} %select_reduce_fusion.6.refs_5_, s32[8]{0:T(128)} %copy-done.12, ...), custom_call_target="tpu_custom_call" | custom-call | flops 8000000000 | bytes 4000000 | tf_op jit(solution)/shard_map/attend/pallas_call | solution.py:373
  60.3 5.2 %attend.7 = bf16[128,1536]{1,0:T(8,128)(2,1)} custom-call(s32[4,5]{1,0:T(4,128)} %fusion.5.refs_0_, s32[4]{0:T(128)} %compare_convert_fusion.refs_1_, s32[4,8]{1,0:T(4,128)} %copy-done.10, s32[4,8]{1,0:T(4,128)} %select_reduce_fusion.3.refs_3_, s32[4]{0:T(128)} %convert_reduce_fusion.1.refs_4_, s32[8]{0:T(128)} %select_reduce_fusion.6.refs_5_, s32[8]{0:T(128)} %copy-done.12, ...), custom_call_target="tpu_custom_call" | custom-call | flops 8000000000 | bytes 4000000 | tf_op jit(solution)/shard_map/attend/pallas_call | solution.py:373
  65.5 3.5 %collective-permute-start.14 = (bf16[128,1536]{1,0:T(8,128)(2,1)}, bf16[128,1536]{1,0:T(8,128)(2,1)S(1)}, u32[]{:S(2)}, u32[]{:S(2)}) collective-permute-start(bf16[128,1536]{1,0:T(8,128)(2,1)} %attend.7), channel_id=1, source_target_pairs={{0,1},{1,2},{2,3},{3,0},{4,5},{5,6},{6,7},{7,4},{8,9},{9,10},{10,1... | collective-permute-start | bytes 1179656 | tf_op jit(solution)/shard_map/ppermute | solution.py:791
  69.0 10.3 %attend.5 = bf16[128,1536]{1,0:T(8,128)(2,1)} custom-call(s32[4,5]{1,0:T(4,128)} %fusion.5.refs_0_, s32[4]{0:T(128)} %compare_convert_fusion.refs_1_, s32[4,8]{1,0:T(4,128)} %copy-done.10, s32[4,8]{1,0:T(4,128)} %select_reduce_fusion.3.refs_3_, s32[4]{0:T(128)} %convert_reduce_fusion.1.refs_4_, s32[8]{0:T(128)} %select_reduce_fusion.6.refs_5_, s32[8]{0:T(128)} %copy-done.12, ...), custom_call_target="tpu_custom_call" | custom-call | flops 8000000000 | bytes 4000000 | tf_op jit(solution)/shard_map/attend/pallas_call | solution.py:373
  79.4 1.4 collective-permute-done.12
  80.8 1.1 add_convert_fusion.4
  81.9 6.2 %attend.4.own = f32[128,1536]{1,0:T(8,128)} custom-call(s32[4,5]{1,0:T(4,128)} %fusion.5.refs_0_, s32[4]{0:T(128)} %compare_convert_fusion.refs_1_, s32[4,8]{1,0:T(4,128)} %copy-done.10, s32[4,8]{1,0:T(4,128)} %select_reduce_fusion.3.refs_3_, s32[4]{0:T(128)} %convert_reduce_fusion.1.refs_4_, s32[8]{0:T(128)} %select_reduce_fusion.6.refs_5_, s32[8]{0:T(128)} %copy-done.12, ...), custom_call_target="tpu_custom_call" | custom-call | flops 8000000000 | bytes 4000000 | tf_op jit(solution)/shard_map/attend/pallas_call | solution.py:373
  88.2 2.1 %route_tables.1 = (s32[4,1024]{1,0:T(4,128)}, f32[4,1024]{1,0:T(4,128)}, s32[1024,8]{1,0:T(8,128)}) custom-call(s32[1]{0:T(128)} %bitcast.21.first_expert, bf16[2112,256]{1,0:T(8,128)(2,1)} %copy-done.7, bf16[2112,256]{1,0:T(8,128)(2,1)} %copy-done.13), custom_call_target="tpu_custom_call" | custom-call | flops 3000000000 | bytes 1000000 | tf_op jit(solution)/shard_map/route_tables/pallas_call | solution.py:659
  90.2 3.5 %collective-permute-done.13.refs_0_ = bf16[128,1536]{1,0:T(8,128)(2,1)S(1)} collective-permute-done((bf16[128,1536]{1,0:T(8,128)(2,1)S(1)}, bf16[128,1536]{1,0:T(8,128)(2,1)S(1)}, u32[]{:S(2)}, u32[]{:S(2)}) %collective-permute-start.13) | collective-permute-done | bytes 393248 | tf_op jit(solution)/shard_map/ppermute | solution.py:791
  93.7 0.7 copy-done.18
  94.5 2.7 %add_and_norm.1 = (f32[128,1536]{1,0:T(8,128)}, bf16[128,1536]{1,0:T(8,128)(2,1)}) custom-call(bf16[128,1536]{1,0:T(8,128)(2,1)} %tokens.1, f32[1,1536]{1,0:T(1,128)} %broadcast_in_dim.130.gain, f32[128,1536]{1,0:T(8,128)} %attend.4.own, bf16[128,1536]{1,0:T(8,128)(2,1)} %copy-done.18, bf16[128,1536]{1,0:T(8,128)(2,1)} %copy-done.15), custom_call_target="tpu_custom_call" | custom-call | flops 1000000000 | bytes 3145728 | tf_op jit(solution)/shard_map/add_and_norm/pallas_call | solution.py:428
  97.2 1.9 %collective-permute-start.16 = (bf16[128,1536]{1,0:T(8,128)(2,1)}, bf16[128,1536]{1,0:T(8,128)(2,1)S(1)}, u32[]{:S(2)}, u32[]{:S(2)}) collective-permute-start(bf16[128,1536]{1,0:T(8,128)(2,1)} %get-tuple-element.57.refs_0_), channel_id=1, source_target_pairs={{0,8},{4,20},{8,0},{12,28},{16,24},{20,4},{24,16},{28,12},{1,9},{5... | collective-permute-start | bytes 1179656 | tf_op jit(solution)/shard_map/ppermute | solution.py:841
  99.1 2.0 %collective-permute-start.15 = (bf16[128,1536]{1,0:T(8,128)(2,1)}, bf16[128,1536]{1,0:T(8,128)(2,1)S(1)}, u32[]{:S(2)}, u32[]{:S(2)}) collective-permute-start(bf16[128,1536]{1,0:T(8,128)(2,1)} %get-tuple-element.57.refs_0_), channel_id=1, source_target_pairs={{0,16},{4,12},{8,24},{12,4},{16,0},{20,28},{24,8},{28,20},{1,17},{... | collective-permute-start | bytes 1179656 | tf_op jit(solution)/shard_map/ppermute | solution.py:840
  101.1 7.8 %collective-permute-done.16.refs_2_ = bf16[128,1536]{1,0:T(8,128)(2,1)S(1)} collective-permute-done((bf16[128,1536]{1,0:T(8,128)(2,1)}, bf16[128,1536]{1,0:T(8,128)(2,1)S(1)}, u32[]{:S(2)}, u32[]{:S(2)}) %collective-permute-start.16) | collective-permute-done | bytes 393248 | tf_op jit(solution)/shard_map/ppermute | solution.py:841
  108.9 2.4 %collective-permute-start.18 = (bf16[64,1536]{1,0:T(8,128)(2,1)S(1)}, bf16[64,1536]{1,0:T(8,128)(2,1)S(1)}, u32[]{:S(2)}, u32[]{:S(2)}) collective-permute-start(bf16[64,1536]{1,0:T(8,128)(2,1)S(1)} %slice.101), channel_id=1, source_target_pairs={{0,16},{4,12},{8,24},{12,4},{16,0},{20,28},{24,8},{28,20},{1,17},{... | collective-permute-start | bytes 589832 | tf_op jit(solution)/shard_map/ppermute | solution.py:844
  111.3 1.3 collective-permute-start.17
  113.1 3.3 %collective-permute-done.18.refs_4_ = bf16[64,1536]{1,0:T(8,128)(2,1)S(1)} collective-permute-done((bf16[64,1536]{1,0:T(8,128)(2,1)S(1)}, bf16[64,1536]{1,0:T(8,128)(2,1)S(1)}, u32[]{:S(2)}, u32[]{:S(2)}) %collective-permute-start.18) | collective-permute-done | bytes 196640 | tf_op jit(solution)/shard_map/ppermute | solution.py:844
  117.0 0.8 collective-permute-done.23.refs_9_
  119.1 0.8 copy-done.17
  119.9 23.6 %experts.1 = (bf16[512,1536]{1,0:T(8,128)(2,1)}, bf16[384,1536]{1,0:T(8,128)(2,1)}, bf16[128,1536]{1,0:T(8,128)(2,1)}) custom-call(s32[4,1024]{1,0:T(4,128)} %get-tuple-element.51.slot_row, f32[4,1024]{1,0:T(4,128)} %get-tuple-element.52.gate_row, s32[1024,8]{1,0:T(8,128)} %get-tuple-element.53.slot_col, bf16[128,1536]{1,0:T(8,128)(2,1)} %get-tuple-element.57.refs_0_, ...), custom_call_target="tpu_custom_call" | custom-call | flops 12884901888 | bytes 25165824 | tf_op jit(solution)/shard_map/experts/pallas_call | solution.py:567
  144.1 1.4 collective-permute-done.25
  145.5 1.1 add_convert_fusion.3
  146.9 1.9 %collective-permute-start.26 = (bf16[64,1536]{1,0:T(8,128)(2,1)S(1)}, bf16[64,1536]{1,0:T(8,128)(2,1)S(1)}, u32[]{:S(2)}, u32[]{:S(2)}) collective-permute-start(bf16[64,1536]{1,0:T(8,128)(2,1)S(1)} %get-tuple-element.68), channel_id=1, source_target_pairs={{0,8},{4,20},{8,0},{12,28},{16,24},{20,4},{24,16},{28,12},{1,9},{5... | collective-permute-start | bytes 589832 | tf_op jit(solution)/shard_map/ppermute | solution.py:119
  148.8 5.3 %collective-permute-done.27 = bf16[64,1536]{1,0:T(8,128)(2,1)S(1)} collective-permute-done((bf16[64,1536]{1,0:T(8,128)(2,1)S(1)}, bf16[64,1536]{1,0:T(8,128)(2,1)S(1)}, u32[]{:S(2)}, u32[]{:S(2)}) %collective-permute-start.27) | collective-permute-done | bytes 196640 | tf_op jit(solution)/shard_map/ppermute | solution.py:120
  154.4 1.3 collective-permute-start.28
  156.1 9.5 %collective-permute-done.28 = bf16[128,1536]{1,0:T(8,128)(2,1)S(1)} collective-permute-done((bf16[128,1536]{1,0:T(8,128)(2,1)S(1)}, bf16[128,1536]{1,0:T(8,128)(2,1)S(1)}, u32[]{:S(2)}, u32[]{:S(2)}) %collective-permute-start.28) | collective-permute-done | bytes 393248 | tf_op jit(solution)/shard_map/ppermute | solution.py:131
  165.7 1.0 add_convert_fusion
  (135 shorter events, 16.1 us)
Async XLA Ops:
  0.0 13.8 %copy-start.8 = (f32[1536]{0:T(1024)S(1)}, f32[1536]{0:T(1024)}, u32[]{:S(2)}) copy-start(f32[1536]{0:T(1024)} %param.22) | copy-start | bytes 18436
  0.0 14.4 %copy-start.11 = (f32[128,8]{0,1:T(8,128)S(1)}, f32[128,8]{0,1:T(8,128)}, u32[]{:S(2)}) copy-start(f32[128,8]{0,1:T(8,128)} %param.28) | copy-start | bytes 12292
  1.1 15.2 %copy-start.3 = (bf16[64,1536]{1,0:T(8,128)(2,1)}, bf16[64,1536]{1,0:T(8,128)(2,1)S(1)}, u32[]{:S(2)}) copy-start(bf16[64,1536]{1,0:T(8,128)(2,1)S(1)} %get-tuple-element.69.refs_1_) | copy-start | bytes 589828
  1.1 15.2 %copy-start.4 = (bf16[64,1536]{1,0:T(8,128)(2,1)}, bf16[64,1536]{1,0:T(8,128)(2,1)S(1)}, u32[]{:S(2)}) copy-start(bf16[64,1536]{1,0:T(8,128)(2,1)S(1)} %get-tuple-element.70.refs_0_) | copy-start | bytes 589828
  1.1 22.9 %collective-permute-start.1 = (bf16[64,1536]{1,0:T(8,128)(2,1)S(1)}, bf16[64,1536]{1,0:T(8,128)(2,1)S(1)}, u32[]{:S(2)}, u32[]{:S(2)}) collective-permute-start(bf16[64,1536]{1,0:T(8,128)(2,1)S(1)} %get-tuple-element.69.refs_1_), channel_id=1, source_target_pairs={{0,1},{1,2},{2,3},{3,0},{4,5},{5,6},{6,7},{7,4},{8,9},{9,10},{10,1... | collective-permute-start | bytes 589832 | tf_op jit(solution)/shard_map/ppermute | solution.py:40
  4.2 15.2 %collective-permute-start = (bf16[64,1536]{1,0:T(8,128)(2,1)S(1)}, bf16[64,1536]{1,0:T(8,128)(2,1)S(1)}, u32[]{:S(2)}, u32[]{:S(2)}) collective-permute-start(bf16[64,1536]{1,0:T(8,128)(2,1)S(1)} %get-tuple-element.70.refs_0_), channel_id=1, source_target_pairs={{0,1},{1,2},{2,3},{3,0},{4,5},{5,6},{6,7},{7,4},{8,9},{9,10},{10,1... | collective-permute-start | bytes 589832 | tf_op jit(solution)/shard_map/ppermute | solution.py:40
  8.3 7.9 %copy-start.12 = (s32[8]{0:T(128)}, s32[8]{0:T(128)S(1)}, u32[]{:S(2)}) copy-start(s32[8]{0:T(128)S(1)} %stack.44.refs_6_) | copy-start | bytes 100
  12.3 5.5 %copy-start.10 = (s32[4,8]{1,0:T(4,128)}, s32[4,8]{1,0:T(4,128)S(1)}, u32[]{:S(2)}) copy-start(s32[4,8]{1,0:T(4,128)S(1)} %get-tuple-element.88.refs_2_) | copy-start | bytes 388
  16.3 2.5 %copy-start.2 = (bf16[512,256]{1,0:T(8,128)(2,1)S(1)}, bf16[512,256]{1,0:T(8,128)(2,1)}, u32[]{:S(2)}) copy-start(bf16[512,256]{1,0:T(8,128)(2,1)} %param.21) | copy-start | bytes 786436
  19.4 4.8 %copy-start.19 = (bf16[64,1536]{1,0:T(8,128)(2,1)}, bf16[64,1536]{1,0:T(8,128)(2,1)S(1)}, u32[]{:S(2)}) copy-start(bf16[64,1536]{1,0:T(8,128)(2,1)S(1)} %collective-permute-done.refs_2_) | copy-start | bytes 589828
  19.4 14.6 %collective-permute-start.6 = (bf16[528,256]{1,0:T(8,128)(2,1)S(1)}, bf16[528,256]{1,0:T(8,128)(2,1)S(1)}, u32[]{:S(2)}, u32[]{:S(2)}) collective-permute-start(bf16[528,256]{1,0:T(8,128)(2,1)S(1)} %maximum_maximum_fusion), channel_id=1, source_target_pairs={{0,8},{4,20},{8,0},{12,28},{16,24},{20,4},{24,16},{28,12},{1,9},{5... | collective-permute-start | bytes 811016 | tf_op jit(solution)/shard_map/ppermute | solution.py:67
  20.9 13.1 %collective-permute-start.5 = (bf16[528,256]{1,0:T(8,128)(2,1)S(1)}, bf16[528,256]{1,0:T(8,128)(2,1)S(1)}, u32[]{:S(2)}, u32[]{:S(2)}) collective-permute-start(bf16[528,256]{1,0:T(8,128)(2,1)S(1)} %maximum_maximum_fusion), channel_id=1, source_target_pairs={{0,16},{4,12},{8,24},{12,4},{16,0},{20,28},{24,8},{28,20},{1,17},{... | collective-permute-start | bytes 811016 | tf_op jit(solution)/shard_map/ppermute | solution.py:67
  22.4 11.5 %collective-permute-start.3 = (bf16[64,1536]{1,0:T(8,128)(2,1)S(1)}, bf16[64,1536]{1,0:T(8,128)(2,1)S(1)}, u32[]{:S(2)}, u32[]{:S(2)}) collective-permute-start(bf16[64,1536]{1,0:T(8,128)(2,1)S(1)} %collective-permute-done.refs_2_), channel_id=1, source_target_pairs={{0,1},{1,2},{2,3},{3,0},{4,5},{5,6},{6,7},{7,4},{8,9},{9,10},{10,1... | collective-permute-start | bytes 589832 | tf_op jit(solution)/shard_map/ppermute | solution.py:40
  24.0 10.0 %collective-permute-start.4 = (bf16[64,1536]{1,0:T(8,128)(2,1)S(1)}, bf16[64,1536]{1,0:T(8,128)(2,1)S(1)}, u32[]{:S(2)}, u32[]{:S(2)}) collective-permute-start(bf16[64,1536]{1,0:T(8,128)(2,1)S(1)} %collective-permute-done.1.refs_3_), channel_id=1, source_target_pairs={{0,1},{1,2},{2,3},{3,0},{4,5},{5,6},{6,7},{7,4},{8,9},{9,10},{10,1... | collective-permute-start | bytes 589832 | tf_op jit(solution)/shard_map/ppermute | solution.py:40
  33.9 10.7 %copy-start.23 = (bf16[64,1536]{1,0:T(8,128)(2,1)}, bf16[64,1536]{1,0:T(8,128)(2,1)S(1)}, u32[]{:S(2)}) copy-start(bf16[64,1536]{1,0:T(8,128)(2,1)S(1)} %collective-permute-done.4.refs_1_) | copy-start | bytes 589828
  34.0 10.7 %copy-start.21 = (bf16[64,1536]{1,0:T(8,128)(2,1)}, bf16[64,1536]{1,0:T(8,128)(2,1)S(1)}, u32[]{:S(2)}) copy-start(bf16[64,1536]{1,0:T(8,128)(2,1)S(1)} %collective-permute-done.3.refs_0_) | copy-start | bytes 589828
  34.0 8.6 %collective-permute-start.7 = (bf16[64,1536]{1,0:T(8,128)(2,1)S(1)}, bf16[64,1536]{1,0:T(8,128)(2,1)S(1)}, u32[]{:S(2)}, u32[]{:S(2)}) collective-permute-start(bf16[64,1536]{1,0:T(8,128)(2,1)S(1)} %collective-permute-done.3.refs_0_), channel_id=1, source_target_pairs={{0,1},{1,2},{2,3},{3,0},{4,5},{5,6},{6,7},{7,4},{8,9},{9,10},{10,1... | collective-permute-start | bytes 589832 | tf_op jit(solution)/shard_map/ppermute | solution.py:40
  34.0 10.6 %collective-permute-start.8 = (bf16[64,1536]{1,0:T(8,128)(2,1)S(1)}, bf16[64,1536]{1,0:T(8,128)(2,1)S(1)}, u32[]{:S(2)}, u32[]{:S(2)}) collective-permute-start(bf16[64,1536]{1,0:T(8,128)(2,1)S(1)} %collective-permute-done.4.refs_1_), channel_id=1, source_target_pairs={{0,1},{1,2},{2,3},{3,0},{4,5},{5,6},{6,7},{7,4},{8,9},{9,10},{10,1... | collective-permute-start | bytes 589832 | tf_op jit(solution)/shard_map/ppermute | solution.py:40
  34.1 2.5 %collective-permute-start.2 = (bf16[256,256]{1,0:T(8,128)(2,1)}, bf16[256,256]{1,0:T(8,128)(2,1)S(1)}, u32[]{:S(2)}, u32[]{:S(2)}) collective-permute-start(bf16[256,256]{1,0:T(8,128)(2,1)} %get-tuple-element.35.refs_12_), channel_id=1, source_target_pairs={{0,4},{4,8},{8,12},{12,16},{16,20},{20,24},{24,28},{1,5},{5,9},{9,... | collective-permute-start | bytes 393224 | tf_op jit(solution)/shard_map/ppermute | solution.py:788
  35.4 13.8 %collective-permute-start.10 = (bf16[528,256]{1,0:T(8,128)(2,1)S(1)}, bf16[528,256]{1,0:T(8,128)(2,1)S(1)}, u32[]{:S(2)}, u32[]{:S(2)}) collective-permute-start(bf16[528,256]{1,0:T(8,128)(2,1)S(1)} %collective-permute-done.5), channel_id=1, source_target_pairs={{0,8},{4,20},{8,0},{12,28},{16,24},{20,4},{24,16},{28,12},{1,9},{5... | collective-permute-start | bytes 811016 | tf_op jit(solution)/shard_map/ppermute | solution.py:77
  36.7 12.5 %copy-start.29 = (bf16[256,256]{1,0:T(8,128)(2,1)}, bf16[256,256]{1,0:T(8,128)(2,1)S(1)}, u32[]{:S(2)}) copy-start(bf16[256,256]{1,0:T(8,128)(2,1)S(1)} %collective-permute-done.2.refs_10_) | copy-start | bytes 393220
  42.5 2.1 %copy-start.26 = (bf16[64,1536]{1,0:T(8,128)(2,1)}, bf16[64,1536]{1,0:T(8,128)(2,1)S(1)}, u32[]{:S(2)}) copy-start(bf16[64,1536]{1,0:T(8,128)(2,1)S(1)} %collective-permute-done.7.refs_2_) | copy-start | bytes 589828
  49.3 4.1 %copy-start.7 = (bf16[2112,256]{1,0:T(8,128)(2,1)}, bf16[2112,256]{1,0:T(8,128)(2,1)S(1)}, u32[]{:S(2)}) copy-start(bf16[2112,256]{1,0:T(8,128)(2,1)S(1)} %constant_dynamic-update-slice_fusion.refs_14_.refs_0_) | copy-start | bytes 3244036
  49.3 4.1 %collective-permute-start.11 = (bf16[2112,256]{1,0:T(8,128)(2,1)S(1)}, bf16[2112,256]{1,0:T(8,128)(2,1)S(1)}, u32[]{:S(2)}, u32[]{:S(2)}) collective-permute-start(bf16[2112,256]{1,0:T(8,128)(2,1)S(1)} %constant_dynamic-update-slice_fusion.refs_14_.refs_0_), channel_id=1, source_target_pairs={{0,4},{4,0},{8,12},{12,8},{16,20},{20,16},{24,28},{28,24},{1,5},{5... | collective-permute-start | bytes 3244040 | tf_op jit(solution)/shard_map/ppermute | solution.py:81
  50.5 2.9 %collective-permute-start.9 = (bf16[256,256]{1,0:T(8,128)(2,1)S(1)}, bf16[256,256]{1,0:T(8,128)(2,1)S(1)}, u32[]{:S(2)}, u32[]{:S(2)}) collective-permute-start(bf16[256,256]{1,0:T(8,128)(2,1)S(1)} %copy-done.30), channel_id=1, source_target_pairs={{0,4},{4,8},{8,12},{12,16},{16,20},{20,24},{24,28},{1,5},{5,9},{9,... | collective-permute-start | bytes 393224 | tf_op jit(solution)/shard_map/ppermute | solution.py:788
  60.3 20.5 %collective-permute-start.12 = (bf16[128,1536]{1,0:T(8,128)(2,1)}, bf16[128,1536]{1,0:T(8,128)(2,1)S(1)}, u32[]{:S(2)}, u32[]{:S(2)}) collective-permute-start(bf16[128,1536]{1,0:T(8,128)(2,1)} %attend.6), channel_id=1, source_target_pairs={{0,3},{1,0},{2,1},{3,2},{4,7},{5,4},{6,5},{7,6},{8,11},{9,8},{10,9... | collective-permute-start | bytes 1179656 | tf_op jit(solution)/shard_map/ppermute | solution.py:791
  65.5 24.7 %collective-permute-start.14 = (bf16[128,1536]{1,0:T(8,128)(2,1)}, bf16[128,1536]{1,0:T(8,128)(2,1)S(1)}, u32[]{:S(2)}, u32[]{:S(2)}) collective-permute-start(bf16[128,1536]{1,0:T(8,128)(2,1)} %attend.7), channel_id=1, source_target_pairs={{0,1},{1,2},{2,3},{3,0},{4,5},{5,6},{6,7},{7,4},{8,9},{9,10},{10,1... | collective-permute-start | bytes 1179656 | tf_op jit(solution)/shard_map/ppermute | solution.py:791
  81.9 11.8 %collective-permute-start.13 = (bf16[128,1536]{1,0:T(8,128)(2,1)S(1)}, bf16[128,1536]{1,0:T(8,128)(2,1)S(1)}, u32[]{:S(2)}, u32[]{:S(2)}) collective-permute-start(bf16[128,1536]{1,0:T(8,128)(2,1)S(1)} %add_convert_fusion.4), channel_id=1, source_target_pairs={{0,3},{1,0},{2,1},{3,2},{4,7},{5,4},{6,5},{7,6},{8,11},{9,8},{10,9... | collective-permute-start | bytes 1179656 | tf_op jit(solution)/shard_map/ppermute | solution.py:791
  90.2 3.5 %copy-start.15 = (bf16[128,1536]{1,0:T(8,128)(2,1)}, bf16[128,1536]{1,0:T(8,128)(2,1)S(1)}, u32[]{:S(2)}) copy-start(bf16[128,1536]{1,0:T(8,128)(2,1)S(1)} %collective-permute-done.14.refs_1_) | copy-start | bytes 1179652
  97.2 11.7 %collective-permute-start.16 = (bf16[128,1536]{1,0:T(8,128)(2,1)}, bf16[128,1536]{1,0:T(8,128)(2,1)S(1)}, u32[]{:S(2)}, u32[]{:S(2)}) collective-permute-start(bf16[128,1536]{1,0:T(8,128)(2,1)} %get-tuple-element.57.refs_0_), channel_id=1, source_target_pairs={{0,8},{4,20},{8,0},{12,28},{16,24},{20,4},{24,16},{28,12},{1,9},{5... | collective-permute-start | bytes 1179656 | tf_op jit(solution)/shard_map/ppermute | solution.py:841
  99.1 12.2 %collective-permute-start.15 = (bf16[128,1536]{1,0:T(8,128)(2,1)}, bf16[128,1536]{1,0:T(8,128)(2,1)S(1)}, u32[]{:S(2)}, u32[]{:S(2)}) collective-permute-start(bf16[128,1536]{1,0:T(8,128)(2,1)} %get-tuple-element.57.refs_0_), channel_id=1, source_target_pairs={{0,16},{4,12},{8,24},{12,4},{16,0},{20,28},{24,8},{28,20},{1,17},{... | collective-permute-start | bytes 1179656 | tf_op jit(solution)/shard_map/ppermute | solution.py:840
  101.1 16.0 %collective-permute-start.19 = (bf16[128,1536]{1,0:T(8,128)(2,1)}, bf16[128,1536]{1,0:T(8,128)(2,1)S(1)}, u32[]{:S(2)}, u32[]{:S(2)}) collective-permute-start(bf16[128,1536]{1,0:T(8,128)(2,1)} %get-tuple-element.57.refs_0_), channel_id=1, source_target_pairs={{0,4},{4,0},{8,12},{12,8},{16,20},{20,16},{24,28},{28,24},{1,5},{5... | collective-permute-start | bytes 1179656 | tf_op jit(solution)/shard_map/ppermute | solution.py:838
  108.9 9.6 %copy-start.5 = (bf16[128,1536]{1,0:T(8,128)(2,1)}, bf16[128,1536]{1,0:T(8,128)(2,1)S(1)}, u32[]{:S(2)}) copy-start(bf16[128,1536]{1,0:T(8,128)(2,1)S(1)} %collective-permute-done.16.refs_2_) | copy-start | bytes 1179652
  108.9 7.5 %collective-permute-start.18 = (bf16[64,1536]{1,0:T(8,128)(2,1)S(1)}, bf16[64,1536]{1,0:T(8,128)(2,1)S(1)}, u32[]{:S(2)}, u32[]{:S(2)}) collective-permute-start(bf16[64,1536]{1,0:T(8,128)(2,1)S(1)} %slice.101), channel_id=1, source_target_pairs={{0,16},{4,12},{8,24},{12,4},{16,0},{20,28},{24,8},{28,20},{1,17},{... | collective-permute-start | bytes 589832 | tf_op jit(solution)/shard_map/ppermute | solution.py:844
  111.3 7.2 %copy-start.6 = (bf16[128,1536]{1,0:T(8,128)(2,1)}, bf16[128,1536]{1,0:T(8,128)(2,1)S(1)}, u32[]{:S(2)}) copy-start(bf16[128,1536]{1,0:T(8,128)(2,1)S(1)} %collective-permute-done.15.refs_1_) | copy-start | bytes 1179652
  111.3 5.7 %collective-permute-start.17 = (bf16[64,1536]{1,0:T(8,128)(2,1)S(1)}, bf16[64,1536]{1,0:T(8,128)(2,1)S(1)}, u32[]{:S(2)}, u32[]{:S(2)}) collective-permute-start(bf16[64,1536]{1,0:T(8,128)(2,1)S(1)} %slice.100), channel_id=1, source_target_pairs={{0,8},{4,20},{8,0},{12,28},{16,24},{20,4},{24,16},{28,12},{1,9},{5... | collective-permute-start | bytes 589832 | tf_op jit(solution)/shard_map/ppermute | solution.py:843
  112.6 5.2 %collective-permute-start.21 = (bf16[128,1536]{1,0:T(8,128)(2,1)S(1)}, bf16[128,1536]{1,0:T(8,128)(2,1)S(1)}, u32[]{:S(2)}, u32[]{:S(2)}) collective-permute-start(bf16[128,1536]{1,0:T(8,128)(2,1)S(1)} %collective-permute-done.16.refs_2_), channel_id=1, source_target_pairs={{0,4},{4,0},{8,12},{12,8},{16,20},{20,16},{24,28},{28,24},{1,5},{5... | collective-permute-start | bytes 1179656 | tf_op jit(solution)/shard_map/ppermute | solution.py:838
  112.6 5.9 %collective-permute-start.20 = (bf16[128,1536]{1,0:T(8,128)(2,1)S(1)}, bf16[128,1536]{1,0:T(8,128)(2,1)S(1)}, u32[]{:S(2)}, u32[]{:S(2)}) collective-permute-start(bf16[128,1536]{1,0:T(8,128)(2,1)S(1)} %collective-permute-done.15.refs_1_), channel_id=1, source_target_pairs={{0,4},{4,0},{8,12},{12,8},{16,20},{20,16},{24,28},{28,24},{1,5},{5... | collective-permute-start | bytes 1179656 | tf_op jit(solution)/shard_map/ppermute | solution.py:838
  116.4 1.4 collective-permute-start.23
  117.0 1.4 collective-permute-start.22
  143.5 10.7 %copy-start = (bf16[512,1536]{1,0:T(8,128)(2,1)S(1)}, bf16[512,1536]{1,0:T(8,128)(2,1)}, u32[]{:S(2)}) copy-start(bf16[512,1536]{1,0:T(8,128)(2,1)} %get-tuple-element.61) | copy-start | bytes 4718596
  143.5 2.0 %collective-permute-start.25 = (bf16[128,1536]{1,0:T(8,128)(2,1)}, bf16[128,1536]{1,0:T(8,128)(2,1)S(1)}, u32[]{:S(2)}, u32[]{:S(2)}) collective-permute-start(bf16[128,1536]{1,0:T(8,128)(2,1)} %get-tuple-element.60), channel_id=1, source_target_pairs={{0,4},{4,0},{8,12},{12,8},{16,20},{20,16},{24,28},{28,24},{1,5},{5... | collective-permute-start | bytes 1179656 | tf_op jit(solution)/shard_map/ppermute | solution.py:116
  143.7 10.5 %collective-permute-start.24 = (bf16[384,1536]{1,0:T(8,128)(2,1)}, bf16[384,1536]{1,0:T(8,128)(2,1)S(1)}, u32[]{:S(2)}, u32[]{:S(2)}) collective-permute-start(bf16[384,1536]{1,0:T(8,128)(2,1)} %get-tuple-element.59), channel_id=1, source_target_pairs={{0,4},{4,0},{8,12},{12,8},{16,20},{20,16},{24,28},{28,24},{1,5},{5... | collective-permute-start | bytes 3538952 | tf_op jit(solution)/shard_map/ppermute | solution.py:117
  146.6 7.5 %collective-permute-start.27 = (bf16[64,1536]{1,0:T(8,128)(2,1)S(1)}, bf16[64,1536]{1,0:T(8,128)(2,1)S(1)}, u32[]{:S(2)}, u32[]{:S(2)}) collective-permute-start(bf16[64,1536]{1,0:T(8,128)(2,1)S(1)} %get-tuple-element.67), channel_id=1, source_target_pairs={{0,16},{4,12},{8,24},{12,4},{16,0},{20,28},{24,8},{28,20},{1,17},{... | collective-permute-start | bytes 589832 | tf_op jit(solution)/shard_map/ppermute | solution.py:120
  146.9 18.8 %copy-start.1 = (f32[128,1536]{1,0:T(8,128)S(1)}, f32[128,1536]{1,0:T(8,128)}, u32[]{:S(2)}) copy-start(f32[128,1536]{1,0:T(8,128)} %get-tuple-element.56) | copy-start | bytes 2359300
  146.9 7.3 %collective-permute-start.26 = (bf16[64,1536]{1,0:T(8,128)(2,1)S(1)}, bf16[64,1536]{1,0:T(8,128)(2,1)S(1)}, u32[]{:S(2)}, u32[]{:S(2)}) collective-permute-start(bf16[64,1536]{1,0:T(8,128)(2,1)S(1)} %get-tuple-element.68), channel_id=1, source_target_pairs={{0,8},{4,20},{8,0},{12,28},{16,24},{20,4},{24,16},{28,12},{1,9},{5... | collective-permute-start | bytes 589832 | tf_op jit(solution)/shard_map/ppermute | solution.py:119
  154.4 11.3 %collective-permute-start.28 = (bf16[128,1536]{1,0:T(8,128)(2,1)S(1)}, bf16[128,1536]{1,0:T(8,128)(2,1)S(1)}, u32[]{:S(2)}, u32[]{:S(2)}) collective-permute-start(bf16[128,1536]{1,0:T(8,128)(2,1)S(1)} %get-tuple-element.65), channel_id=1, source_target_pairs={{0,8},{4,20},{8,0},{12,28},{16,24},{20,4},{24,16},{28,12},{1,9},{5... | collective-permute-start | bytes 1179656 | tf_op jit(solution)/shard_map/ppermute | solution.py:131
  155.7 10.0 %collective-permute-start.29 = (bf16[128,1536]{1,0:T(8,128)(2,1)S(1)}, bf16[128,1536]{1,0:T(8,128)(2,1)S(1)}, u32[]{:S(2)}, u32[]{:S(2)}) collective-permute-start(bf16[128,1536]{1,0:T(8,128)(2,1)S(1)} %get-tuple-element.66), channel_id=1, source_target_pairs={{0,16},{4,12},{8,24},{12,4},{16,0},{20,28},{24,8},{28,20},{1,17},{... | collective-permute-start | bytes 1179656 | tf_op jit(solution)/shard_map/ppermute | solution.py:130
  (14 other events, 13.7 us)

commit v4 on v3

--- a/solution.py
+++ b/solution.py
@@ -28,11 +28,6 @@
 
 def params(**more):
     return pltpu.CompilerParams(vmem_limit_bytes=VMEM_BYTES, **more)
-
-
-def lookup(table, index):
-    entries = jnp.arange(table.shape[0], dtype=jnp.int32)
-    return jnp.sum(jnp.where(index[..., None] == entries, table, 0), axis=-1)
 
 
 def next_turn(block, axis):
@@ -132,11 +127,86 @@
     return pair(0) + beside.astype(F32) + along.astype(F32)
 
 
+BEGIN, PLACE, BLOCK = 120, 121, 122
+
+
+def table_kernel(groups, me, owner_of, fill_of, group_ids, inverse, segs, *outs):
+    cosines, sines, info, marks = outs[:2], outs[2:4], outs[4], outs[5]
+    ids = group_ids[...]
+    owner = jnp.zeros(ids.shape, F32)
+    fill = jnp.zeros(ids.shape, F32)
+    for g in range(owner_of.shape[0]):
+        owner = jnp.where(ids == g, owner_of[g].astype(F32), owner)
+        fill = jnp.where(ids == g, fill_of[owner_of[g]].astype(F32), fill)
+    square = (LANES, LANES)
+    row = lax.broadcasted_iota(jnp.int32, square, 0)
+    lane = lax.broadcasted_iota(jnp.int32, square, 1)
+    request = lax.broadcasted_iota(jnp.int32, (LANES, ids.shape[1]), 1).astype(F32)
+    sign = jnp.where(lane % HS < HS // 2, -1.0, 1.0)
+    many = segs.shape[0]
+    for j in range(groups):
+        block = lax.rem(me[1] - j + groups, groups)
+        which = me[0] * groups + block
+        here = segs[pl.ds(which, 1), :].astype(F32)
+        own = jnp.sum(jnp.where(row == lane, here, 0.0), axis=1, keepdims=True)
+        wide = jnp.broadcast_to(own, square)
+        earlier = jnp.zeros(square, F32)
+        for u in range(many):
+            earlier += jnp.where(segs[u : u + 1, :].astype(F32) < wide, 1.0, 0.0)
+        begin = jnp.sum(earlier, axis=1, keepdims=True)
+        match = own == request
+        slab = jnp.sum(jnp.where(match, owner, 0.0), axis=1, keepdims=True)
+        start = jnp.sum(jnp.where(match, fill, 0.0), axis=1, keepdims=True)
+        first = which * LANES
+        place = (first + row).astype(F32)
+        angles = (start + place - begin) * inverse[...]
+        side, at = (0, j) if j < groups // 2 else (1, j - groups // 2)
+        cosines[side][at * LANES : (at + 1) * LANES, :] = jnp.cos(angles)
+        sines[side][at * LANES : (at + 1) * LANES, :] = jnp.sin(angles) * sign
+        slab_wide = jnp.broadcast_to(slab, square).astype(jnp.int32)
+        begin_wide = jnp.broadcast_to(begin, square)
+        info[j, 0] = slab_wide
+        info[j, 1] = begin_wide.astype(jnp.int32)
+        read = jnp.max(jnp.where(slab_wide == lane, 1.0, 0.0), axis=0, keepdims=True)
+        lowest = jnp.min(begin_wide, axis=0, keepdims=True)
+        spot = lane[:1]
+        line = jnp.where(spot == BEGIN, lowest, read).astype(jnp.int32)
+        line = jnp.where(spot == PLACE, first, line)
+        marks[j : j + 1, :] = jnp.where(spot == BLOCK, block, line)
+
+
+def row_tables(groups, me, prefix_owner, slab_fill, group_ids, inverse, segments):
+    half = jax.ShapeDtypeStruct((groups // 2 * LANES, LANES), F32)
+    outs = pl.pallas_call(
+        functools.partial(table_kernel, groups),
+        out_shape=(half,) * 4
+        + (
+            jax.ShapeDtypeStruct((groups, 2, LANES, LANES), jnp.int32),
+            jax.ShapeDtypeStruct((groups, LANES), jnp.int32),
+        ),
+        in_specs=[SMEM] * 3 + [vmem()] * 3,
+        out_specs=(vmem(),) * 6,
+        compiler_params=params(),
+        cost_estimate=pl.CostEstimate(
+            flops=4 * 10**9, bytes_accessed=10**6, transcendentals=10**5
+        ),
+        name="row_tables",
+    )(
+        me,
+        prefix_owner,
+        slab_fill,
+        group_ids.reshape(1, -1),
+        inverse.reshape(1, LANES),
+        segments.reshape(-1, LANES),
+    )
+    return outs[:2], outs[2:4], outs[4], outs[5]
+
+
 def project_kernel(blocks, kv_local, q_local, *refs):
-    pieces = refs[: 2 * blocks]
-    gain, wq, wkv, cos, sin = refs[2 * blocks : 2 * blocks + 5]
-    q_outs = refs[2 * blocks + 5 : 3 * blocks + 5]
-    kv_out, normed = refs[3 * blocks + 5 :]
+    pieces = refs[:blocks]
+    gain, wq, wkv, cos, sin = refs[blocks : blocks + 5]
+    q_outs = refs[blocks + 5 : 2 * blocks + 5]
+    kv_out, normed = refs[2 * blocks + 5 :]
     half = pieces[0].shape[0]
     for i, piece in enumerate(pieces):
         wide = piece[...].astype(F32)
@@ -182,14 +252,14 @@
 
 
 def project(pieces, gain, w_query, w_keyval, cos, sin, kv_local, q_local):
-    blocks = len(pieces) // 2
-    rows_dev, width = 2 * pieces[0].shape[0], pieces[0].shape[1]
+    blocks = len(pieces)
+    rows_dev, width = pieces[0].shape
     share = q_local // kv_local
     outs = pl.pallas_call(
         functools.partial(project_kernel, blocks, kv_local, q_local),
         out_shape=[jax.ShapeDtypeStruct((kv_local, share * rows_dev, LANES), BF16)] * blocks
         + [jax.ShapeDtypeStruct((blocks * rows_dev, kv_local * LANES), BF16)],
-        in_specs=[vmem()] * (2 * blocks + 5),
+        in_specs=[vmem()] * (blocks + 5),
         out_specs=[vmem()] * (blocks + 1),
         scratch_shapes=[pltpu.VMEM((blocks * rows_dev, width), BF16)],
         compiler_params=params(),
@@ -197,21 +267,20 @@
             flops=4 * 10**9, bytes_accessed=4 * 10**6, transcendentals=blocks * rows_dev
         ),
         name="norm_project_rotate",
-    )(*pieces, gain, w_query, w_keyval, cos.reshape(-1, LANES), sin.reshape(-1, LANES))
+    )(*pieces, gain, w_query, w_keyval, cos, sin)
     return list(outs[:-1]), outs[-1]
 
 
 def attend_kernel(block, near_parts, slab_spec, q_local, *refs):
-    near_list, reach, read, slab_list, slab_count, fill, slab_id, place = refs[:8]
-    info, query = refs[8:10]
-    near_refs = refs[10 : 10 + near_parts]
-    slab_refs = refs[10 + near_parts : -16]
-    w_ref, out = refs[-16:-14]
-    near, far, scores, peak, total, accum, begin, owner, heads, mixed, w_all = refs[-14:-3]
-    near_sems, slab_sems, w_sem = refs[-3:]
-    parts = near_list.shape[0]
+    marks, slab_id, fill_of, query, info = refs[:5]
+    near_refs = refs[5 : 5 + near_parts]
+    slab_refs = refs[5 + near_parts : -18]
+    w_ref, out = refs[-18:-16]
+    near, far, scores, peak, total, accum, begin, owner, heads, mixed, w_all, held = refs[-16:-4]
+    near_sems, slab_sems, w_sem, info_sem = refs[-4:]
+    parts = info.shape[0]
     kv_local, stack, _ = query.shape
-    rows_dev = info.shape[0]
+    rows_dev = info.shape[2]
     share = stack // rows_dev
     cuts = PREFIX // LANES
     window = parts + 1
@@ -236,7 +305,7 @@
 
     def each_slab(act):
         for i, [(array, start, _)] in enumerate(slab_spec):
-            @pl.when(read[block, i] != 0)
+            @pl.when(marks[block, slab_id[i]] != 0)
             def _(i=i, array=array, start=start):
                 for g in range(kv_local):
                     act(
@@ -248,20 +317,22 @@
                     )
 
     w_copy = pltpu.make_async_copy(w_ref, w_all, w_sem)
+    info_copy = pltpu.make_async_copy(info.at[block], held, info_sem)
+    info_copy.start()
     for copy in copies:
         copy.start()
     each_slab(lambda copy: copy.start())
     w_copy.start()
-    for ref, column in ((owner, 0), (begin, 1)):
-        tall = jnp.concatenate([info[:, column : column + 1]] * share, axis=0)
-        ref[...] = jnp.broadcast_to(tall, wide)
+    info_copy.wait()
+    for ref, kind in ((owner, 0), (begin, 1)):
+        ref[...] = jnp.concatenate([held[kind]] * share, axis=0)
     row = lax.broadcasted_iota(jnp.int32, wide, 0)
     order = row - lax.div(row, rows_dev) * rows_dev
     for copy in copies:
         copy.wait()
 
     def rows_near(g, back):
-        unit = near_list[block, back]
+        unit = lax.rem(block + back, parts) + jnp.where(marks[block, BLOCK] >= back, parts, 0)
         return near[g, pl.ds(pl.multiple_of(unit * rows_dev, rows_dev), rows_dev), :]
 
     def rows_window(g, backs):
@@ -280,7 +351,7 @@
             every = score(g, rows_window(g, backs))
             top = None if opening else peak[g]
             for at, back in enumerate(backs):
-                there = place[near_list[block, back]] + lane
+                there = marks[block, PLACE] - back * rows_dev + lane
                 seen = there >= begin[...]
                 if back == 0:
                     seen = seen & (lane <= order)
@@ -298,7 +369,7 @@
             for c in range(cuts):
                 here = every[:, c * LANES : (c + 1) * LANES]
                 if (c + 1) * LANES > PREFIX // 2:
-                    here = jnp.where(lane + c * LANES < fill[slab], here, NEG_FILL)
+                    here = jnp.where(lane + c * LANES < fill_of[slab_id[slab]], here, NEG_FILL)
                 scores[g, window + slab * cuts + c] = here
                 top = here if top is None else jnp.maximum(top, here)
             old = peak[g]
@@ -331,16 +402,18 @@
     def sweep(near_body, far_body, between=None):
         near_body((0, 1), True)
 
-        @pl.when(reach[block] != 0)
+        @pl.when(marks[block, BEGIN] < marks[block, PLACE] - rows_dev)
         def _():
             near_body(tuple(range(2, window)), False)
 
         if between is not None:
             between()
 
-        @pl.loop(0, slab_count[block])
-        def _(turn):
-            far_body(slab_list[block, turn])
+        @pl.loop(0, len(slab_spec))
+        def _(slab):
+            @pl.when(marks[block, slab_id[slab]] != 0)
+            def _():
+                far_body(slab)
 
     sweep(near_scores, far_scores, lambda: each_slab(lambda copy: copy.wait()))
     for g in range(kv_local):
@@ -363,17 +436,17 @@
     out[...] = jnp.dot(mixed[...], w_all[...], preferred_element_type=F32).astype(out.dtype)
 
 
-def attend(block, tables, info, query, near, slabs, w_out, q_local, held_as):
+def attend(block, marks, origins, slab_fill, info, query, near, slabs, w_out, q_local, held_as):
     parts = info.shape[0]
     kv_local, stack, _ = query.shape
-    rows_dev = info.shape[1]
+    rows_dev = info.shape[2]
     units = parts + 1 + len(slabs) * (PREFIX // LANES)
     wide = (stack, LANES)
     arrays, slab_spec = flatten(slabs)
     return pl.pallas_call(
         functools.partial(attend_kernel, block, len(near), slab_spec, q_local),
         out_shape=jax.ShapeDtypeStruct((rows_dev, w_out.shape[1]), held_as),
-        in_specs=[SMEM] * 8 + [vmem()] * 2 + [ANY] * (len(near) + len(arrays) + 1),
+        in_specs=[SMEM] * 3 + [vmem()] + [ANY] * (len(near) + len(arrays) + 2),
         out_specs=vmem(),
         scratch_shapes=[
             pltpu.VMEM((kv_local, 2 * parts * rows_dev, LANES), BF16),
@@ -387,8 +460,10 @@
             pltpu.VMEM((q_local, rows_dev, LANES), F32),
             pltpu.VMEM((rows_dev, q_local * HS), BF16),
             pltpu.VMEM(w_out.shape, BF16),
+            pltpu.VMEM(info.shape[1:], jnp.int32),
             pltpu.SemaphoreType.DMA((len(near), kv_local)),
             pltpu.SemaphoreType.DMA((len(slabs), kv_local)),
+            pltpu.SemaphoreType.DMA,
             pltpu.SemaphoreType.DMA,
         ],
         compiler_params=params(),
@@ -397,16 +472,11 @@
         ),
         name="attend",
     )(
-        tables["near_list"],
-        tables["reach"],
-        tables["read"],
-        tables["slab_list"],
-        tables["slab_count"],
-        tables["fill"],
-        tables["slab_id"],
-        tables["place"],
-        info[block],
+        marks,
+        origins,
+        slab_fill,
         query,
+        info,
         *near,
         *arrays,
         w_out,
@@ -700,86 +770,51 @@
     me_tok = lax.axis_index("tok")
     me_head = lax.axis_index("head")
     rows_dev, width = tokens.shape
-    row_len = rows_dev * groups
-    row_first = me_tok * row_len
     kv_local = w_keyval.shape[1] // (2 * HS)
     q_local = w_query.shape[1] // HS
     origins = plane_origins()
 
-    half = rows_dev // 2
-    turns = [(tokens[:half], tokens[half:])]
+    turns = [tokens]
 
     def turn_on(tie):
-        turns.append(tuple(next_turn(after(part, tie), "head") for part in turns[-1]))
+        turns.append(next_turn(after(turns[-1], tie), "head"))
 
     for _ in range(groups // 2):
         turn_on(None)
 
-    steps = jnp.arange(groups, dtype=jnp.int32)
-    block_of = (me_head - steps) % groups
-    token_id = row_first + block_of[:, None] * rows_dev + jnp.arange(rows_dev, dtype=jnp.int32)
-    row_segs = lax.dynamic_slice_in_dim(segments, row_first, row_len, 0).reshape(groups, rows_dev)
-    segs = jnp.sum(
-        jnp.where((block_of[:, None] == steps[None, :])[:, :, None], row_segs[None], 0), axis=1
-    )
-    requests = jnp.arange(group_ids.shape[0], dtype=jnp.int32)
-    starts = jnp.sum((segments[None, :] < requests[:, None]).astype(jnp.int32), axis=1)
-    begin = lookup(starts, segs)
-    slab = lookup(lookup(prefix_owner, group_ids), segs)
-    fill = lookup(slab_fill, slab)
-    position = fill + token_id - begin
     steps_idx = jnp.arange(HS // 2, dtype=F32)
     inverse = jnp.exp(steps_idx * (-2.0 * jnp.log(10000.0) / HS))
-    angles = position.astype(F32)[:, :, None] * inverse
-    cosine = jnp.cos(angles)
-    sine = jnp.sin(angles)
-    cos = jnp.concatenate([cosine] * 4, axis=2)
-    sin = jnp.concatenate([-sine, sine, -sine, sine], axis=2)
-    info = jnp.stack([slab, begin, token_id, token_id], axis=2)
-    place = token_id[:, 0]
-    backs = jnp.arange(groups + 1, dtype=jnp.int32)
-    read = jnp.any(slab[:, :, None] == origins, axis=1).astype(jnp.int32)
-    spot = jnp.arange(read.shape[1], dtype=jnp.int32)
-    rank = jnp.sum(jnp.where(spot[:, None] < spot[None, :], read[:, :, None], 0), axis=1)
-    tables = {
-        "near_list": (steps[:, None] + backs[None, :]) % groups
-        + jnp.where(block_of[:, None] >= backs[None, :], groups, 0),
-        "reach": (begin[:, 0] < place - rows_dev).astype(jnp.int32),
-        "read": read,
-        "slab_list": jnp.sum(
-            jnp.where(
-                (rank[:, :, None] == spot[None, None, :]) & (read[:, :, None] != 0),
-                spot[None, :, None],
-                0,
-            ),
-            axis=1,
-        ),
-        "slab_count": jnp.sum(read, axis=1),
-        "fill": lookup(slab_fill, origins),
-        "slab_id": origins,
-        "place": jnp.concatenate([place - row_len, place]),
-    }
+    cos, sin, info, marks = row_tables(
+        groups,
+        jnp.stack([me_tok, me_head]).astype(jnp.int32),
+        prefix_owner,
+        slab_fill,
+        group_ids,
+        jnp.concatenate([inverse] * 4),
+        segments,
+    )
 
     missing = -w_query.shape[1] % LANES
     if missing:
         w_query = jnp.pad(w_query, ((0, 0), (0, missing)))
+
     lanes = prefix_cache.shape[1]
     packed = packed_routes(routes, route_gates, lanes)
-    prefix_rows = after(jnp.concatenate([prefix_cache, packed], axis=0), turns[1][0])
+    prefix_rows = after(jnp.concatenate([prefix_cache, packed], axis=0), turns[1])
     neighbours = to_neighbours(prefix_rows)
 
     queries, own, prev = [], [], []
     for some in (slice(0, groups // 2), slice(groups // 2, groups)):
         while len(turns) < some.stop:
-            turn_on((own[0], tables, info, neighbours))
-        pieces = [piece for parts in turns[some] for piece in parts]
+            turn_on((own[0], neighbours))
+        pieces = turns[some]
         query, keyval = project(
             after(pieces, prev[0]) if prev else pieces,
             attn_gain[None, :],
             w_query,
             w_keyval,
-            cos[some],
-            sin[some],
+            cos[len(own)],
+            sin[len(own)],
             kv_local,
             q_local,
         )
@@ -795,7 +830,9 @@
     near = prev + own
 
     def term(j, held_as):
-        return attend(j, tables, info, queries[j], near, cached, w_out, q_local, held_as)
+        return attend(
+            j, marks, origins, slab_fill, info, queries[j], near, cached, w_out, q_local, held_as
+        )
 
     down = groups // 2
     up = groups - 1 - down
@@ -839,6 +876,7 @@
 
     one = lax.ppermute(expert_in, "tok", first)
     two = lax.ppermute(expert_in, "tok", second)
+    half = rows_dev // 2
     three = [
         lax.ppermute(one[:half], "tok", second),
         lax.ppermute(two[half:], "tok", first),

time: 167 us -> 162 us (0.970); the launches traced: 167 us -> 159 us
  other arithmetic: 13.6 us -> 6.01 us
  Pallas kernels: 63.7 us -> 68 us
  local copies, waits for them, and re-layouts: 10.7 us -> 6.76 us
    reduce_sum x9 -> x0, other arithmetic: 5.39 us -> none  [the longest x4 2.98 us: lookup(): return jnp.sum(jnp.where(index[..., None] == entries, table, 0), axis=-1)]
    ppermute x3, waiting for transfers between devices: 4.89 us -> 0.01 us  [exchanged(): lax.ppermute(block, 'head', [(i, (i - j) % groups) for i in range(groups)])]
    ppermute x1, starting transfers between devices: 1.87 us -> 6.4 us  [local(): two = lax.ppermute(expert_in, 'tok', second)]
    pallas_call x0 -> x1, Pallas kernels: none -> 3.75 us  [row_tables(): pl.pallas_call(functools.partial(table_kernel, groups), out_shape=(half,)...]
    ppermute x6 -> x3, starting transfers between devices: 6.62 us -> 3.03 us  [next_turn(): lax.ppermute(block, axis, [(i, (i + 1) % count) for i in range(count)])]
    slice x4 -> x0, local copies, waits for them, and re-layouts: 2.66 us -> none  [the longest x1 1.07 us: local(): turns = [(tokens[:half], tokens[half:])]]
    ppermute x6 -> x3, waiting for transfers between devices: 13.3 us -> 15.6 us  [next_turn(): lax.ppermute(block, axis, [(i, (i + 1) % count) for i in range(count)])]
    ppermute x1, starting transfers between devices: 1.99 us -> 0.01 us  [local(): one = lax.ppermute(expert_in, 'tok', first)]
  transfers between devices with their start and end apart: 30 -> 27, of which waited for: 14 -> 12; matrix products, arithmetic and copies ran while one was open for 10% -> 4% of each run, Pallas kernels for 19% -> 23%
where the time goes in v4:
time: 162 us; the launch traced here: 159 us
  Pallas kernels  68 us (42%)
  waiting for transfers between devices  49.2 us (30%)
  starting transfers between devices  28.9 us (18%)
  local copies, waits for them, and re-layouts  6.76 us (4%)
  other arithmetic  6.01 us (4%)
    pallas_call x4, Pallas kernels, attend(): pl.pallas_call(functools.partial(attend_kernel, block, len(near), slab_sp...  28.3 us
    pallas_call x1, Pallas kernels, experts(): pl.pallas_call(functools.partial(expert_kernel, spec, rows, layout), out_...  23.6 us
    ppermute x3, waiting for transfers between devices, next_turn(): lax.ppermute(block, axis, [(i, (i + 1) % count) for i in range(count)])  15.6 us
    ppermute x1, waiting for transfers between devices, plane_sum(): beside = lax.ppermute((pair(2) + add_lower).astype(BF16), 'tok', second)  9.43 us
    ppermute x1, waiting for transfers between devices, local(): two = lax.ppermute(expert_in, 'tok', second)  9.24 us
    pallas_call x2, Pallas kernels, project(): pl.pallas_call(functools.partial(project_kernel, blocks, kv_local, q_loca...  7.59 us
    ppermute x1, starting transfers between devices, local(): two = lax.ppermute(expert_in, 'tok', second)  6.4 us
    ppermute x1, waiting for transfers between devices, plane_sum(): across_lower = lax.ppermute(three[half:], 'tok', first)  5.28 us
  transfers between devices with their start and end apart: 27, of which 12 were waited for; matrix products, arithmetic and copies ran while one was open for 4% of the time, Pallas kernels for 23%

profile of v4, /device:TPU:0, one launch (start us, length us, event | category | flops | bytes accessed | tf_op | source)
XLA Modules:
  0.0 159.3 jit_solution(4874323089044066633)
XLA Ops:
  0.0 3.0 %collective-permute-start = (bf16[128,1536]{1,0:T(8,128)(2,1)}, bf16[128,1536]{1,0:T(8,128)(2,1)S(1)}, u32[]{:S(2)}, u32[]{:S(2)}) collective-permute-start(bf16[128,1536]{1,0:T(8,128)(2,1)} %tokens.1), channel_id=1, source_target_pairs={{0,1},{1,2},{2,3},{3,0},{4,5},{5,6},{6,7},{7,4},{8,9},{9,10},{10,1... | collective-permute-start | bytes 1179656 | tf_op jit(solution)/shard_map/ppermute | solution.py:35
  3.0 0.6 maximum_bitcast_fusion.inverse
  3.6 0.7 convert_bitcast_fusion
  4.3 0.7 reduce-precision_convert_fusion.1
  5.6 3.7 %row_tables.1 = (f32[256,128]{1,0:T(8,128)}, f32[256,128]{1,0:T(8,128)}, f32[256,128]{1,0:T(8,128)}, f32[256,128]{1,0:T(8,128)}, s32[4,2,128,128]{3,2,1,0:T(8,128)}, /*index=5*/s32[4,128]{1,0:T(4,128)}) custom-call(s32[2]{0:T(128)} %pad_add_fusion.me, s32[8]{0:T(128)} %owner_of.1, s32[8]{0:T(128)} %refs_2_.7, s32[1,64]{1,0:T(1,128)} %bitcast.24, ...), custom_call_target="tpu_custom_call" | custom-call | flops 4000000000 | bytes 1000000 | tf_op jit(solution)/shard_map/row_tables/pallas_call | solution.py:180
  9.4 5.0 %collective-permute-done.refs_1_ = bf16[128,1536]{1,0:T(8,128)(2,1)S(1)} collective-permute-done((bf16[128,1536]{1,0:T(8,128)(2,1)}, bf16[128,1536]{1,0:T(8,128)(2,1)S(1)}, u32[]{:S(2)}, u32[]{:S(2)}) %collective-permute-start) | collective-permute-done | bytes 393248 | tf_op jit(solution)/shard_map/ppermute | solution.py:35
  14.4 0.7 broadcast_in_dim.9.refs_2_
  15.1 1.5 collective-permute-start.4
  16.6 1.5 collective-permute-start.3
  18.1 3.8 %norm_project_rotate.2 = (bf16[2,384,128]{2,1,0:T(8,128)(2,1)}, bf16[2,384,128]{2,1,0:T(8,128)(2,1)}, bf16[256,256]{1,0:T(8,128)(2,1)}) custom-call(bf16[128,1536]{1,0:T(8,128)(2,1)} %tokens.1, bf16[128,1536]{1,0:T(8,128)(2,1)} %copy-done.9, f32[1,1536]{1,0:T(1,128)} %broadcast_in_dim.9.refs_2_, bf16[1536,384]{1,0:T(8,128)(2,1)} %refs_3_.3, ...), custom_call_target="tpu_custom_call" | custom-call | flops 4000000000 | bytes 4000000 | tf_op jit(solution)/shard_map/norm_project_rotate/pallas_call | solution.py:258
  21.9 1.8 %collective-permute-done.4 = bf16[528,256]{1,0:T(8,128)(2,1)S(1)} collective-permute-done((bf16[528,256]{1,0:T(8,128)(2,1)S(1)}, bf16[528,256]{1,0:T(8,128)(2,1)S(1)}, u32[]{:S(2)}, u32[]{:S(2)}) %collective-permute-start.4) | collective-permute-done | bytes 270368 | tf_op jit(solution)/shard_map/ppermute | solution.py:62
  23.8 2.7 %collective-permute-done.2.refs_0_ = bf16[128,1536]{1,0:T(8,128)(2,1)S(1)} collective-permute-done((bf16[128,1536]{1,0:T(8,128)(2,1)S(1)}, bf16[128,1536]{1,0:T(8,128)(2,1)S(1)}, u32[]{:S(2)}, u32[]{:S(2)}) %collective-permute-start.2) | collective-permute-done | bytes 393248 | tf_op jit(solution)/shard_map/ppermute | solution.py:35
  26.5 1.3 collective-permute-start.1
  27.8 1.9 %collective-permute-start.7 = (bf16[528,256]{1,0:T(8,128)(2,1)S(1)}, bf16[528,256]{1,0:T(8,128)(2,1)S(1)}, u32[]{:S(2)}, u32[]{:S(2)}) collective-permute-start(bf16[528,256]{1,0:T(8,128)(2,1)S(1)} %collective-permute-done.3), channel_id=1, source_target_pairs={{0,8},{4,20},{8,0},{12,28},{16,24},{20,4},{24,16},{28,12},{1,9},{5... | collective-permute-start | bytes 811016 | tf_op jit(solution)/shard_map/ppermute | solution.py:72
  29.7 7.9 %collective-permute-done.5.refs_1_ = bf16[128,1536]{1,0:T(8,128)(2,1)S(1)} collective-permute-done((bf16[128,1536]{1,0:T(8,128)(2,1)S(1)}, bf16[128,1536]{1,0:T(8,128)(2,1)S(1)}, u32[]{:S(2)}, u32[]{:S(2)}) %collective-permute-start.5) | collective-permute-done | bytes 393248 | tf_op jit(solution)/shard_map/ppermute | solution.py:35
  37.7 0.8 copy-done.16
  38.4 3.8 %norm_project_rotate.3 = (bf16[2,384,128]{2,1,0:T(8,128)(2,1)}, bf16[2,384,128]{2,1,0:T(8,128)(2,1)}, bf16[256,256]{1,0:T(8,128)(2,1)}) custom-call(bf16[128,1536]{1,0:T(8,128)(2,1)} %copy-done.11, bf16[128,1536]{1,0:T(8,128)(2,1)} %copy-done.16, f32[1,1536]{1,0:T(1,128)} %broadcast_in_dim.9.refs_2_, bf16[1536,384]{1,0:T(8,128)(2,1)} %refs_3_.3, ...), custom_call_target="tpu_custom_call" | custom-call | flops 4000000000 | bytes 4000000 | tf_op jit(solution)/shard_map/norm_project_rotate/pallas_call | solution.py:258
  42.4 0.7 copy-done.22
  43.1 1.7 %collective-permute-start.6 = (bf16[256,256]{1,0:T(8,128)(2,1)S(1)}, bf16[256,256]{1,0:T(8,128)(2,1)S(1)}, u32[]{:S(2)}, u32[]{:S(2)}) collective-permute-start(bf16[256,256]{1,0:T(8,128)(2,1)S(1)} %copy-done.22), channel_id=1, source_target_pairs={{0,4},{4,8},{8,12},{12,16},{16,20},{20,24},{24,28},{1,5},{5,9},{9,... | collective-permute-start | bytes 393224 | tf_op jit(solution)/shard_map/ppermute | solution.py:823
  44.9 0.6 broadcast_in_dim.8.gain
  45.5 0.6 stack.44.refs_1_
  46.1 0.6 copy-done.23
  47.1 5.6 %attend.6 = bf16[128,1536]{1,0:T(8,128)(2,1)} custom-call(s32[4,128]{1,0:T(4,128)} %get-tuple-element.37.refs_0_, s32[8]{0:T(128)} %stack.44.refs_1_, s32[8]{0:T(128)} %refs_2_.7, bf16[2,384,128]{2,1,0:T(8,128)(2,1)} %get-tuple-element.55.refs_3_, s32[4,2,128,128]{3,2,1,0:T(8,128)} %get-tuple-element.41.refs_4_, bf16[256,256]{1,0:T(8,128)(2,1)} %copy-done.21, ...), custom_call_target="tpu_custom_call" | custom-call | flops 8000000000 | bytes 4000000 | tf_op jit(solution)/shard_map/attend/pallas_call | solution.py:446
  52.7 1.5 collective-permute-start.9
  54.2 7.3 %attend.7 = bf16[128,1536]{1,0:T(8,128)(2,1)} custom-call(s32[4,128]{1,0:T(4,128)} %get-tuple-element.37.refs_0_, s32[8]{0:T(128)} %stack.44.refs_1_, s32[8]{0:T(128)} %refs_2_.7, bf16[2,384,128]{2,1,0:T(8,128)(2,1)} %get-tuple-element.56.refs_3_, s32[4,2,128,128]{3,2,1,0:T(8,128)} %get-tuple-element.41.refs_4_, bf16[256,256]{1,0:T(8,128)(2,1)} %copy-done.21, ...), custom_call_target="tpu_custom_call" | custom-call | flops 8000000000 | bytes 4000000 | tf_op jit(solution)/shard_map/attend/pallas_call | solution.py:446
  61.6 8.1 %attend.5 = bf16[128,1536]{1,0:T(8,128)(2,1)} custom-call(s32[4,128]{1,0:T(4,128)} %get-tuple-element.37.refs_0_, s32[8]{0:T(128)} %stack.44.refs_1_, s32[8]{0:T(128)} %refs_2_.7, bf16[2,384,128]{2,1,0:T(8,128)(2,1)} %get-tuple-element.54.refs_3_, s32[4,2,128,128]{3,2,1,0:T(8,128)} %get-tuple-element.41.refs_4_, bf16[256,256]{1,0:T(8,128)(2,1)} %copy-done.21, ...), custom_call_target="tpu_custom_call" | custom-call | flops 8000000000 | bytes 4000000 | tf_op jit(solution)/shard_map/attend/pallas_call | solution.py:446
  69.7 1.1 add_convert_fusion.4
  70.8 1.5 collective-permute-start.10
  72.3 7.4 %attend.4.own = f32[128,1536]{1,0:T(8,128)} custom-call(s32[4,128]{1,0:T(4,128)} %get-tuple-element.37.refs_0_, s32[8]{0:T(128)} %stack.44.refs_1_, s32[8]{0:T(128)} %refs_2_.7, bf16[2,384,128]{2,1,0:T(8,128)(2,1)} %get-tuple-element.40.refs_3_, s32[4,2,128,128]{3,2,1,0:T(8,128)} %get-tuple-element.41.refs_4_, bf16[256,256]{1,0:T(8,128)(2,1)} %copy-done.21, ...), custom_call_target="tpu_custom_call" | custom-call | flops 8000000000 | bytes 4000000 | tf_op jit(solution)/shard_map/attend/pallas_call | solution.py:446
  79.7 2.1 %route_tables.1 = (s32[4,1024]{1,0:T(4,128)}, f32[4,1024]{1,0:T(4,128)}, s32[1024,8]{1,0:T(8,128)}) custom-call(s32[1]{0:T(128)} %bitcast.14.first_expert, bf16[2112,256]{1,0:T(8,128)(2,1)} %copy-done.5, bf16[2112,256]{1,0:T(8,128)(2,1)} %copy-done.8), custom_call_target="tpu_custom_call" | custom-call | flops 3000000000 | bytes 1000000 | tf_op jit(solution)/shard_map/route_tables/pallas_call | solution.py:729
  81.8 0.7 copy-done.14
  82.7 2.7 %add_and_norm.1 = (f32[128,1536]{1,0:T(8,128)}, bf16[128,1536]{1,0:T(8,128)(2,1)}) custom-call(bf16[128,1536]{1,0:T(8,128)(2,1)} %tokens.1, f32[1,1536]{1,0:T(1,128)} %broadcast_in_dim.8.gain, f32[128,1536]{1,0:T(8,128)} %attend.4.own, bf16[128,1536]{1,0:T(8,128)(2,1)} %copy-done.15, bf16[128,1536]{1,0:T(8,128)(2,1)} %copy-done.14), custom_call_target="tpu_custom_call" | custom-call | flops 1000000000 | bytes 3145728 | tf_op jit(solution)/shard_map/add_and_norm/pallas_call | solution.py:498
  85.4 6.4 %collective-permute-start.13 = (bf16[128,1536]{1,0:T(8,128)(2,1)}, bf16[128,1536]{1,0:T(8,128)(2,1)S(1)}, u32[]{:S(2)}, u32[]{:S(2)}) collective-permute-start(bf16[128,1536]{1,0:T(8,128)(2,1)} %get-tuple-element.63.refs_0_), channel_id=1, source_target_pairs={{0,8},{4,20},{8,0},{12,28},{16,24},{20,4},{24,16},{28,12},{1,9},{5... | collective-permute-start | bytes 1179656 | tf_op jit(solution)/shard_map/ppermute | solution.py:878
  91.8 9.2 %collective-permute-done.13.refs_2_ = bf16[128,1536]{1,0:T(8,128)(2,1)S(1)} collective-permute-done((bf16[128,1536]{1,0:T(8,128)(2,1)}, bf16[128,1536]{1,0:T(8,128)(2,1)S(1)}, u32[]{:S(2)}, u32[]{:S(2)}) %collective-permute-start.13) | collective-permute-done | bytes 393248 | tf_op jit(solution)/shard_map/ppermute | solution.py:878
  101.1 2.2 %collective-permute-start.15 = (bf16[64,1536]{1,0:T(8,128)(2,1)S(1)}, bf16[64,1536]{1,0:T(8,128)(2,1)S(1)}, u32[]{:S(2)}, u32[]{:S(2)}) collective-permute-start(bf16[64,1536]{1,0:T(8,128)(2,1)S(1)} %slice.45), channel_id=1, source_target_pairs={{0,16},{4,12},{8,24},{12,4},{16,0},{20,28},{24,8},{28,20},{1,17},{... | collective-permute-start | bytes 589832 | tf_op jit(solution)/shard_map/ppermute | solution.py:882
  103.9 4.7 %collective-permute-done.15.refs_4_ = bf16[64,1536]{1,0:T(8,128)(2,1)S(1)} collective-permute-done((bf16[64,1536]{1,0:T(8,128)(2,1)S(1)}, bf16[64,1536]{1,0:T(8,128)(2,1)S(1)}, u32[]{:S(2)}, u32[]{:S(2)}) %collective-permute-start.15) | collective-permute-done | bytes 196640 | tf_op jit(solution)/shard_map/ppermute | solution.py:882
  109.2 0.9 collective-permute-done.20.refs_9_
  111.1 0.8 copy-done.13
  111.9 23.6 %experts.1 = (bf16[512,1536]{1,0:T(8,128)(2,1)}, bf16[384,1536]{1,0:T(8,128)(2,1)}, bf16[128,1536]{1,0:T(8,128)(2,1)}) custom-call(s32[4,1024]{1,0:T(4,128)} %get-tuple-element.57.slot_row, f32[4,1024]{1,0:T(4,128)} %get-tuple-element.58.gate_row, s32[1024,8]{1,0:T(8,128)} %get-tuple-element.59.slot_col, bf16[128,1536]{1,0:T(8,128)(2,1)} %get-tuple-element.63.refs_0_, ...), custom_call_target="tpu_custom_call" | custom-call | flops 12884901888 | bytes 25165824 | tf_op jit(solution)/shard_map/experts/pallas_call | solution.py:637
  136.1 1.4 collective-permute-done.22
  137.5 1.1 add_convert_fusion.3
  138.6 1.4 collective-permute-start.24
  140.0 0.9 collective-permute-start.23
  140.9 5.3 %collective-permute-done.24 = bf16[64,1536]{1,0:T(8,128)(2,1)S(1)} collective-permute-done((bf16[64,1536]{1,0:T(8,128)(2,1)S(1)}, bf16[64,1536]{1,0:T(8,128)(2,1)S(1)}, u32[]{:S(2)}, u32[]{:S(2)}) %collective-permute-start.24) | collective-permute-done | bytes 196640 | tf_op jit(solution)/shard_map/ppermute | solution.py:115
  146.4 0.9 collective-permute-start.25
  147.3 1.6 collective-permute-start.26
  148.9 9.4 %collective-permute-done.25 = bf16[128,1536]{1,0:T(8,128)(2,1)S(1)} collective-permute-done((bf16[128,1536]{1,0:T(8,128)(2,1)S(1)}, bf16[128,1536]{1,0:T(8,128)(2,1)S(1)}, u32[]{:S(2)}, u32[]{:S(2)}) %collective-permute-start.25) | collective-permute-done | bytes 393248 | tf_op jit(solution)/shard_map/ppermute | solution.py:126
  158.3 1.0 add_convert_fusion
  (84 shorter events, 4.5 us)
Async XLA Ops:
  0.0 14.4 %collective-permute-start = (bf16[128,1536]{1,0:T(8,128)(2,1)}, bf16[128,1536]{1,0:T(8,128)(2,1)S(1)}, u32[]{:S(2)}, u32[]{:S(2)}) collective-permute-start(bf16[128,1536]{1,0:T(8,128)(2,1)} %tokens.1), channel_id=1, source_target_pairs={{0,1},{1,2},{2,3},{3,0},{4,5},{5,6},{6,7},{7,4},{8,9},{9,10},{10,1... | collective-permute-start | bytes 1179656 | tf_op jit(solution)/shard_map/ppermute | solution.py:35
  5.6 8.8 %copy-start.2 = (bf16[512,256]{1,0:T(8,128)(2,1)S(1)}, bf16[512,256]{1,0:T(8,128)(2,1)}, u32[]{:S(2)}) copy-start(bf16[512,256]{1,0:T(8,128)(2,1)} %param.21) | copy-start | bytes 786436
  5.6 8.8 %copy-start.6 = (f32[1536]{0:T(1024)S(1)}, f32[1536]{0:T(1024)}, u32[]{:S(2)}) copy-start(f32[1536]{0:T(1024)} %param.22) | copy-start | bytes 18436
  14.4 3.8 %copy-start.9 = (bf16[128,1536]{1,0:T(8,128)(2,1)}, bf16[128,1536]{1,0:T(8,128)(2,1)S(1)}, u32[]{:S(2)}) copy-start(bf16[128,1536]{1,0:T(8,128)(2,1)S(1)} %collective-permute-done.refs_1_) | copy-start | bytes 1179652
  14.4 12.1 %collective-permute-start.2 = (bf16[128,1536]{1,0:T(8,128)(2,1)S(1)}, bf16[128,1536]{1,0:T(8,128)(2,1)S(1)}, u32[]{:S(2)}, u32[]{:S(2)}) collective-permute-start(bf16[128,1536]{1,0:T(8,128)(2,1)S(1)} %collective-permute-done.refs_1_), channel_id=1, source_target_pairs={{0,1},{1,2},{2,3},{3,0},{4,5},{5,6},{6,7},{7,4},{8,9},{9,10},{10,1... | collective-permute-start | bytes 1179656 | tf_op jit(solution)/shard_map/ppermute | solution.py:35
  15.1 8.7 %collective-permute-start.4 = (bf16[528,256]{1,0:T(8,128)(2,1)S(1)}, bf16[528,256]{1,0:T(8,128)(2,1)S(1)}, u32[]{:S(2)}, u32[]{:S(2)}) collective-permute-start(bf16[528,256]{1,0:T(8,128)(2,1)S(1)} %maximum_maximum_fusion), channel_id=1, source_target_pairs={{0,8},{4,20},{8,0},{12,28},{16,24},{20,4},{24,16},{28,12},{1,9},{5... | collective-permute-start | bytes 811016 | tf_op jit(solution)/shard_map/ppermute | solution.py:62
  16.6 7.2 %collective-permute-start.3 = (bf16[528,256]{1,0:T(8,128)(2,1)S(1)}, bf16[528,256]{1,0:T(8,128)(2,1)S(1)}, u32[]{:S(2)}, u32[]{:S(2)}) collective-permute-start(bf16[528,256]{1,0:T(8,128)(2,1)S(1)} %maximum_maximum_fusion), channel_id=1, source_target_pairs={{0,16},{4,12},{8,24},{12,4},{16,0},{20,28},{24,8},{28,20},{1,17},{... | collective-permute-start | bytes 811016 | tf_op jit(solution)/shard_map/ppermute | solution.py:62
  26.5 11.2 %copy-start.11 = (bf16[128,1536]{1,0:T(8,128)(2,1)}, bf16[128,1536]{1,0:T(8,128)(2,1)S(1)}, u32[]{:S(2)}) copy-start(bf16[128,1536]{1,0:T(8,128)(2,1)S(1)} %collective-permute-done.2.refs_0_) | copy-start | bytes 1179652
  26.5 11.2 %collective-permute-start.5 = (bf16[128,1536]{1,0:T(8,128)(2,1)S(1)}, bf16[128,1536]{1,0:T(8,128)(2,1)S(1)}, u32[]{:S(2)}, u32[]{:S(2)}) collective-permute-start(bf16[128,1536]{1,0:T(8,128)(2,1)S(1)} %collective-permute-done.2.refs_0_), channel_id=1, source_target_pairs={{0,1},{1,2},{2,3},{3,0},{4,5},{5,6},{6,7},{7,4},{8,9},{9,10},{10,1... | collective-permute-start | bytes 1179656 | tf_op jit(solution)/shard_map/ppermute | solution.py:35
  26.5 3.2 %collective-permute-start.1 = (bf16[256,256]{1,0:T(8,128)(2,1)}, bf16[256,256]{1,0:T(8,128)(2,1)S(1)}, u32[]{:S(2)}, u32[]{:S(2)}) collective-permute-start(bf16[256,256]{1,0:T(8,128)(2,1)} %get-tuple-element.42.refs_7_), channel_id=1, source_target_pairs={{0,4},{4,8},{8,12},{12,16},{16,20},{20,24},{24,28},{1,5},{5,9},{9,... | collective-permute-start | bytes 393224 | tf_op jit(solution)/shard_map/ppermute | solution.py:823
  27.8 14.5 %collective-permute-start.7 = (bf16[528,256]{1,0:T(8,128)(2,1)S(1)}, bf16[528,256]{1,0:T(8,128)(2,1)S(1)}, u32[]{:S(2)}, u32[]{:S(2)}) collective-permute-start(bf16[528,256]{1,0:T(8,128)(2,1)S(1)} %collective-permute-done.3), channel_id=1, source_target_pairs={{0,8},{4,20},{8,0},{12,28},{16,24},{20,4},{24,16},{28,12},{1,9},{5... | collective-permute-start | bytes 811016 | tf_op jit(solution)/shard_map/ppermute | solution.py:72
  29.7 12.5 %copy-start.21 = (bf16[256,256]{1,0:T(8,128)(2,1)}, bf16[256,256]{1,0:T(8,128)(2,1)S(1)}, u32[]{:S(2)}) copy-start(bf16[256,256]{1,0:T(8,128)(2,1)S(1)} %collective-permute-done.1.refs_5_) | copy-start | bytes 393220
  37.7 0.8 copy-start.16
  42.2 0.9 copy-start.22
  42.2 2.7 %copy-start.7 = (f32[1536]{0:T(1024)S(1)}, f32[1536]{0:T(1024)}, u32[]{:S(2)}) copy-start(f32[1536]{0:T(1024)} %param.26) | copy-start | bytes 18436
  42.3 3.7 %copy-start.5 = (bf16[2112,256]{1,0:T(8,128)(2,1)}, bf16[2112,256]{1,0:T(8,128)(2,1)S(1)}, u32[]{:S(2)}) copy-start(bf16[2112,256]{1,0:T(8,128)(2,1)S(1)} %constant_dynamic-update-slice_fusion.refs_9_.refs_0_) | copy-start | bytes 3244036
  42.4 3.7 %collective-permute-start.8 = (bf16[2112,256]{1,0:T(8,128)(2,1)S(1)}, bf16[2112,256]{1,0:T(8,128)(2,1)S(1)}, u32[]{:S(2)}, u32[]{:S(2)}) collective-permute-start(bf16[2112,256]{1,0:T(8,128)(2,1)S(1)} %constant_dynamic-update-slice_fusion.refs_9_.refs_0_), channel_id=1, source_target_pairs={{0,4},{4,0},{8,12},{12,8},{16,20},{20,16},{24,28},{28,24},{1,5},{5... | collective-permute-start | bytes 3244040 | tf_op jit(solution)/shard_map/ppermute | solution.py:76
  43.1 3.0 %collective-permute-start.6 = (bf16[256,256]{1,0:T(8,128)(2,1)S(1)}, bf16[256,256]{1,0:T(8,128)(2,1)S(1)}, u32[]{:S(2)}, u32[]{:S(2)}) collective-permute-start(bf16[256,256]{1,0:T(8,128)(2,1)S(1)} %copy-done.22), channel_id=1, source_target_pairs={{0,4},{4,8},{8,12},{12,16},{16,20},{20,24},{24,28},{1,5},{5,9},{9,... | collective-permute-start | bytes 393224 | tf_op jit(solution)/shard_map/ppermute | solution.py:823
  46.1 1.0 copy-start.8
  52.7 17.0 %collective-permute-start.9 = (bf16[128,1536]{1,0:T(8,128)(2,1)}, bf16[128,1536]{1,0:T(8,128)(2,1)S(1)}, u32[]{:S(2)}, u32[]{:S(2)}) collective-permute-start(bf16[128,1536]{1,0:T(8,128)(2,1)} %attend.6), channel_id=1, source_target_pairs={{0,3},{1,0},{2,1},{3,2},{4,7},{5,4},{6,5},{7,6},{8,11},{9,8},{10,9... | collective-permute-start | bytes 1179656 | tf_op jit(solution)/shard_map/ppermute | solution.py:826
  61.5 20.3 %collective-permute-start.11 = (bf16[128,1536]{1,0:T(8,128)(2,1)}, bf16[128,1536]{1,0:T(8,128)(2,1)S(1)}, u32[]{:S(2)}, u32[]{:S(2)}) collective-permute-start(bf16[128,1536]{1,0:T(8,128)(2,1)} %attend.7), channel_id=1, source_target_pairs={{0,1},{1,2},{2,3},{3,0},{4,5},{5,6},{6,7},{7,4},{8,9},{9,10},{10,1... | collective-permute-start | bytes 1179656 | tf_op jit(solution)/shard_map/ppermute | solution.py:826
  70.8 11.0 %collective-permute-start.10 = (bf16[128,1536]{1,0:T(8,128)(2,1)S(1)}, bf16[128,1536]{1,0:T(8,128)(2,1)S(1)}, u32[]{:S(2)}, u32[]{:S(2)}) collective-permute-start(bf16[128,1536]{1,0:T(8,128)(2,1)S(1)} %add_convert_fusion.4), channel_id=1, source_target_pairs={{0,3},{1,0},{2,1},{3,2},{4,7},{5,4},{6,5},{7,6},{8,11},{9,8},{10,9... | collective-permute-start | bytes 1179656 | tf_op jit(solution)/shard_map/ppermute | solution.py:826
  81.8 0.8 copy-start.14
  81.8 0.9 copy-start.15
  85.4 15.7 %collective-permute-start.13 = (bf16[128,1536]{1,0:T(8,128)(2,1)}, bf16[128,1536]{1,0:T(8,128)(2,1)S(1)}, u32[]{:S(2)}, u32[]{:S(2)}) collective-permute-start(bf16[128,1536]{1,0:T(8,128)(2,1)} %get-tuple-element.63.refs_0_), channel_id=1, source_target_pairs={{0,8},{4,20},{8,0},{12,28},{16,24},{20,4},{24,16},{28,12},{1,9},{5... | collective-permute-start | bytes 1179656 | tf_op jit(solution)/shard_map/ppermute | solution.py:878
  91.8 11.5 %collective-permute-start.12 = (bf16[128,1536]{1,0:T(8,128)(2,1)}, bf16[128,1536]{1,0:T(8,128)(2,1)S(1)}, u32[]{:S(2)}, u32[]{:S(2)}) collective-permute-start(bf16[128,1536]{1,0:T(8,128)(2,1)} %get-tuple-element.63.refs_0_), channel_id=1, source_target_pairs={{0,16},{4,12},{8,24},{12,4},{16,0},{20,28},{24,8},{28,20},{1,17},{... | collective-permute-start | bytes 1179656 | tf_op jit(solution)/shard_map/ppermute | solution.py:877
  91.8 17.4 %collective-permute-start.16 = (bf16[128,1536]{1,0:T(8,128)(2,1)}, bf16[128,1536]{1,0:T(8,128)(2,1)S(1)}, u32[]{:S(2)}, u32[]{:S(2)}) collective-permute-start(bf16[128,1536]{1,0:T(8,128)(2,1)} %get-tuple-element.63.refs_0_), channel_id=1, source_target_pairs={{0,4},{4,0},{8,12},{12,8},{16,20},{20,16},{24,28},{28,24},{1,5},{5... | collective-permute-start | bytes 1179656 | tf_op jit(solution)/shard_map/ppermute | solution.py:875
  101.0 9.4 %copy-start.3 = (bf16[128,1536]{1,0:T(8,128)(2,1)}, bf16[128,1536]{1,0:T(8,128)(2,1)S(1)}, u32[]{:S(2)}) copy-start(bf16[128,1536]{1,0:T(8,128)(2,1)S(1)} %collective-permute-done.13.refs_2_) | copy-start | bytes 1179652
  101.1 7.6 %collective-permute-start.15 = (bf16[64,1536]{1,0:T(8,128)(2,1)S(1)}, bf16[64,1536]{1,0:T(8,128)(2,1)S(1)}, u32[]{:S(2)}, u32[]{:S(2)}) collective-permute-start(bf16[64,1536]{1,0:T(8,128)(2,1)S(1)} %slice.45), channel_id=1, source_target_pairs={{0,16},{4,12},{8,24},{12,4},{16,0},{20,28},{24,8},{28,20},{1,17},{... | collective-permute-start | bytes 589832 | tf_op jit(solution)/shard_map/ppermute | solution.py:882
  103.3 7.2 %copy-start.4 = (bf16[128,1536]{1,0:T(8,128)(2,1)}, bf16[128,1536]{1,0:T(8,128)(2,1)S(1)}, u32[]{:S(2)}) copy-start(bf16[128,1536]{1,0:T(8,128)(2,1)S(1)} %collective-permute-done.12.refs_1_) | copy-start | bytes 1179652
  103.3 5.7 %collective-permute-start.14 = (bf16[64,1536]{1,0:T(8,128)(2,1)S(1)}, bf16[64,1536]{1,0:T(8,128)(2,1)S(1)}, u32[]{:S(2)}, u32[]{:S(2)}) collective-permute-start(bf16[64,1536]{1,0:T(8,128)(2,1)S(1)} %slice.44), channel_id=1, source_target_pairs={{0,8},{4,20},{8,0},{12,28},{16,24},{20,4},{24,16},{28,12},{1,9},{5... | collective-permute-start | bytes 589832 | tf_op jit(solution)/shard_map/ppermute | solution.py:881
  103.4 6.7 %collective-permute-start.18 = (bf16[128,1536]{1,0:T(8,128)(2,1)S(1)}, bf16[128,1536]{1,0:T(8,128)(2,1)S(1)}, u32[]{:S(2)}, u32[]{:S(2)}) collective-permute-start(bf16[128,1536]{1,0:T(8,128)(2,1)S(1)} %collective-permute-done.13.refs_2_), channel_id=1, source_target_pairs={{0,4},{4,0},{8,12},{12,8},{16,20},{20,16},{24,28},{28,24},{1,5},{5... | collective-permute-start | bytes 1179656 | tf_op jit(solution)/shard_map/ppermute | solution.py:875
  103.4 7.0 %collective-permute-start.17 = (bf16[128,1536]{1,0:T(8,128)(2,1)S(1)}, bf16[128,1536]{1,0:T(8,128)(2,1)S(1)}, u32[]{:S(2)}, u32[]{:S(2)}) collective-permute-start(bf16[128,1536]{1,0:T(8,128)(2,1)S(1)} %collective-permute-done.12.refs_1_), channel_id=1, source_target_pairs={{0,4},{4,0},{8,12},{12,8},{16,20},{20,16},{24,28},{28,24},{1,5},{5... | collective-permute-start | bytes 1179656 | tf_op jit(solution)/shard_map/ppermute | solution.py:875
  108.7 1.8 %copy-start.17 = (bf16[64,1536]{1,0:T(8,128)(2,1)}, bf16[64,1536]{1,0:T(8,128)(2,1)S(1)}, u32[]{:S(2)}) copy-start(bf16[64,1536]{1,0:T(8,128)(2,1)S(1)} %collective-permute-done.15.refs_4_) | copy-start | bytes 589828
  108.7 1.4 collective-permute-start.20
  109.0 1.5 copy-start.18
  109.0 1.4 collective-permute-start.19
  109.2 1.3 copy-start.10
  110.1 0.8 copy-start.12
  111.1 0.8 copy-start.13
  135.5 10.7 %copy-start = (bf16[512,1536]{1,0:T(8,128)(2,1)S(1)}, bf16[512,1536]{1,0:T(8,128)(2,1)}, u32[]{:S(2)}) copy-start(bf16[512,1536]{1,0:T(8,128)(2,1)} %get-tuple-element.67) | copy-start | bytes 4718596
  135.5 2.0 %collective-permute-start.22 = (bf16[128,1536]{1,0:T(8,128)(2,1)}, bf16[128,1536]{1,0:T(8,128)(2,1)S(1)}, u32[]{:S(2)}, u32[]{:S(2)}) collective-permute-start(bf16[128,1536]{1,0:T(8,128)(2,1)} %get-tuple-element.66), channel_id=1, source_target_pairs={{0,4},{4,0},{8,12},{12,8},{16,20},{20,16},{24,28},{28,24},{1,5},{5... | collective-permute-start | bytes 1179656 | tf_op jit(solution)/shard_map/ppermute | solution.py:111
  135.7 10.5 %collective-permute-start.21 = (bf16[384,1536]{1,0:T(8,128)(2,1)}, bf16[384,1536]{1,0:T(8,128)(2,1)S(1)}, u32[]{:S(2)}, u32[]{:S(2)}) collective-permute-start(bf16[384,1536]{1,0:T(8,128)(2,1)} %get-tuple-element.65), channel_id=1, source_target_pairs={{0,4},{4,0},{8,12},{12,8},{16,20},{20,16},{24,28},{28,24},{1,5},{5... | collective-permute-start | bytes 3538952 | tf_op jit(solution)/shard_map/ppermute | solution.py:112
  138.6 7.6 %collective-permute-start.24 = (bf16[64,1536]{1,0:T(8,128)(2,1)S(1)}, bf16[64,1536]{1,0:T(8,128)(2,1)S(1)}, u32[]{:S(2)}, u32[]{:S(2)}) collective-permute-start(bf16[64,1536]{1,0:T(8,128)(2,1)S(1)} %get-tuple-element.71), channel_id=1, source_target_pairs={{0,16},{4,12},{8,24},{12,4},{16,0},{20,28},{24,8},{28,20},{1,17},{... | collective-permute-start | bytes 589832 | tf_op jit(solution)/shard_map/ppermute | solution.py:115
  140.0 18.3 %copy-start.1 = (f32[128,1536]{1,0:T(8,128)S(1)}, f32[128,1536]{1,0:T(8,128)}, u32[]{:S(2)}) copy-start(f32[128,1536]{1,0:T(8,128)} %get-tuple-element.62) | copy-start | bytes 2359300
  140.0 6.2 %collective-permute-start.23 = (bf16[64,1536]{1,0:T(8,128)(2,1)S(1)}, bf16[64,1536]{1,0:T(8,128)(2,1)S(1)}, u32[]{:S(2)}, u32[]{:S(2)}) collective-permute-start(bf16[64,1536]{1,0:T(8,128)(2,1)S(1)} %get-tuple-element.72), channel_id=1, source_target_pairs={{0,8},{4,20},{8,0},{12,28},{16,24},{20,4},{24,16},{28,12},{1,9},{5... | collective-permute-start | bytes 589832 | tf_op jit(solution)/shard_map/ppermute | solution.py:114
  146.4 11.8 %collective-permute-start.25 = (bf16[128,1536]{1,0:T(8,128)(2,1)S(1)}, bf16[128,1536]{1,0:T(8,128)(2,1)S(1)}, u32[]{:S(2)}, u32[]{:S(2)}) collective-permute-start(bf16[128,1536]{1,0:T(8,128)(2,1)S(1)} %get-tuple-element.69), channel_id=1, source_target_pairs={{0,8},{4,20},{8,0},{12,28},{16,24},{20,4},{24,16},{28,12},{1,9},{5... | collective-permute-start | bytes 1179656 | tf_op jit(solution)/shard_map/ppermute | solution.py:126
  147.3 11.0 %collective-permute-start.26 = (bf16[128,1536]{1,0:T(8,128)(2,1)S(1)}, bf16[128,1536]{1,0:T(8,128)(2,1)S(1)}, u32[]{:S(2)}, u32[]{:S(2)}) collective-permute-start(bf16[128,1536]{1,0:T(8,128)(2,1)S(1)} %get-tuple-element.70), channel_id=1, source_target_pairs={{0,16},{4,12},{8,24},{12,4},{16,0},{20,28},{24,8},{28,20},{1,17},{... | collective-permute-start | bytes 1179656 | tf_op jit(solution)/shard_map/ppermute | solution.py:125
  (3 other events, 2.0 us)

commit v5 on v4

--- a/solution.py
+++ b/solution.py
@@ -203,10 +203,10 @@
 
 
 def project_kernel(blocks, kv_local, q_local, *refs):
-    pieces = refs[:blocks]
-    gain, wq, wkv, cos, sin = refs[blocks : blocks + 5]
-    q_outs = refs[blocks + 5 : 2 * blocks + 5]
-    kv_out, normed = refs[2 * blocks + 5 :]
+    pieces = refs[: 2 * blocks]
+    gain, wq, wkv, cos, sin = refs[2 * blocks : 2 * blocks + 5]
+    q_outs = refs[2 * blocks + 5 : 3 * blocks + 5]
+    kv_out, normed = refs[3 * blocks + 5 :]
     half = pieces[0].shape[0]
     for i, piece in enumerate(pieces):
         wide = piece[...].astype(F32)
@@ -252,14 +252,14 @@
 
 
 def project(pieces, gain, w_query, w_keyval, cos, sin, kv_local, q_local):
-    blocks = len(pieces)
-    rows_dev, width = pieces[0].shape
+    blocks = len(pieces) // 2
+    rows_dev, width = 2 * pieces[0].shape[0], pieces[0].shape[1]
     share = q_local // kv_local
     outs = pl.pallas_call(
         functools.partial(project_kernel, blocks, kv_local, q_local),
         out_shape=[jax.ShapeDtypeStruct((kv_local, share * rows_dev, LANES), BF16)] * blocks
         + [jax.ShapeDtypeStruct((blocks * rows_dev, kv_local * LANES), BF16)],
-        in_specs=[vmem()] * (blocks + 5),
+        in_specs=[vmem()] * (2 * blocks + 5),
         out_specs=[vmem()] * (blocks + 1),
         scratch_shapes=[pltpu.VMEM((blocks * rows_dev, width), BF16)],
         compiler_params=params(),
@@ -774,10 +774,11 @@
     q_local = w_query.shape[1] // HS
     origins = plane_origins()
 
-    turns = [tokens]
+    half = rows_dev // 2
+    turns = [(tokens[:half], tokens[half:])]
 
     def turn_on(tie):
-        turns.append(next_turn(after(turns[-1], tie), "head"))
+        turns.append(tuple(next_turn(after(part, tie), "head") for part in turns[-1]))
 
     for _ in range(groups // 2):
         turn_on(None)
@@ -800,14 +801,14 @@
 
     lanes = prefix_cache.shape[1]
     packed = packed_routes(routes, route_gates, lanes)
-    prefix_rows = after(jnp.concatenate([prefix_cache, packed], axis=0), turns[1])
+    prefix_rows = after(jnp.concatenate([prefix_cache, packed], axis=0), turns[1][0])
     neighbours = to_neighbours(prefix_rows)
 
     queries, own, prev = [], [], []
     for some in (slice(0, groups // 2), slice(groups // 2, groups)):
         while len(turns) < some.stop:
             turn_on((own[0], neighbours))
-        pieces = turns[some]
+        pieces = [piece for parts in turns[some] for piece in parts]
         query, keyval = project(
             after(pieces, prev[0]) if prev else pieces,
             attn_gain[None, :],
@@ -876,7 +877,6 @@
 
     one = lax.ppermute(expert_in, "tok", first)
     two = lax.ppermute(expert_in, "tok", second)
-    half = rows_dev // 2
     three = [
         lax.ppermute(one[:half], "tok", second),
         lax.ppermute(two[half:], "tok", first),

time: 162 us -> 162 us (level); the launches traced: 159 us -> 161 us
    ppermute x3 -> x6, starting transfers between devices: 3.03 us -> 6.06 us  [next_turn(): lax.ppermute(block, axis, [(i, (i + 1) % count) for i in range(count)])]
    ppermute x1, starting transfers between devices: 6.4 us -> 3.72 us  [local(): two = lax.ppermute(expert_in, 'tok', second)]
    ppermute x1, waiting for transfers between devices: 4.73 us -> 2.7 us  [local(): lax.ppermute(two[half:], 'tok', first)]
    ppermute x1, waiting for transfers between devices: 1.85 us -> 0.01 us  [to_neighbours(): lax.ppermute(block, 'tok', second)]
    ppermute x1, starting transfers between devices: 0.01 us -> 1.76 us  [local(): one = lax.ppermute(expert_in, 'tok', first)]
    ppermute x1, waiting for transfers between devices: 0.35 us -> 2.1 us  [local(): lax.ppermute(one[:half], 'tok', second)]
    ppermute x3 -> x6, waiting for transfers between devices: 15.6 us -> 17.1 us  [next_turn(): lax.ppermute(block, axis, [(i, (i + 1) % count) for i in range(count)])]
    unnamed x51 -> x63, local copies, waits for them, and re-layouts: 4.81 us -> 4.72 us
  transfers between devices with their start and end apart: 27 -> 30, of which waited for: 12 -> 11; matrix products, arithmetic and copies ran while one was open for 4% -> 4% of each run, Pallas kernels for 23% -> 22%
where the time goes in v5:
time: 162 us; the launch traced here: 161 us
  Pallas kernels  69.3 us (43%)
  waiting for transfers between devices  48.7 us (30%)
  starting transfers between devices  29.6 us (18%)
  local copies, waits for them, and re-layouts  7.66 us (5%)
  other arithmetic  5.3 us (3%)
    pallas_call x4, Pallas kernels, attend(): pl.pallas_call(functools.partial(attend_kernel, block, len(near), slab_sp...  29.3 us
    pallas_call x1, Pallas kernels, experts(): pl.pallas_call(functools.partial(expert_kernel, spec, rows, layout), out_...  23.6 us
    ppermute x6, waiting for transfers between devices, next_turn(): lax.ppermute(block, axis, [(i, (i + 1) % count) for i in range(count)])  17.1 us
    ppermute x1, waiting for transfers between devices, plane_sum(): beside = lax.ppermute((pair(2) + add_lower).astype(BF16), 'tok', second)  9.53 us
    ppermute x1, waiting for transfers between devices, local(): two = lax.ppermute(expert_in, 'tok', second)  7.97 us
    pallas_call x2, Pallas kernels, project(): pl.pallas_call(functools.partial(project_kernel, blocks, kv_local, q_loca...  7.83 us
    ppermute x1, waiting for transfers between devices, plane_sum(): across_lower = lax.ppermute(three[half:], 'tok', first)  6.49 us
    ppermute x6, starting transfers between devices, next_turn(): lax.ppermute(block, axis, [(i, (i + 1) % count) for i in range(count)])  6.06 us
  transfers between devices with their start and end apart: 30, of which 11 were waited for; matrix products, arithmetic and copies ran while one was open for 4% of the time, Pallas kernels for 22%

profile of v5, /device:TPU:0, one launch (start us, length us, event | category | flops | bytes accessed | tf_op | source)
XLA Modules:
  0.0 161.0 jit_solution(2996338201416511358)
XLA Ops:
  0.0 1.0 fusion.3
  1.1 3.1 %collective-permute-start.1 = (bf16[64,1536]{1,0:T(8,128)(2,1)S(1)}, bf16[64,1536]{1,0:T(8,128)(2,1)S(1)}, u32[]{:S(2)}, u32[]{:S(2)}) collective-permute-start(bf16[64,1536]{1,0:T(8,128)(2,1)S(1)} %get-tuple-element.79.refs_1_), channel_id=1, source_target_pairs={{0,1},{1,2},{2,3},{3,0},{4,5},{5,6},{6,7},{7,4},{8,9},{9,10},{10,1... | collective-permute-start | bytes 589832 | tf_op jit(solution)/shard_map/ppermute | solution.py:35
  4.1 1.6 collective-permute-start
  6.3 0.7 reduce-precision_convert_fusion.1
  7.6 3.7 %row_tables.1 = (f32[256,128]{1,0:T(8,128)}, f32[256,128]{1,0:T(8,128)}, f32[256,128]{1,0:T(8,128)}, f32[256,128]{1,0:T(8,128)}, s32[4,2,128,128]{3,2,1,0:T(8,128)}, /*index=5*/s32[4,128]{1,0:T(4,128)}) custom-call(s32[2]{0:T(128)} %pad_add_fusion.me, s32[8]{0:T(128)} %owner_of.1, s32[8]{0:T(128)} %refs_2_.7, s32[1,64]{1,0:T(1,128)} %bitcast.24, ...), custom_call_target="tpu_custom_call" | custom-call | flops 4000000000 | bytes 1000000 | tf_op jit(solution)/shard_map/row_tables/pallas_call | solution.py:180
  11.4 0.6 broadcast_in_dim.9.refs_4_
  12.0 3.3 %collective-permute-done.refs_2_ = bf16[64,1536]{1,0:T(8,128)(2,1)S(1)} collective-permute-done((bf16[64,1536]{1,0:T(8,128)(2,1)S(1)}, bf16[64,1536]{1,0:T(8,128)(2,1)S(1)}, u32[]{:S(2)}, u32[]{:S(2)}) %collective-permute-start) | collective-permute-done | bytes 196640 | tf_op jit(solution)/shard_map/ppermute | solution.py:35
  15.3 1.5 collective-permute-start.6
  16.8 1.5 collective-permute-start.5
  18.3 1.3 collective-permute-start.4
  19.6 3.9 %norm_project_rotate.2 = (bf16[2,384,128]{2,1,0:T(8,128)(2,1)}, bf16[2,384,128]{2,1,0:T(8,128)(2,1)}, bf16[256,256]{1,0:T(8,128)(2,1)}) custom-call(bf16[64,1536]{1,0:T(8,128)(2,1)} %copy-done.4, bf16[64,1536]{1,0:T(8,128)(2,1)} %copy-done.3, bf16[64,1536]{1,0:T(8,128)(2,1)} %copy-done.17, bf16[64,1536]{1,0:T(8,128)(2,1)} %copy-done.18, ...), custom_call_target="tpu_custom_call" | custom-call | flops 4000000000 | bytes 4000000 | tf_op jit(solution)/shard_map/norm_project_rotate/pallas_call | solution.py:258
  23.6 6.0 %collective-permute-done.4.refs_1_ = bf16[64,1536]{1,0:T(8,128)(2,1)S(1)} collective-permute-done((bf16[64,1536]{1,0:T(8,128)(2,1)S(1)}, bf16[64,1536]{1,0:T(8,128)(2,1)S(1)}, u32[]{:S(2)}, u32[]{:S(2)}) %collective-permute-start.4) | collective-permute-done | bytes 196640 | tf_op jit(solution)/shard_map/ppermute | solution.py:35
  29.8 1.3 collective-permute-start.2
  31.1 1.2 collective-permute-start.10
  32.3 5.7 %collective-permute-done.7.refs_2_ = bf16[64,1536]{1,0:T(8,128)(2,1)S(1)} collective-permute-done((bf16[64,1536]{1,0:T(8,128)(2,1)S(1)}, bf16[64,1536]{1,0:T(8,128)(2,1)S(1)}, u32[]{:S(2)}, u32[]{:S(2)}) %collective-permute-start.7) | collective-permute-done | bytes 196640 | tf_op jit(solution)/shard_map/ppermute | solution.py:35
  37.9 2.1 %collective-permute-done.8.refs_3_ = bf16[64,1536]{1,0:T(8,128)(2,1)S(1)} collective-permute-done((bf16[64,1536]{1,0:T(8,128)(2,1)S(1)}, bf16[64,1536]{1,0:T(8,128)(2,1)S(1)}, u32[]{:S(2)}, u32[]{:S(2)}) %collective-permute-start.8) | collective-permute-done | bytes 196640 | tf_op jit(solution)/shard_map/ppermute | solution.py:35
  40.1 0.7 copy-done.26
  40.7 3.9 %norm_project_rotate.3 = (bf16[2,384,128]{2,1,0:T(8,128)(2,1)}, bf16[2,384,128]{2,1,0:T(8,128)(2,1)}, bf16[256,256]{1,0:T(8,128)(2,1)}) custom-call(bf16[64,1536]{1,0:T(8,128)(2,1)} %copy-done.19, bf16[64,1536]{1,0:T(8,128)(2,1)} %copy-done.21, bf16[64,1536]{1,0:T(8,128)(2,1)} %copy-done.25, bf16[64,1536]{1,0:T(8,128)(2,1)} %copy-done.26, ...), custom_call_target="tpu_custom_call" | custom-call | flops 4000000000 | bytes 4000000 | tf_op jit(solution)/shard_map/norm_project_rotate/pallas_call | solution.py:258
  44.9 0.7 copy-done.28
  45.5 1.7 %collective-permute-start.9 = (bf16[256,256]{1,0:T(8,128)(2,1)S(1)}, bf16[256,256]{1,0:T(8,128)(2,1)S(1)}, u32[]{:S(2)}, u32[]{:S(2)}) collective-permute-start(bf16[256,256]{1,0:T(8,128)(2,1)S(1)} %copy-done.28), channel_id=1, source_target_pairs={{0,4},{4,8},{8,12},{12,16},{16,20},{20,24},{24,28},{1,5},{5,9},{9,... | collective-permute-start | bytes 393224 | tf_op jit(solution)/shard_map/ppermute | solution.py:824
  47.9 0.6 stack.44.refs_1_
  48.5 0.6 copy-done.29
  49.6 7.2 %attend.6 = bf16[128,1536]{1,0:T(8,128)(2,1)} custom-call(s32[4,128]{1,0:T(4,128)} %get-tuple-element.40.refs_0_, s32[8]{0:T(128)} %stack.44.refs_1_, s32[8]{0:T(128)} %refs_2_.7, bf16[2,384,128]{2,1,0:T(8,128)(2,1)} %get-tuple-element.61.refs_3_, s32[4,2,128,128]{3,2,1,0:T(8,128)} %get-tuple-element.44.refs_4_, bf16[256,256]{1,0:T(8,128)(2,1)} %copy-done.27, ...), custom_call_target="tpu_custom_call" | custom-call | flops 8000000000 | bytes 4000000 | tf_op jit(solution)/shard_map/attend/pallas_call | solution.py:446
  56.9 7.3 %attend.7 = bf16[128,1536]{1,0:T(8,128)(2,1)} custom-call(s32[4,128]{1,0:T(4,128)} %get-tuple-element.40.refs_0_, s32[8]{0:T(128)} %stack.44.refs_1_, s32[8]{0:T(128)} %refs_2_.7, bf16[2,384,128]{2,1,0:T(8,128)(2,1)} %get-tuple-element.62.refs_3_, s32[4,2,128,128]{3,2,1,0:T(8,128)} %get-tuple-element.44.refs_4_, bf16[256,256]{1,0:T(8,128)(2,1)} %copy-done.27, ...), custom_call_target="tpu_custom_call" | custom-call | flops 8000000000 | bytes 4000000 | tf_op jit(solution)/shard_map/attend/pallas_call | solution.py:446
  64.2 2.0 %collective-permute-start.14 = (bf16[128,1536]{1,0:T(8,128)(2,1)}, bf16[128,1536]{1,0:T(8,128)(2,1)S(1)}, u32[]{:S(2)}, u32[]{:S(2)}) collective-permute-start(bf16[128,1536]{1,0:T(8,128)(2,1)} %attend.7), channel_id=1, source_target_pairs={{0,1},{1,2},{2,3},{3,0},{4,5},{5,6},{6,7},{7,4},{8,9},{9,10},{10,1... | collective-permute-start | bytes 1179656 | tf_op jit(solution)/shard_map/ppermute | solution.py:827
  66.2 7.4 %attend.5 = bf16[128,1536]{1,0:T(8,128)(2,1)} custom-call(s32[4,128]{1,0:T(4,128)} %get-tuple-element.40.refs_0_, s32[8]{0:T(128)} %stack.44.refs_1_, s32[8]{0:T(128)} %refs_2_.7, bf16[2,384,128]{2,1,0:T(8,128)(2,1)} %get-tuple-element.60.refs_3_, s32[4,2,128,128]{3,2,1,0:T(8,128)} %get-tuple-element.44.refs_4_, bf16[256,256]{1,0:T(8,128)(2,1)} %copy-done.27, ...), custom_call_target="tpu_custom_call" | custom-call | flops 8000000000 | bytes 4000000 | tf_op jit(solution)/shard_map/attend/pallas_call | solution.py:446
  73.6 1.1 add_convert_fusion.4
  74.7 1.9 %collective-permute-start.13 = (bf16[128,1536]{1,0:T(8,128)(2,1)S(1)}, bf16[128,1536]{1,0:T(8,128)(2,1)S(1)}, u32[]{:S(2)}, u32[]{:S(2)}) collective-permute-start(bf16[128,1536]{1,0:T(8,128)(2,1)S(1)} %add_convert_fusion.4), channel_id=1, source_target_pairs={{0,3},{1,0},{2,1},{3,2},{4,7},{5,4},{6,5},{7,6},{8,11},{9,8},{10,9... | collective-permute-start | bytes 1179656 | tf_op jit(solution)/shard_map/ppermute | solution.py:827
  76.6 7.4 %attend.4.own = f32[128,1536]{1,0:T(8,128)} custom-call(s32[4,128]{1,0:T(4,128)} %get-tuple-element.40.refs_0_, s32[8]{0:T(128)} %stack.44.refs_1_, s32[8]{0:T(128)} %refs_2_.7, bf16[2,384,128]{2,1,0:T(8,128)(2,1)} %get-tuple-element.43.refs_3_, s32[4,2,128,128]{3,2,1,0:T(8,128)} %get-tuple-element.44.refs_4_, bf16[256,256]{1,0:T(8,128)(2,1)} %copy-done.27, ...), custom_call_target="tpu_custom_call" | custom-call | flops 8000000000 | bytes 4000000 | tf_op jit(solution)/shard_map/attend/pallas_call | solution.py:446
  84.0 2.1 %route_tables.1 = (s32[4,1024]{1,0:T(4,128)}, f32[4,1024]{1,0:T(4,128)}, s32[1024,8]{1,0:T(8,128)}) custom-call(s32[1]{0:T(128)} %bitcast.14.first_expert, bf16[2112,256]{1,0:T(8,128)(2,1)} %copy-done.7, bf16[2112,256]{1,0:T(8,128)(2,1)} %copy-done.11), custom_call_target="tpu_custom_call" | custom-call | flops 3000000000 | bytes 1000000 | tf_op jit(solution)/shard_map/route_tables/pallas_call | solution.py:729
  86.1 0.7 copy-done.15
  87.0 2.7 %add_and_norm.1 = (f32[128,1536]{1,0:T(8,128)}, bf16[128,1536]{1,0:T(8,128)(2,1)}) custom-call(bf16[128,1536]{1,0:T(8,128)(2,1)} %tokens.1, f32[1,1536]{1,0:T(1,128)} %broadcast_in_dim.8.gain, f32[128,1536]{1,0:T(8,128)} %attend.4.own, bf16[128,1536]{1,0:T(8,128)(2,1)} %copy-done.16, bf16[128,1536]{1,0:T(8,128)(2,1)} %copy-done.15), custom_call_target="tpu_custom_call" | custom-call | flops 1000000000 | bytes 3145728 | tf_op jit(solution)/shard_map/add_and_norm/pallas_call | solution.py:498
  89.7 3.7 %collective-permute-start.16 = (bf16[128,1536]{1,0:T(8,128)(2,1)}, bf16[128,1536]{1,0:T(8,128)(2,1)S(1)}, u32[]{:S(2)}, u32[]{:S(2)}) collective-permute-start(bf16[128,1536]{1,0:T(8,128)(2,1)} %get-tuple-element.69.refs_0_), channel_id=1, source_target_pairs={{0,8},{4,20},{8,0},{12,28},{16,24},{20,4},{24,16},{28,12},{1,9},{5... | collective-permute-start | bytes 1179656 | tf_op jit(solution)/shard_map/ppermute | solution.py:879
  93.4 1.8 %collective-permute-start.15 = (bf16[128,1536]{1,0:T(8,128)(2,1)}, bf16[128,1536]{1,0:T(8,128)(2,1)S(1)}, u32[]{:S(2)}, u32[]{:S(2)}) collective-permute-start(bf16[128,1536]{1,0:T(8,128)(2,1)} %get-tuple-element.69.refs_0_), channel_id=1, source_target_pairs={{0,16},{4,12},{8,24},{12,4},{16,0},{20,28},{24,8},{28,20},{1,17},{... | collective-permute-start | bytes 1179656 | tf_op jit(solution)/shard_map/ppermute | solution.py:878
  95.2 8.0 %collective-permute-done.16.refs_2_ = bf16[128,1536]{1,0:T(8,128)(2,1)S(1)} collective-permute-done((bf16[128,1536]{1,0:T(8,128)(2,1)}, bf16[128,1536]{1,0:T(8,128)(2,1)S(1)}, u32[]{:S(2)}, u32[]{:S(2)}) %collective-permute-start.16) | collective-permute-done | bytes 393248 | tf_op jit(solution)/shard_map/ppermute | solution.py:879
  103.2 3.6 %collective-permute-start.18 = (bf16[64,1536]{1,0:T(8,128)(2,1)S(1)}, bf16[64,1536]{1,0:T(8,128)(2,1)S(1)}, u32[]{:S(2)}, u32[]{:S(2)}) collective-permute-start(bf16[64,1536]{1,0:T(8,128)(2,1)S(1)} %slice.53), channel_id=1, source_target_pairs={{0,16},{4,12},{8,24},{12,4},{16,0},{20,28},{24,8},{28,20},{1,17},{... | collective-permute-start | bytes 589832 | tf_op jit(solution)/shard_map/ppermute | solution.py:882
  107.7 2.7 %collective-permute-done.18.refs_4_ = bf16[64,1536]{1,0:T(8,128)(2,1)S(1)} collective-permute-done((bf16[64,1536]{1,0:T(8,128)(2,1)S(1)}, bf16[64,1536]{1,0:T(8,128)(2,1)S(1)}, u32[]{:S(2)}, u32[]{:S(2)}) %collective-permute-start.18) | collective-permute-done | bytes 196640 | tf_op jit(solution)/shard_map/ppermute | solution.py:882
  110.4 2.1 %collective-permute-done.17.refs_3_ = bf16[64,1536]{1,0:T(8,128)(2,1)S(1)} collective-permute-done((bf16[64,1536]{1,0:T(8,128)(2,1)S(1)}, bf16[64,1536]{1,0:T(8,128)(2,1)S(1)}, u32[]{:S(2)}, u32[]{:S(2)}) %collective-permute-start.17) | collective-permute-done | bytes 196640 | tf_op jit(solution)/shard_map/ppermute | solution.py:881
  112.5 1.4 collective-permute-done.22.refs_8_
  114.0 0.6 copy-done.24
  114.6 0.7 copy-done.14
  115.4 23.6 %experts.1 = (bf16[512,1536]{1,0:T(8,128)(2,1)}, bf16[384,1536]{1,0:T(8,128)(2,1)}, bf16[128,1536]{1,0:T(8,128)(2,1)}) custom-call(s32[4,1024]{1,0:T(4,128)} %get-tuple-element.63.slot_row, f32[4,1024]{1,0:T(4,128)} %get-tuple-element.64.gate_row, s32[1024,8]{1,0:T(8,128)} %get-tuple-element.65.slot_col, bf16[128,1536]{1,0:T(8,128)(2,1)} %get-tuple-element.69.refs_0_, ...), custom_call_target="tpu_custom_call" | custom-call | flops 12884901888 | bytes 25165824 | tf_op jit(solution)/shard_map/experts/pallas_call | solution.py:637
  139.5 1.4 collective-permute-done.25
  140.9 1.1 add_convert_fusion.3
  142.7 6.5 %collective-permute-done.27 = bf16[64,1536]{1,0:T(8,128)(2,1)S(1)} collective-permute-done((bf16[64,1536]{1,0:T(8,128)(2,1)S(1)}, bf16[64,1536]{1,0:T(8,128)(2,1)S(1)}, u32[]{:S(2)}, u32[]{:S(2)}) %collective-permute-start.27) | collective-permute-done | bytes 196640 | tf_op jit(solution)/shard_map/ppermute | solution.py:115
  149.4 0.6 collective-permute-start.28
  150.5 9.5 %collective-permute-done.28 = bf16[128,1536]{1,0:T(8,128)(2,1)S(1)} collective-permute-done((bf16[128,1536]{1,0:T(8,128)(2,1)S(1)}, bf16[128,1536]{1,0:T(8,128)(2,1)S(1)}, u32[]{:S(2)}, u32[]{:S(2)}) %collective-permute-start.28) | collective-permute-done | bytes 393248 | tf_op jit(solution)/shard_map/ppermute | solution.py:126
  160.0 1.0 add_convert_fusion
  (103 shorter events, 5.6 us)
Async XLA Ops:
  1.1 10.3 %copy-start.3 = (bf16[64,1536]{1,0:T(8,128)(2,1)}, bf16[64,1536]{1,0:T(8,128)(2,1)S(1)}, u32[]{:S(2)}) copy-start(bf16[64,1536]{1,0:T(8,128)(2,1)S(1)} %get-tuple-element.79.refs_1_) | copy-start | bytes 589828
  1.1 10.3 %copy-start.4 = (bf16[64,1536]{1,0:T(8,128)(2,1)}, bf16[64,1536]{1,0:T(8,128)(2,1)S(1)}, u32[]{:S(2)}) copy-start(bf16[64,1536]{1,0:T(8,128)(2,1)S(1)} %get-tuple-element.80.refs_0_) | copy-start | bytes 589828
  1.1 17.2 %collective-permute-start.1 = (bf16[64,1536]{1,0:T(8,128)(2,1)S(1)}, bf16[64,1536]{1,0:T(8,128)(2,1)S(1)}, u32[]{:S(2)}, u32[]{:S(2)}) collective-permute-start(bf16[64,1536]{1,0:T(8,128)(2,1)S(1)} %get-tuple-element.79.refs_1_), channel_id=1, source_target_pairs={{0,1},{1,2},{2,3},{3,0},{4,5},{5,6},{6,7},{7,4},{8,9},{9,10},{10,1... | collective-permute-start | bytes 589832 | tf_op jit(solution)/shard_map/ppermute | solution.py:35
  4.1 11.1 %collective-permute-start = (bf16[64,1536]{1,0:T(8,128)(2,1)S(1)}, bf16[64,1536]{1,0:T(8,128)(2,1)S(1)}, u32[]{:S(2)}, u32[]{:S(2)}) collective-permute-start(bf16[64,1536]{1,0:T(8,128)(2,1)S(1)} %get-tuple-element.80.refs_0_), channel_id=1, source_target_pairs={{0,1},{1,2},{2,3},{3,0},{4,5},{5,6},{6,7},{7,4},{8,9},{9,10},{10,1... | collective-permute-start | bytes 589832 | tf_op jit(solution)/shard_map/ppermute | solution.py:35
  7.6 3.8 %copy-start.10 = (s32[128,8]{0,1:T(8,128)S(1)}, s32[128,8]{0,1:T(8,128)}, u32[]{:S(2)}) copy-start(s32[128,8]{0,1:T(8,128)} %param.27) | copy-start | bytes 12292
  7.6 3.8 %copy-start.8 = (f32[1536]{0:T(1024)S(1)}, f32[1536]{0:T(1024)}, u32[]{:S(2)}) copy-start(f32[1536]{0:T(1024)} %param.22) | copy-start | bytes 18436
  7.6 4.4 %copy-start.2 = (bf16[512,256]{1,0:T(8,128)(2,1)S(1)}, bf16[512,256]{1,0:T(8,128)(2,1)}, u32[]{:S(2)}) copy-start(bf16[512,256]{1,0:T(8,128)(2,1)} %param.21) | copy-start | bytes 786436
  15.3 4.3 %copy-start.17 = (bf16[64,1536]{1,0:T(8,128)(2,1)}, bf16[64,1536]{1,0:T(8,128)(2,1)S(1)}, u32[]{:S(2)}) copy-start(bf16[64,1536]{1,0:T(8,128)(2,1)S(1)} %collective-permute-done.refs_2_) | copy-start | bytes 589828
  15.3 14.3 %collective-permute-start.6 = (bf16[528,256]{1,0:T(8,128)(2,1)S(1)}, bf16[528,256]{1,0:T(8,128)(2,1)S(1)}, u32[]{:S(2)}, u32[]{:S(2)}) collective-permute-start(bf16[528,256]{1,0:T(8,128)(2,1)S(1)} %maximum_maximum_fusion), channel_id=1, source_target_pairs={{0,8},{4,20},{8,0},{12,28},{16,24},{20,4},{24,16},{28,12},{1,9},{5... | collective-permute-start | bytes 811016 | tf_op jit(solution)/shard_map/ppermute | solution.py:62
  16.8 12.8 %collective-permute-start.5 = (bf16[528,256]{1,0:T(8,128)(2,1)S(1)}, bf16[528,256]{1,0:T(8,128)(2,1)S(1)}, u32[]{:S(2)}, u32[]{:S(2)}) collective-permute-start(bf16[528,256]{1,0:T(8,128)(2,1)S(1)} %maximum_maximum_fusion), channel_id=1, source_target_pairs={{0,16},{4,12},{8,24},{12,4},{16,0},{20,28},{24,8},{28,20},{1,17},{... | collective-permute-start | bytes 811016 | tf_op jit(solution)/shard_map/ppermute | solution.py:62
  18.3 11.3 %collective-permute-start.3 = (bf16[64,1536]{1,0:T(8,128)(2,1)S(1)}, bf16[64,1536]{1,0:T(8,128)(2,1)S(1)}, u32[]{:S(2)}, u32[]{:S(2)}) collective-permute-start(bf16[64,1536]{1,0:T(8,128)(2,1)S(1)} %collective-permute-done.refs_2_), channel_id=1, source_target_pairs={{0,1},{1,2},{2,3},{3,0},{4,5},{5,6},{6,7},{7,4},{8,9},{9,10},{10,1... | collective-permute-start | bytes 589832 | tf_op jit(solution)/shard_map/ppermute | solution.py:35
  18.3 11.3 %collective-permute-start.4 = (bf16[64,1536]{1,0:T(8,128)(2,1)S(1)}, bf16[64,1536]{1,0:T(8,128)(2,1)S(1)}, u32[]{:S(2)}, u32[]{:S(2)}) collective-permute-start(bf16[64,1536]{1,0:T(8,128)(2,1)S(1)} %collective-permute-done.1.refs_3_), channel_id=1, source_target_pairs={{0,1},{1,2},{2,3},{3,0},{4,5},{5,6},{6,7},{7,4},{8,9},{9,10},{10,1... | collective-permute-start | bytes 589832 | tf_op jit(solution)/shard_map/ppermute | solution.py:35
  29.6 10.5 %copy-start.21 = (bf16[64,1536]{1,0:T(8,128)(2,1)}, bf16[64,1536]{1,0:T(8,128)(2,1)S(1)}, u32[]{:S(2)}) copy-start(bf16[64,1536]{1,0:T(8,128)(2,1)S(1)} %collective-permute-done.4.refs_1_) | copy-start | bytes 589828
  29.6 10.4 %copy-start.19 = (bf16[64,1536]{1,0:T(8,128)(2,1)}, bf16[64,1536]{1,0:T(8,128)(2,1)S(1)}, u32[]{:S(2)}) copy-start(bf16[64,1536]{1,0:T(8,128)(2,1)S(1)} %collective-permute-done.3.refs_0_) | copy-start | bytes 589828
  29.6 8.3 %collective-permute-start.7 = (bf16[64,1536]{1,0:T(8,128)(2,1)S(1)}, bf16[64,1536]{1,0:T(8,128)(2,1)S(1)}, u32[]{:S(2)}, u32[]{:S(2)}) collective-permute-start(bf16[64,1536]{1,0:T(8,128)(2,1)S(1)} %collective-permute-done.3.refs_0_), channel_id=1, source_target_pairs={{0,1},{1,2},{2,3},{3,0},{4,5},{5,6},{6,7},{7,4},{8,9},{9,10},{10,1... | collective-permute-start | bytes 589832 | tf_op jit(solution)/shard_map/ppermute | solution.py:35
  29.7 10.4 %collective-permute-start.8 = (bf16[64,1536]{1,0:T(8,128)(2,1)S(1)}, bf16[64,1536]{1,0:T(8,128)(2,1)S(1)}, u32[]{:S(2)}, u32[]{:S(2)}) collective-permute-start(bf16[64,1536]{1,0:T(8,128)(2,1)S(1)} %collective-permute-done.4.refs_1_), channel_id=1, source_target_pairs={{0,1},{1,2},{2,3},{3,0},{4,5},{5,6},{6,7},{7,4},{8,9},{9,10},{10,1... | collective-permute-start | bytes 589832 | tf_op jit(solution)/shard_map/ppermute | solution.py:35
  29.8 2.5 %collective-permute-start.2 = (bf16[256,256]{1,0:T(8,128)(2,1)}, bf16[256,256]{1,0:T(8,128)(2,1)S(1)}, u32[]{:S(2)}, u32[]{:S(2)}) collective-permute-start(bf16[256,256]{1,0:T(8,128)(2,1)} %get-tuple-element.45.refs_7_), channel_id=1, source_target_pairs={{0,4},{4,8},{8,12},{12,16},{16,20},{20,24},{24,28},{1,5},{5,9},{9,... | collective-permute-start | bytes 393224 | tf_op jit(solution)/shard_map/ppermute | solution.py:824
  31.1 13.6 %collective-permute-start.10 = (bf16[528,256]{1,0:T(8,128)(2,1)S(1)}, bf16[528,256]{1,0:T(8,128)(2,1)S(1)}, u32[]{:S(2)}, u32[]{:S(2)}) collective-permute-start(bf16[528,256]{1,0:T(8,128)(2,1)S(1)} %collective-permute-done.5), channel_id=1, source_target_pairs={{0,8},{4,20},{8,0},{12,28},{16,24},{20,4},{24,16},{28,12},{1,9},{5... | collective-permute-start | bytes 811016 | tf_op jit(solution)/shard_map/ppermute | solution.py:72
  32.3 12.3 %copy-start.27 = (bf16[256,256]{1,0:T(8,128)(2,1)}, bf16[256,256]{1,0:T(8,128)(2,1)S(1)}, u32[]{:S(2)}) copy-start(bf16[256,256]{1,0:T(8,128)(2,1)S(1)} %collective-permute-done.2.refs_5_) | copy-start | bytes 393220
  37.9 2.1 %copy-start.25 = (bf16[64,1536]{1,0:T(8,128)(2,1)}, bf16[64,1536]{1,0:T(8,128)(2,1)S(1)}, u32[]{:S(2)}) copy-start(bf16[64,1536]{1,0:T(8,128)(2,1)S(1)} %collective-permute-done.7.refs_2_) | copy-start | bytes 589828
  44.6 2.7 %copy-start.9 = (f32[1536]{0:T(1024)S(1)}, f32[1536]{0:T(1024)}, u32[]{:S(2)}) copy-start(f32[1536]{0:T(1024)} %param.26) | copy-start | bytes 18436
  44.8 3.8 %copy-start.7 = (bf16[2112,256]{1,0:T(8,128)(2,1)}, bf16[2112,256]{1,0:T(8,128)(2,1)S(1)}, u32[]{:S(2)}) copy-start(bf16[2112,256]{1,0:T(8,128)(2,1)S(1)} %constant_dynamic-update-slice_fusion.refs_9_.refs_0_) | copy-start | bytes 3244036
  44.8 3.8 %collective-permute-start.11 = (bf16[2112,256]{1,0:T(8,128)(2,1)S(1)}, bf16[2112,256]{1,0:T(8,128)(2,1)S(1)}, u32[]{:S(2)}, u32[]{:S(2)}) collective-permute-start(bf16[2112,256]{1,0:T(8,128)(2,1)S(1)} %constant_dynamic-update-slice_fusion.refs_9_.refs_0_), channel_id=1, source_target_pairs={{0,4},{4,0},{8,12},{12,8},{16,20},{20,16},{24,28},{28,24},{1,5},{5... | collective-permute-start | bytes 3244040 | tf_op jit(solution)/shard_map/ppermute | solution.py:76
  45.5 3.0 %collective-permute-start.9 = (bf16[256,256]{1,0:T(8,128)(2,1)S(1)}, bf16[256,256]{1,0:T(8,128)(2,1)S(1)}, u32[]{:S(2)}, u32[]{:S(2)}) collective-permute-start(bf16[256,256]{1,0:T(8,128)(2,1)S(1)} %copy-done.28), channel_id=1, source_target_pairs={{0,4},{4,8},{8,12},{12,16},{16,20},{20,24},{24,28},{1,5},{5,9},{9,... | collective-permute-start | bytes 393224 | tf_op jit(solution)/shard_map/ppermute | solution.py:824
  56.8 16.8 %collective-permute-start.12 = (bf16[128,1536]{1,0:T(8,128)(2,1)}, bf16[128,1536]{1,0:T(8,128)(2,1)S(1)}, u32[]{:S(2)}, u32[]{:S(2)}) collective-permute-start(bf16[128,1536]{1,0:T(8,128)(2,1)} %attend.6), channel_id=1, source_target_pairs={{0,3},{1,0},{2,1},{3,2},{4,7},{5,4},{6,5},{7,6},{8,11},{9,8},{10,9... | collective-permute-start | bytes 1179656 | tf_op jit(solution)/shard_map/ppermute | solution.py:827
  64.2 21.9 %collective-permute-start.14 = (bf16[128,1536]{1,0:T(8,128)(2,1)}, bf16[128,1536]{1,0:T(8,128)(2,1)S(1)}, u32[]{:S(2)}, u32[]{:S(2)}) collective-permute-start(bf16[128,1536]{1,0:T(8,128)(2,1)} %attend.7), channel_id=1, source_target_pairs={{0,1},{1,2},{2,3},{3,0},{4,5},{5,6},{6,7},{7,4},{8,9},{9,10},{10,1... | collective-permute-start | bytes 1179656 | tf_op jit(solution)/shard_map/ppermute | solution.py:827
  74.7 11.4 %collective-permute-start.13 = (bf16[128,1536]{1,0:T(8,128)(2,1)S(1)}, bf16[128,1536]{1,0:T(8,128)(2,1)S(1)}, u32[]{:S(2)}, u32[]{:S(2)}) collective-permute-start(bf16[128,1536]{1,0:T(8,128)(2,1)S(1)} %add_convert_fusion.4), channel_id=1, source_target_pairs={{0,3},{1,0},{2,1},{3,2},{4,7},{5,4},{6,5},{7,6},{8,11},{9,8},{10,9... | collective-permute-start | bytes 1179656 | tf_op jit(solution)/shard_map/ppermute | solution.py:827
  89.7 13.5 %collective-permute-start.16 = (bf16[128,1536]{1,0:T(8,128)(2,1)}, bf16[128,1536]{1,0:T(8,128)(2,1)S(1)}, u32[]{:S(2)}, u32[]{:S(2)}) collective-permute-start(bf16[128,1536]{1,0:T(8,128)(2,1)} %get-tuple-element.69.refs_0_), channel_id=1, source_target_pairs={{0,8},{4,20},{8,0},{12,28},{16,24},{20,4},{24,16},{28,12},{1,9},{5... | collective-permute-start | bytes 1179656 | tf_op jit(solution)/shard_map/ppermute | solution.py:879
  93.4 13.3 %collective-permute-start.15 = (bf16[128,1536]{1,0:T(8,128)(2,1)}, bf16[128,1536]{1,0:T(8,128)(2,1)S(1)}, u32[]{:S(2)}, u32[]{:S(2)}) collective-permute-start(bf16[128,1536]{1,0:T(8,128)(2,1)} %get-tuple-element.69.refs_0_), channel_id=1, source_target_pairs={{0,16},{4,12},{8,24},{12,4},{16,0},{20,28},{24,8},{28,20},{1,17},{... | collective-permute-start | bytes 1179656 | tf_op jit(solution)/shard_map/ppermute | solution.py:878
  95.2 17.3 %collective-permute-start.19 = (bf16[128,1536]{1,0:T(8,128)(2,1)}, bf16[128,1536]{1,0:T(8,128)(2,1)S(1)}, u32[]{:S(2)}, u32[]{:S(2)}) collective-permute-start(bf16[128,1536]{1,0:T(8,128)(2,1)} %get-tuple-element.69.refs_0_), channel_id=1, source_target_pairs={{0,4},{4,0},{8,12},{12,8},{16,20},{20,16},{24,28},{28,24},{1,5},{5... | collective-permute-start | bytes 1179656 | tf_op jit(solution)/shard_map/ppermute | solution.py:876
  103.1 10.8 %copy-start.5 = (bf16[128,1536]{1,0:T(8,128)(2,1)}, bf16[128,1536]{1,0:T(8,128)(2,1)S(1)}, u32[]{:S(2)}) copy-start(bf16[128,1536]{1,0:T(8,128)(2,1)S(1)} %collective-permute-done.16.refs_2_) | copy-start | bytes 1179652
  103.2 7.2 %collective-permute-start.18 = (bf16[64,1536]{1,0:T(8,128)(2,1)S(1)}, bf16[64,1536]{1,0:T(8,128)(2,1)S(1)}, u32[]{:S(2)}, u32[]{:S(2)}) collective-permute-start(bf16[64,1536]{1,0:T(8,128)(2,1)S(1)} %slice.53), channel_id=1, source_target_pairs={{0,16},{4,12},{8,24},{12,4},{16,0},{20,28},{24,8},{28,20},{1,17},{... | collective-permute-start | bytes 589832 | tf_op jit(solution)/shard_map/ppermute | solution.py:882
  106.7 7.2 %copy-start.6 = (bf16[128,1536]{1,0:T(8,128)(2,1)}, bf16[128,1536]{1,0:T(8,128)(2,1)S(1)}, u32[]{:S(2)}) copy-start(bf16[128,1536]{1,0:T(8,128)(2,1)S(1)} %collective-permute-done.15.refs_1_) | copy-start | bytes 1179652
  106.8 5.7 %collective-permute-start.17 = (bf16[64,1536]{1,0:T(8,128)(2,1)S(1)}, bf16[64,1536]{1,0:T(8,128)(2,1)S(1)}, u32[]{:S(2)}, u32[]{:S(2)}) collective-permute-start(bf16[64,1536]{1,0:T(8,128)(2,1)S(1)} %slice.52), channel_id=1, source_target_pairs={{0,8},{4,20},{8,0},{12,28},{16,24},{20,4},{24,16},{28,12},{1,9},{5... | collective-permute-start | bytes 589832 | tf_op jit(solution)/shard_map/ppermute | solution.py:881
  107.2 5.4 %collective-permute-start.21 = (bf16[128,1536]{1,0:T(8,128)(2,1)S(1)}, bf16[128,1536]{1,0:T(8,128)(2,1)S(1)}, u32[]{:S(2)}, u32[]{:S(2)}) collective-permute-start(bf16[128,1536]{1,0:T(8,128)(2,1)S(1)} %collective-permute-done.16.refs_2_), channel_id=1, source_target_pairs={{0,4},{4,0},{8,12},{12,8},{16,20},{20,16},{24,28},{28,24},{1,5},{5... | collective-permute-start | bytes 1179656 | tf_op jit(solution)/shard_map/ppermute | solution.py:876
  107.2 6.8 %collective-permute-start.20 = (bf16[128,1536]{1,0:T(8,128)(2,1)S(1)}, bf16[128,1536]{1,0:T(8,128)(2,1)S(1)}, u32[]{:S(2)}, u32[]{:S(2)}) collective-permute-start(bf16[128,1536]{1,0:T(8,128)(2,1)S(1)} %collective-permute-done.15.refs_1_), channel_id=1, source_target_pairs={{0,4},{4,0},{8,12},{12,8},{16,20},{20,16},{24,28},{28,24},{1,5},{5... | collective-permute-start | bytes 1179656 | tf_op jit(solution)/shard_map/ppermute | solution.py:876
  110.4 3.6 %copy-start.20 = (bf16[64,1536]{1,0:T(8,128)(2,1)}, bf16[64,1536]{1,0:T(8,128)(2,1)S(1)}, u32[]{:S(2)}) copy-start(bf16[64,1536]{1,0:T(8,128)(2,1)S(1)} %collective-permute-done.18.refs_4_) | copy-start | bytes 589828
  110.4 2.1 %collective-permute-start.23 = (bf16[64,1536]{1,0:T(8,128)(2,1)S(1)}, bf16[64,1536]{1,0:T(8,128)(2,1)S(1)}, u32[]{:S(2)}, u32[]{:S(2)}) collective-permute-start(bf16[64,1536]{1,0:T(8,128)(2,1)S(1)} %collective-permute-done.18.refs_4_), channel_id=1, source_target_pairs={{0,4},{4,0},{8,12},{12,8},{16,20},{20,16},{24,28},{28,24},{1,5},{5... | collective-permute-start | bytes 589832 | tf_op jit(solution)/shard_map/ppermute | solution.py:876
  112.5 1.5 copy-start.22
  112.5 1.4 collective-permute-start.22
  138.9 10.2 %copy-start = (bf16[512,1536]{1,0:T(8,128)(2,1)S(1)}, bf16[512,1536]{1,0:T(8,128)(2,1)}, u32[]{:S(2)}) copy-start(bf16[512,1536]{1,0:T(8,128)(2,1)} %get-tuple-element.73) | copy-start | bytes 4718596
  138.9 2.0 %collective-permute-start.25 = (bf16[128,1536]{1,0:T(8,128)(2,1)}, bf16[128,1536]{1,0:T(8,128)(2,1)S(1)}, u32[]{:S(2)}, u32[]{:S(2)}) collective-permute-start(bf16[128,1536]{1,0:T(8,128)(2,1)} %get-tuple-element.72), channel_id=1, source_target_pairs={{0,4},{4,0},{8,12},{12,8},{16,20},{20,16},{24,28},{28,24},{1,5},{5... | collective-permute-start | bytes 1179656 | tf_op jit(solution)/shard_map/ppermute | solution.py:111
  139.1 10.0 %collective-permute-start.24 = (bf16[384,1536]{1,0:T(8,128)(2,1)}, bf16[384,1536]{1,0:T(8,128)(2,1)S(1)}, u32[]{:S(2)}, u32[]{:S(2)}) collective-permute-start(bf16[384,1536]{1,0:T(8,128)(2,1)} %get-tuple-element.71), channel_id=1, source_target_pairs={{0,4},{4,0},{8,12},{12,8},{16,20},{20,16},{24,28},{28,24},{1,5},{5... | collective-permute-start | bytes 3538952 | tf_op jit(solution)/shard_map/ppermute | solution.py:112
  142.1 7.1 %collective-permute-start.27 = (bf16[64,1536]{1,0:T(8,128)(2,1)S(1)}, bf16[64,1536]{1,0:T(8,128)(2,1)S(1)}, u32[]{:S(2)}, u32[]{:S(2)}) collective-permute-start(bf16[64,1536]{1,0:T(8,128)(2,1)S(1)} %get-tuple-element.77), channel_id=1, source_target_pairs={{0,16},{4,12},{8,24},{12,4},{16,0},{20,28},{24,8},{28,20},{1,17},{... | collective-permute-start | bytes 589832 | tf_op jit(solution)/shard_map/ppermute | solution.py:115
  142.3 17.7 %copy-start.1 = (f32[128,1536]{1,0:T(8,128)S(1)}, f32[128,1536]{1,0:T(8,128)}, u32[]{:S(2)}) copy-start(f32[128,1536]{1,0:T(8,128)} %get-tuple-element.68) | copy-start | bytes 2359300
  142.3 6.8 %collective-permute-start.26 = (bf16[64,1536]{1,0:T(8,128)(2,1)S(1)}, bf16[64,1536]{1,0:T(8,128)(2,1)S(1)}, u32[]{:S(2)}, u32[]{:S(2)}) collective-permute-start(bf16[64,1536]{1,0:T(8,128)(2,1)S(1)} %get-tuple-element.78), channel_id=1, source_target_pairs={{0,8},{4,20},{8,0},{12,28},{16,24},{20,4},{24,16},{28,12},{1,9},{5... | collective-permute-start | bytes 589832 | tf_op jit(solution)/shard_map/ppermute | solution.py:114
  149.4 10.6 %collective-permute-start.28 = (bf16[128,1536]{1,0:T(8,128)(2,1)S(1)}, bf16[128,1536]{1,0:T(8,128)(2,1)S(1)}, u32[]{:S(2)}, u32[]{:S(2)}) collective-permute-start(bf16[128,1536]{1,0:T(8,128)(2,1)S(1)} %get-tuple-element.75), channel_id=1, source_target_pairs={{0,8},{4,20},{8,0},{12,28},{16,24},{20,4},{24,16},{28,12},{1,9},{5... | collective-permute-start | bytes 1179656 | tf_op jit(solution)/shard_map/ppermute | solution.py:126
  150.1 10.0 %collective-permute-start.29 = (bf16[128,1536]{1,0:T(8,128)(2,1)S(1)}, bf16[128,1536]{1,0:T(8,128)(2,1)S(1)}, u32[]{:S(2)}, u32[]{:S(2)}) collective-permute-start(bf16[128,1536]{1,0:T(8,128)(2,1)S(1)} %get-tuple-element.76), channel_id=1, source_target_pairs={{0,16},{4,12},{8,24},{12,4},{16,0},{20,28},{24,8},{28,20},{1,17},{... | collective-permute-start | bytes 1179656 | tf_op jit(solution)/shard_map/ppermute | solution.py:125
  (12 other events, 12.0 us)
